TPU v7x, 32 devices: a whole 2x2x4 slice. The times are simulated.
32 devices in a mesh: group: 4 (over y, x), expert: 4 (over z), dp: 2 (over core).
Axes of the slice: x: 2, y: 2, z: 4, core: 2. Of those that a mesh axis runs over, the one named last changes fastest.
Arguments:
- patches: bfloat16 [32768, 16], P(('group', 'expert', 'dp')), may hold values from -6 to 6
- target_noise: float32 [32768, 16], P(('group', 'expert', 'dp')), may hold values from -12 to 12
- timesteps: int32 [128], P(('group', 'expert', 'dp')), may hold values from 0 to 999
- labels: int32 [128], P(('group', 'expert', 'dp')), may hold values from 0 to 1000
- routes: int32 [2, 32768, 2], P(None, ('group', 'expert', 'dp')), may hold values from 0 to 3, all different within a row; in each aligned block of 1024 rows (0 to 1023, 1024 to 2047, ..., all dimensions but the last counted through in order) at most 1024 rows name the same one
- route_gates: float32 [2, 32768, 2], P(None, ('group', 'expert', 'dp')), may hold values from 0.3 to 1
- stem_weights: float32 [2441, 384], P(None, ('expert', 'dp')), may hold values from -3 to 3
- layer_in: float32 [2, 384, 6912], P(None, None, ('expert', 'dp')), may hold values from -2 to 2
- layer_out: float32 [2, 3072, 384], P(None, ('expert', 'dp')), may hold values from -0.15625 to 0.15625
- experts: float32 [2, 4, 2, 384, 1536], P(None, 'expert', None, None, 'dp'), may hold values from -0.21875 to 0.21875
- stem_first: float32 [4, 2441, 384], P('group', None, ('expert', 'dp')), may hold values from -16 to 16
- layer_in_first: float32 [4, 2, 384, 6912], P('group', None, None, ('expert', 'dp')), may hold values from -4 to 4
- layer_out_first: float32 [4, 2, 3072, 384], P('group', None, ('expert', 'dp')), may hold values from -4 to 4
- experts_first: float32 [4, 2, 4, 2, 384, 1536], P('group', None, 'expert', None, None, 'dp'), may hold values from -4 to 4
- stem_second: float32 [4, 2441, 384], P('group', None, ('expert', 'dp')), may hold values from 38.5024 to 155.648
- layer_in_second: float32 [4, 2, 384, 6912], P('group', None, None, ('expert', 'dp')), may hold values from 4.34176 to 17.2032
- layer_out_second: float32 [4, 2, 3072, 384], P('group', None, ('expert', 'dp')), may hold values from 4.34176 to 17.2032
- experts_second: float32 [4, 2, 4, 2, 384, 1536], P('group', None, 'expert', None, None, 'dp'), may hold values from 2.17088 to 8.6016
- stem_moment: float32 [2441, 384], P(None, ('expert', 'dp')), may hold values from -0.15625 to 0.15625
- layer_in_moment: float32 [2, 384, 6912], P(None, None, ('expert', 'dp')), may hold values from -0.15625 to 0.15625
- layer_out_moment: float32 [2, 3072, 384], P(None, ('expert', 'dp')), may hold values from -0.15625 to 0.15625
- experts_moment: float32 [2, 4, 2, 384, 1536], P(None, 'expert', None, None, 'dp'), may hold values from -0.15625 to 0.15625
Outputs:
- loss_sum: float32 [], replicated
- stem_new: float32 [2441, 384], P(None, ('expert', 'dp'))
- layer_in_new: float32 [2, 384, 6912], P(None, None, ('expert', 'dp'))
- layer_out_new: float32 [2, 3072, 384], P(None, ('expert', 'dp'))
- experts_new: float32 [2, 4, 2, 384, 1536], P(None, 'expert', None, None, 'dp')
- stem_half: bfloat16 [2441, 384], P(None, ('expert', 'dp'))
- layer_in_half: bfloat16 [2, 384, 6912], P(None, None, ('expert', 'dp'))
- layer_out_half: bfloat16 [2, 3072, 384], P(None, ('expert', 'dp'))
- experts_half: bfloat16 [2, 4, 2, 384, 1536], P(None, 'expert', None, None, 'dp')
- stem_first_new: float32 [4, 2441, 384], P('group', None, ('expert', 'dp'))
- layer_in_first_new: float32 [4, 2, 384, 6912], P('group', None, None, ('expert', 'dp'))
- layer_out_first_new: float32 [4, 2, 3072, 384], P('group', None, ('expert', 'dp'))
- experts_first_new: float32 [4, 2, 4, 2, 384, 1536], P('group', None, 'expert', None, None, 'dp')
- stem_second_new: float32 [4, 2441, 384], P('group', None, ('expert', 'dp'))
- layer_in_second_new: float32 [4, 2, 384, 6912], P('group', None, None, ('expert', 'dp'))
- layer_out_second_new: float32 [4, 2, 3072, 384], P('group', None, ('expert', 'dp'))
- experts_second_new: float32 [4, 2, 4, 2, 384, 1536], P('group', None, 'expert', None, None, 'dp')
- stem_moment_new: float32 [2441, 384], P(None, ('expert', 'dp'))
- layer_in_moment_new: float32 [2, 384, 6912], P(None, None, ('expert', 'dp'))
- layer_out_moment_new: float32 [2, 3072, 384], P(None, ('expert', 'dp'))
- experts_moment_new: float32 [2, 4, 2, 384, 1536], P(None, 'expert', None, None, 'dp')
Inputs may be any that keep to these rules, and one draw needn't show every extreme that they name: `routes`: within the rows of one device in each layer, no expert is named more than 1024 times; some expert is named exactly 1024 times.
All inputs are finite; a program needn't handle non-finite values.
Results may differ from a plain program's by a relative error of at most 0.015.
The roundings to bfloat16 on the way count: a program that leaves them out, or rounds other values in their place, can miss the bound.
Values may be sent and summed in bfloat16 or wider, within the bound.
A program may use at most 448 MiB of HBM per device.

v0:
```python
import jax
import jax.numpy as jnp
from jax import lax
from jax.sharding import PartitionSpec as P

D = 384
HEADS = 6
IMG = 32
FREQ = 256
CLASSES = 1000
LAYERS = 2
STEP = 10
PATCH_DIM = 16
PATCHES = 256


highest = lax.Precision.HIGHEST
beta_one = 0.9
beta_two = 0.95
eps_adam = 1e-08
inner_rate = 0.03
weight_decay = 0.05
outer_rate = 0.7
outer_mom = 0.9
ln_eps = 1e-06


def to_half(values):
    return values.astype(jnp.bfloat16)


def product(left_in, right_in):
    return jnp.dot(left_in, right_in, preferred_element_type=jnp.float32)


def product_tn(left_in, right_in):
    return lax.dot_general(
        left_in, right_in, (((0,), (0,)), ((), ())), preferred_element_type=jnp.float32
    )


def product_nt(left_in, right_in):
    return lax.dot_general(
        left_in, right_in, (((1,), (1,)), ((), ())), preferred_element_type=jnp.float32
    )


def gelu_tanh(values):
    return jax.nn.gelu(values, approximate=True)


def gelu_back(values, gradient):
    _, pull = jax.vjp(gelu_tanh, values)
    return pull(gradient)[0]


def norm_mod(values, shift_in, scale_in):
    centre = values - jnp.mean(values, axis=-1, keepdims=True)
    spread = jnp.mean(centre * centre, axis=-1, keepdims=True)
    return centre * lax.rsqrt(spread + ln_eps) * (1.0 + scale_in) + shift_in


def positions_table():
    grid_side = IMG // 2
    quarter = D // 4
    omegas = 1.0 / 10000.0 ** (jnp.arange(quarter, dtype=jnp.float32) / quarter)
    index_all = jnp.arange(PATCHES, dtype=jnp.int32)
    row_angle = (index_all // grid_side).astype(jnp.float32)[:, None] * omegas[None, :]
    col_angle = (index_all % grid_side).astype(jnp.float32)[:, None] * omegas[None, :]
    return jnp.concatenate(
        [jnp.sin(row_angle), jnp.cos(row_angle), jnp.sin(col_angle), jnp.cos(col_angle)], axis=1
    )


def time_features(step_ids):
    half_freq = FREQ // 2
    frequency = jnp.exp(-jnp.log(10000.0) * jnp.arange(half_freq, dtype=jnp.float32) / half_freq)
    angles = step_ids.astype(jnp.float32)[:, None] * frequency[None, :]
    return jnp.concatenate([jnp.cos(angles), jnp.sin(angles)], axis=1)


def label_table(label_ids):
    return (label_ids[:, None] == jnp.arange(CLASSES + 1, dtype=jnp.int32)[None, :]).astype(
        jnp.float32
    )


def split_stem(stem_all):
    end_patch = PATCH_DIM
    end_time = end_patch + FREQ
    end_second = end_time + D
    end_table = end_second + CLASSES + 1
    end_ada = end_table + 2 * D
    return (
        stem_all[:end_patch],
        stem_all[end_patch:end_time],
        stem_all[end_time:end_second],
        stem_all[end_second:end_table],
        stem_all[end_table:end_ada],
        stem_all[end_ada:],
    )


def slot_places(route_ids, expert_count, capacity):
    flat_ids = route_ids.reshape(-1)
    one_hot_ids = (flat_ids[:, None] == jnp.arange(expert_count, dtype=jnp.int32)[None, :]).astype(
        jnp.int32
    )
    rank_in = jnp.sum((jnp.cumsum(one_hot_ids, axis=0) - one_hot_ids) * one_hot_ids, axis=1)
    return flat_ids * capacity + rank_in


def expert_major(received, local_count):
    sources = received.shape[0] // local_count
    shaped = received.reshape(sources, local_count, received.shape[1], received.shape[2])
    return jnp.swapaxes(shaped, 0, 1).reshape(local_count, -1, received.shape[2])


def source_major(rows_in, sources):
    local_count = rows_in.shape[0]
    shaped = rows_in.reshape(local_count, sources, -1, rows_in.shape[2])
    return jnp.swapaxes(shaped, 0, 1).reshape(sources * local_count, -1, rows_in.shape[2])


def attention_split(qkv, item_count):
    head_dim = qkv.shape[1] // (3 * HEADS)
    shaped = qkv.reshape(item_count, -1, 3, HEADS, head_dim)
    return (shaped[:, :, 0], shaped[:, :, 1], shaped[:, :, 2], head_dim ** (-0.5))


def attention_forward(qkv, item_count):
    queries, keys_in, values_in, scale_att = attention_split(qkv, item_count)
    scores = (
        jnp.einsum("bqhd,bkhd->bhqk", queries, keys_in, preferred_element_type=jnp.float32)
        * scale_att
    )
    row_max = jnp.max(scores, axis=-1, keepdims=True)
    log_sums = row_max + jnp.log(jnp.sum(jnp.exp(scores - row_max), axis=-1, keepdims=True))
    attn_probs = to_half(jnp.exp(scores - log_sums))
    attended = jnp.einsum(
        "bhqk,bkhd->bqhd", attn_probs, values_in, preferred_element_type=jnp.float32
    )
    return (to_half(attended.reshape(qkv.shape[0], -1)), log_sums)


def attention_backward(qkv, log_sums, grad_attended, item_count):
    queries, keys_in, values_in, scale_att = attention_split(qkv, item_count)
    scores = (
        jnp.einsum("bqhd,bkhd->bhqk", queries, keys_in, preferred_element_type=jnp.float32)
        * scale_att
    )
    probs_full = jnp.exp(scores - log_sums)
    grad_out = grad_attended.reshape(queries.shape)
    grad_values = jnp.einsum(
        "bhqk,bqhd->bkhd", to_half(probs_full), grad_out, preferred_element_type=jnp.float32
    )
    grad_probs = jnp.einsum(
        "bqhd,bkhd->bhqk", grad_out, values_in, preferred_element_type=jnp.float32
    )
    grad_scores = probs_full * (
        grad_probs - jnp.sum(probs_full * grad_probs, axis=-1, keepdims=True)
    )
    grad_half = to_half(grad_scores)
    grad_queries = (
        jnp.einsum("bhqk,bkhd->bqhd", grad_half, keys_in, preferred_element_type=jnp.float32)
        * scale_att
    )
    grad_keys = (
        jnp.einsum("bhqk,bqhd->bkhd", grad_half, queries, preferred_element_type=jnp.float32)
        * scale_att
    )
    stacked = jnp.stack([grad_queries, grad_keys, grad_values], axis=2)
    return to_half(stacked.reshape(qkv.shape[0], -1))


def layer_forward(tokens, cond_act, lin, lout, expert_w, route_ids, gate_vals):
    item_count = cond_act.shape[0]
    model_width = tokens.shape[1]
    local_count = expert_w.shape[0]
    expert_count = lax.axis_size("expert") * local_count
    capacity = 4 * tokens.shape[0] // expert_count
    mods = jnp.dot(
        cond_act, lin[:, 4 * model_width : 10 * model_width].astype(jnp.float32), precision=highest
    )
    mods = mods.reshape(item_count, 6, 1, model_width)
    shaped = tokens.reshape(item_count, -1, model_width)
    normed = to_half(norm_mod(shaped, mods[:, 0], mods[:, 1]).reshape(-1, model_width))
    qkv = to_half(product(normed, lin[:, : 3 * model_width]))
    attended, log_sums = attention_forward(qkv, item_count)
    branch = product(attended, lin[:, 3 * model_width : 4 * model_width])
    middle = shaped + mods[:, 2] * branch.reshape(item_count, -1, model_width)
    normed_two = to_half(norm_mod(middle, mods[:, 3], mods[:, 4]).reshape(-1, model_width))
    inner_pre = product(normed_two, lin[:, 10 * model_width :])
    active = to_half(gelu_tanh(inner_pre))
    shared = product(active, lout)
    slot_index = slot_places(route_ids, expert_count, capacity)
    send_rows = jnp.zeros((expert_count * capacity, model_width), jnp.bfloat16)
    send_rows = send_rows.at[slot_index].set(jnp.repeat(normed_two, 2, axis=0))
    received = lax.all_to_all(
        send_rows.reshape(expert_count, capacity, model_width),
        "expert",
        split_axis=0,
        concat_axis=0,
        tiled=True,
    )
    rows_exp = expert_major(received, local_count)
    inner_exp = jnp.einsum(
        "erd,edf->erf", rows_exp, expert_w[:, 0], preferred_element_type=jnp.float32
    )
    active_exp = to_half(gelu_tanh(inner_exp))
    out_exp = to_half(
        jnp.einsum("erf,edf->erd", active_exp, expert_w[:, 1], preferred_element_type=jnp.float32)
    )
    returned = lax.all_to_all(
        source_major(out_exp, lax.axis_size("expert")),
        "expert",
        split_axis=0,
        concat_axis=0,
        tiled=True,
    )
    picked = (
        returned.reshape(-1, model_width)[slot_index]
        .astype(jnp.float32)
        .reshape(-1, 2, model_width)
    )
    mixed_out = shared + jnp.sum(gate_vals[:, :, None] * picked, axis=1)
    result = middle + mods[:, 5] * mixed_out.reshape(item_count, -1, model_width)
    saved = (
        tokens,
        mods,
        normed,
        qkv,
        attended,
        log_sums,
        branch,
        middle,
        normed_two,
        inner_pre,
        active,
        mixed_out,
        slot_index,
        rows_exp,
        inner_exp,
        active_exp,
    )
    return (result.reshape(-1, model_width), saved)


def layer_backward(grad_tokens, saved, cond_act, lin, lout, expert_w, gate_vals):
    (
        tokens,
        mods,
        normed,
        qkv,
        attended,
        log_sums,
        branch,
        middle,
        normed_two,
        inner_pre,
        active,
        mixed_out,
        slot_index,
        rows_exp,
        inner_exp,
        active_exp,
    ) = saved
    item_count = cond_act.shape[0]
    model_width = tokens.shape[1]
    local_count = expert_w.shape[0]
    expert_count = lax.axis_size("expert") * local_count
    capacity = 4 * tokens.shape[0] // expert_count
    grad_shaped = grad_tokens.reshape(item_count, -1, model_width)
    grad_gate_two = jnp.sum(
        grad_shaped * mixed_out.reshape(item_count, -1, model_width), axis=1, keepdims=True
    )
    grad_mixed = (mods[:, 5] * grad_shaped).reshape(-1, model_width)
    grad_shared = to_half(grad_mixed)
    grad_lout = product_tn(active, grad_shared)
    grad_inner = to_half(gelu_back(inner_pre, product_nt(grad_shared, lout)))
    grad_w_up = product_tn(normed_two, grad_inner)
    grad_normed_two = product_nt(grad_inner, lin[:, 10 * model_width :])
    routed_grad = to_half(gate_vals[:, :, None] * grad_mixed[:, None, :]).reshape(-1, model_width)
    send_grad = (
        jnp.zeros((expert_count * capacity, model_width), jnp.bfloat16)
        .at[slot_index]
        .set(routed_grad)
    )
    received = lax.all_to_all(
        send_grad.reshape(expert_count, capacity, model_width),
        "expert",
        split_axis=0,
        concat_axis=0,
        tiled=True,
    )
    grad_rows = expert_major(received, local_count)
    grad_down_exp = jnp.einsum(
        "erd,erf->edf", grad_rows, active_exp, preferred_element_type=jnp.float32
    )
    grad_active_exp = jnp.einsum(
        "erd,edf->erf", grad_rows, expert_w[:, 1], preferred_element_type=jnp.float32
    )
    grad_inner_exp = to_half(gelu_back(inner_exp, grad_active_exp))
    grad_up_exp = jnp.einsum(
        "erd,erf->edf", rows_exp, grad_inner_exp, preferred_element_type=jnp.float32
    )
    grad_rows_in = to_half(
        jnp.einsum(
            "erf,edf->erd", grad_inner_exp, expert_w[:, 0], preferred_element_type=jnp.float32
        )
    )
    back_rows = lax.all_to_all(
        source_major(grad_rows_in, lax.axis_size("expert")),
        "expert",
        split_axis=0,
        concat_axis=0,
        tiled=True,
    )
    picked = (
        back_rows.reshape(-1, model_width)[slot_index]
        .astype(jnp.float32)
        .reshape(-1, 2, model_width)
    )
    grad_normed_two = grad_normed_two + jnp.sum(picked, axis=1)
    _, second_back = jax.vjp(norm_mod, middle, mods[:, 3], mods[:, 4])
    grad_middle, grad_shift_two, grad_scale_two = second_back(
        grad_normed_two.reshape(item_count, -1, model_width)
    )
    grad_middle = grad_middle + grad_shaped
    grad_gate_one = jnp.sum(
        grad_middle * branch.reshape(item_count, -1, model_width), axis=1, keepdims=True
    )
    grad_branch = to_half((mods[:, 2] * grad_middle).reshape(-1, model_width))
    grad_w_out = product_tn(attended, grad_branch)
    grad_attended = to_half(product_nt(grad_branch, lin[:, 3 * model_width : 4 * model_width]))
    grad_qkv = attention_backward(qkv, log_sums, grad_attended, item_count)
    grad_w_qkv = product_tn(normed, grad_qkv)
    grad_normed = product_nt(grad_qkv, lin[:, : 3 * model_width])
    _, first_back = jax.vjp(
        norm_mod, tokens.reshape(item_count, -1, model_width), mods[:, 0], mods[:, 1]
    )
    grad_input, grad_shift_one, grad_scale_one = first_back(
        grad_normed.reshape(item_count, -1, model_width)
    )
    grad_input = grad_input + grad_middle
    grad_mods = jnp.stack(
        [
            grad_shift_one,
            grad_scale_one,
            grad_gate_one,
            grad_shift_two,
            grad_scale_two,
            grad_gate_two,
        ],
        axis=1,
    )
    grad_mods = grad_mods.reshape(item_count, 6 * model_width)
    grad_ada = jnp.dot(cond_act.T, grad_mods, precision=highest)
    grad_cond = jnp.dot(
        grad_mods,
        lin[:, 4 * model_width : 10 * model_width].astype(jnp.float32).T,
        precision=highest,
    )
    grad_lin = jnp.concatenate([grad_w_qkv, grad_w_out, grad_ada, grad_w_up], axis=1)
    grad_expert = jnp.stack([grad_up_exp, grad_down_exp], axis=1)
    return (grad_input.reshape(-1, model_width), grad_cond, grad_lin, grad_lout, grad_expert)


def adam_step(weight_in, gradient, first_in, second_in):
    first_new = beta_one * first_in + (1.0 - beta_one) * gradient
    second_new = beta_two * second_in + (1.0 - beta_two) * gradient * gradient
    first_hat = first_new / (1.0 - beta_one**STEP)
    second_hat = second_new / (1.0 - beta_two**STEP)
    stepped = weight_in - inner_rate * (
        first_hat / (jnp.sqrt(second_hat) + eps_adam) + weight_decay * weight_in
    )
    return (weight_in - stepped, first_new, second_new)


def per_device(
    patches,
    target_noise,
    timesteps,
    labels,
    routes,
    route_gates,
    stem_weights,
    layer_in,
    layer_out,
    experts,
    stem_first,
    layer_in_first,
    layer_out_first,
    experts_first,
    stem_second,
    layer_in_second,
    layer_out_second,
    experts_second,
    stem_moment,
    layer_in_moment,
    layer_out_moment,
    experts_moment,
):
    stem_all, lin_all, lout_all = (
        lax.all_gather(to_half(stem_weights), ("expert", "dp"), axis=1, tiled=True),
        lax.all_gather(to_half(layer_in), ("expert", "dp"), axis=2, tiled=True),
        lax.all_gather(to_half(layer_out), ("expert", "dp"), axis=1, tiled=True),
    )
    expert_all = lax.all_gather(to_half(experts), "dp", axis=4, tiled=True)
    model_width = stem_all.shape[1]
    item_count = timesteps.shape[0]
    patch_w, time_one, time_two, table_w, final_ada, final_out = split_stem(stem_all)
    features = time_features(timesteps)
    hot_labels = label_table(labels)

    def condition(first_w, second_w, table_in):
        hidden_time = jax.nn.silu(jnp.dot(features, first_w, precision=highest))
        return jax.nn.silu(
            jnp.dot(hidden_time, second_w, precision=highest)
            + jnp.dot(hot_labels, table_in, precision=highest)
        )

    cond_act, cond_back = jax.vjp(
        condition,
        time_one.astype(jnp.float32),
        time_two.astype(jnp.float32),
        table_w.astype(jnp.float32),
    )
    tokens = product(patches, patch_w)
    tokens = (tokens.reshape(item_count, -1, model_width) + positions_table()[None]).reshape(
        -1, model_width
    )
    saved_all = []
    for layer_idx in range(LAYERS):
        tokens, saved = layer_forward(
            tokens,
            cond_act,
            lin_all[layer_idx],
            lout_all[layer_idx],
            expert_all[layer_idx],
            routes[layer_idx],
            route_gates[layer_idx],
        )
        saved_all.append(saved)
    final_ada_f = final_ada.astype(jnp.float32)
    final_mods = jnp.dot(cond_act, final_ada_f.T, precision=highest).reshape(
        item_count, 2, 1, model_width
    )
    final_pre, final_back = jax.vjp(
        norm_mod, tokens.reshape(item_count, -1, model_width), final_mods[:, 0], final_mods[:, 1]
    )
    final_normed = to_half(final_pre.reshape(-1, model_width))
    predicted = product_nt(final_normed, final_out)
    residual_err = predicted - target_noise
    loss_total = lax.psum(jnp.sum(residual_err * residual_err), ("group", "expert", "dp"))
    grad_pred = to_half(2.0 * residual_err)
    grad_final_out = product_tn(grad_pred, final_normed)
    grad_final_normed = product(grad_pred, final_out)
    grad_tokens, grad_fshift, grad_fscale = final_back(
        grad_final_normed.reshape(item_count, -1, model_width)
    )
    grad_tokens = grad_tokens.reshape(-1, model_width)
    grad_final_mods = jnp.concatenate([grad_fshift, grad_fscale], axis=1).reshape(
        item_count, 2 * model_width
    )
    grad_final_ada = jnp.dot(grad_final_mods.T, cond_act, precision=highest)
    grad_cond = jnp.dot(grad_final_mods, final_ada_f, precision=highest)
    lin_grads = []
    lout_grads = []
    expert_grads = []
    for layer_idx in reversed(range(LAYERS)):
        grad_tokens, grad_cond_layer, grad_lin, grad_lout, grad_expert = layer_backward(
            grad_tokens,
            saved_all[layer_idx],
            cond_act,
            lin_all[layer_idx],
            lout_all[layer_idx],
            expert_all[layer_idx],
            route_gates[layer_idx],
        )
        grad_cond = grad_cond + grad_cond_layer
        lin_grads.append(grad_lin)
        lout_grads.append(grad_lout)
        expert_grads.append(grad_expert)
    lin_stack = jnp.stack(lin_grads[::-1])
    lout_stack = jnp.stack(lout_grads[::-1])
    expert_stack = jnp.stack(expert_grads[::-1])
    grad_patch = product_tn(patches, to_half(grad_tokens))
    grad_time_one, grad_time_two, grad_table = cond_back(grad_cond)
    grad_stem = jnp.concatenate(
        [grad_patch, grad_time_one, grad_time_two, grad_table, grad_final_ada, grad_final_out],
        axis=0,
    )
    stem_sum, lin_sum, lout_sum = (
        lax.psum_scatter(grad_stem, ("expert", "dp"), scatter_dimension=1, tiled=True),
        lax.psum_scatter(lin_stack, ("expert", "dp"), scatter_dimension=2, tiled=True),
        lax.psum_scatter(lout_stack, ("expert", "dp"), scatter_dimension=1, tiled=True),
    )
    expert_sum = lax.psum_scatter(
        expert_stack.astype(jnp.bfloat16), "dp", scatter_dimension=4, tiled=True
    ).astype(jnp.float32)
    weights_all = (stem_weights, layer_in, layer_out, experts)
    gradients = (stem_sum, lin_sum, lout_sum, expert_sum)
    firsts = (stem_first, layer_in_first, layer_out_first, experts_first)
    seconds = (stem_second, layer_in_second, layer_out_second, experts_second)
    moments = (stem_moment, layer_in_moment, layer_out_moment, experts_moment)
    stepped = [
        adam_step(
            weights_all[array_idx],
            gradients[array_idx],
            firsts[array_idx][0],
            seconds[array_idx][0],
        )
        for array_idx in range(4)
    ]
    delta_all = (
        lax.psum(stepped[0][0].astype(jnp.bfloat16), "group").astype(jnp.float32),
        lax.psum(stepped[1][0].astype(jnp.bfloat16), "group").astype(jnp.float32),
        lax.psum(stepped[2][0].astype(jnp.bfloat16), "group").astype(jnp.float32),
        lax.psum(stepped[3][0].astype(jnp.bfloat16), "group").astype(jnp.float32),
    )
    group_count = lax.axis_size("group")
    new_weights = []
    new_moments = []
    for array_idx in range(4):
        mean_delta = delta_all[array_idx] / group_count
        moment_new = outer_mom * moments[array_idx] + mean_delta
        new_weights.append(
            weights_all[array_idx] - outer_rate * (mean_delta + outer_mom * moment_new)
        )
        new_moments.append(moment_new)
    return (
        loss_total,
        new_weights[0],
        new_weights[1],
        new_weights[2],
        new_weights[3],
        to_half(new_weights[0]),
        to_half(new_weights[1]),
        to_half(new_weights[2]),
        to_half(new_weights[3]),
        stepped[0][1][None],
        stepped[1][1][None],
        stepped[2][1][None],
        stepped[3][1][None],
        stepped[0][2][None],
        stepped[1][2][None],
        stepped[2][2][None],
        stepped[3][2][None],
        new_moments[0],
        new_moments[1],
        new_moments[2],
        new_moments[3],
    )


def solution(mesh):
    placed = (
        P(("group", "expert", "dp"), None),
        P(("group", "expert", "dp"), None),
        P(("group", "expert", "dp")),
        P(("group", "expert", "dp")),
        P(None, ("group", "expert", "dp"), None),
        P(None, ("group", "expert", "dp"), None),
        P(None, ("expert", "dp")),
        P(None, None, ("expert", "dp")),
        P(None, ("expert", "dp"), None),
        P(None, "expert", None, None, "dp"),
        P("group", None, ("expert", "dp")),
        P("group", None, None, ("expert", "dp")),
        P("group", None, ("expert", "dp"), None),
        P("group", None, "expert", None, None, "dp"),
        P("group", None, ("expert", "dp")),
        P("group", None, None, ("expert", "dp")),
        P("group", None, ("expert", "dp"), None),
        P("group", None, "expert", None, None, "dp"),
        P(None, ("expert", "dp")),
        P(None, None, ("expert", "dp")),
        P(None, ("expert", "dp"), None),
        P(None, "expert", None, None, "dp"),
    )
    return jax.shard_map(
        per_device,
        mesh=mesh,
        in_specs=placed,
        out_specs=(
            P(),
            P(None, ("expert", "dp")),
            P(None, None, ("expert", "dp")),
            P(None, ("expert", "dp"), None),
            P(None, "expert", None, None, "dp"),
            P(None, ("expert", "dp")),
            P(None, None, ("expert", "dp")),
            P(None, ("expert", "dp"), None),
            P(None, "expert", None, None, "dp"),
            P("group", None, ("expert", "dp")),
            P("group", None, None, ("expert", "dp")),
            P("group", None, ("expert", "dp"), None),
            P("group", None, "expert", None, None, "dp"),
            P("group", None, ("expert", "dp")),
            P("group", None, None, ("expert", "dp")),
            P("group", None, ("expert", "dp"), None),
            P("group", None, "expert", None, None, "dp"),
            P(None, ("expert", "dp")),
            P(None, None, ("expert", "dp")),
            P(None, ("expert", "dp"), None),
            P(None, "expert", None, None, "dp"),
        ),
        check_vma=False,
    )
```

profile of v0, /device:TPU:0, one launch (start us, length us, event | category | flops | bytes accessed | tf_op | source)
XLA Modules:
  0.0 2032.0 jit_solution(15394323592573038682)
XLA Ops:
  23.4 17.6 all-gather.5.cloned.1.call-done
  44.9 98.3 %all-gather.7.cloned.1.call-done = bf16[2,384,6912]{1,0,2:T(2,128)(2,1)} async-done(((bf16[2,384,864]{1,0,2:T(2,128)(2,1)}), bf16[2,384,6912]{1,0,2:T(2,128)(2,1)}) %all-gather.7.cloned.1.call-update) | async-done | bytes 10616848 | tf_op jit(solution)/shard_map/all_gather | solution.py:406
  143.2 21.6 %fusion.216 = (bf16[1,384,6912]{1,0,2:T(2,128)(2,1)}, bf16[1,384,6912]{1,0,2:T(2,128)(2,1)}) fusion(bf16[2,384,6912]{1,0,2:T(2,128)(2,1)} %all-gather.7.cloned.1.call-done), kind=kLoop, calls=%fused_computation.444 | loop fusion | bytes 21233664 | tf_op jit(solution)/shard_map/slice | solution.py:438
  164.9 21.7 %copy.342 = bf16[1,384,6912]{2,1,0:T(8,128)(2,1)} copy(bf16[1,384,6912]{1,0,2:T(2,128)(2,1)} %get-tuple-element.152) | data formatting | bytes 10616832
  222.5 11.9 scatter_custom_fusion
  246.7 102.2 %all-to-all-done = bf16[4,1024,384]{2,1,0:T(8,128)(2,1)} async-done(((bf16[4,1024,384]{2,1,0:T(8,128)(2,1)}), bf16[4,1024,384]{2,1,0:T(8,128)(2,1)}, u32[]{:S(2)}, u32[]{:S(2)}) %all-to-all-start) | async-done | bytes 3145760 | tf_op jit(solution)/shard_map/all_to_all | solution.py:199
  348.9 19.8 multiply_convert_fusion.1
  368.7 10.9 convolution_convert_fusion.3
  389.3 21.6 %copy.343 = bf16[1,384,6912]{2,1,0:T(8,128)(2,1)} copy(bf16[1,384,6912]{1,0,2:T(2,128)(2,1)} %get-tuple-element.151) | data formatting | bytes 10616832
  421.4 33.8 %all-to-all-done.1 = bf16[4,1024,384]{2,1,0:T(8,128)(2,1)} async-done(((bf16[4,1024,384]{2,1,0:T(8,128)(2,1)}), bf16[4,1024,384]{2,1,0:T(8,128)(2,1)}, u32[]{:S(2)}, u32[]{:S(2)}) %all-to-all-start.1) | async-done | bytes 3145760 | tf_op jit(solution)/shard_map/all_to_all | solution.py:214
  455.2 9.5 gather_fusion
  467.4 17.6 multiply_reduce_fusion.5
  485.0 8.6 fusion.84
  525.7 11.3 scatter_custom_fusion.1
  537.0 72.9 %all_to_all.40 = bf16[4,1024,384]{2,1,0:T(8,128)(2,1)S(1)} all-to-all(bf16[4,1024,384]{2,1,0:T(8,128)(2,1)S(1)} %bitcast.557), channel_id=1, replica_groups=mesh['group'=4,'expert'=4,'dp'=2] {'expert'}, dimensions={0} | all-to-all | bytes 6291456 | tf_op jit(solution)/shard_map/all_to_all | solution.py:199
  609.9 17.4 multiply_convert_fusion
  627.2 10.8 convolution_convert_fusion.2
  647.0 9.9 fusion.47
  656.9 54.7 %all-to-all-done.3 = bf16[4,1024,384]{2,1,0:T(8,128)(2,1)S(1)} async-done(((bf16[4,1024,384]{2,1,0:T(8,128)(2,1)}), bf16[4,1024,384]{2,1,0:T(8,128)(2,1)S(1)}, u32[]{:S(2)}, u32[]{:S(2)}) %all-to-all-start.3) | async-done | bytes 3145760 | tf_op jit(solution)/shard_map/all_to_all | solution.py:214
  711.7 9.1 gather_fusion.1
  724.3 17.3 multiply_reduce_fusion.4
  741.6 8.7 fusion.83
  769.1 12.4 scatter_custom_fusion.2
  781.5 74.4 %all_to_all.41 = bf16[4,1024,384]{2,1,0:T(8,128)(2,1)S(1)} all-to-all(bf16[4,1024,384]{2,1,0:T(8,128)(2,1)} %bitcast.556), channel_id=1, replica_groups=mesh['group'=4,'expert'=4,'dp'=2] {'expert'}, dimensions={0} | all-to-all | bytes 6291456 | tf_op jit(solution)/shard_map/all_to_all | solution.py:289
  855.9 23.5 %fusion.13 = bf16[4096,1536]{1,0:T(8,128)(2,1)} fusion(f32[4096,1536]{1,0:T(8,128)} %get-tuple-element.219, bf16[4096,384]{1,0:T(8,128)(2,1)S(1)} %bitcast.581, bf16[1,2,384,1536]{3,2,1,0:T(8,128)(2,1)S(1)} %copy-done.78), kind=kOutput, calls=%fused_computation.25 | convolution fusion | flops 4957667328 | bytes 42074112 | tf_op jit(solution)/shard_map/erd,edf->erf/dot_general | solution.py:300
  879.4 10.9 convolution_convert_fusion.1
  904.6 13.7 fusion.27
  918.3 45.6 %all-to-all-done.5 = bf16[4,1024,384]{2,1,0:T(8,128)(2,1)S(1)} async-done(((bf16[4,1024,384]{2,1,0:T(8,128)(2,1)}), bf16[4,1024,384]{2,1,0:T(8,128)(2,1)S(1)}, u32[]{:S(2)}, u32[]{:S(2)}) %all-to-all-start.5) | async-done | bytes 3145760 | tf_op jit(solution)/shard_map/all_to_all | solution.py:312
  963.9 9.1 gather_fusion.2
  1031.1 12.9 scatter_custom_fusion.3
  1049.0 8.4 fusion.39
  1057.4 8.4 fusion.38
  1067.5 10.9 fusion.20
  1078.4 40.7 %all-to-all-done.6 = bf16[4,1024,384]{2,1,0:T(8,128)(2,1)} async-done(((bf16[4,1024,384]{2,1,0:T(8,128)(2,1)}), bf16[4,1024,384]{2,1,0:T(8,128)(2,1)}, u32[]{:S(2)}, u32[]{:S(2)}) %all-to-all-start.6) | async-done | bytes 3145760 | tf_op jit(solution)/shard_map/all_to_all | solution.py:289
  1119.2 21.6 %fusion.6 = bf16[4096,1536]{1,0:T(8,128)(2,1)S(1)} fusion(f32[4096,1536]{1,0:T(8,128)} %get-tuple-element.214, bf16[4096,384]{1,0:T(8,128)(2,1)} %bitcast.69, bf16[1,2,384,1536]{3,2,1,0:T(8,128)(2,1)S(1)} %copy-done.76), kind=kOutput, calls=%fused_computation.18 | convolution fusion | flops 4957667328 | bytes 42074112 | tf_op jit(solution)/shard_map/erd,edf->erf/dot_general | solution.py:300
  1140.8 8.4 convolution_convert_fusion
  1156.3 9.2 fusion.37
  1177.0 46.2 %all-to-all-done.7 = bf16[4,1024,384]{2,1,0:T(8,128)(2,1)S(1)} async-done(((bf16[4,1024,384]{2,1,0:T(8,128)(2,1)}), bf16[4,1024,384]{2,1,0:T(8,128)(2,1)S(1)}, u32[]{:S(2)}, u32[]{:S(2)}) %all-to-all-start.7) | async-done | bytes 3145760 | tf_op jit(solution)/shard_map/all_to_all | solution.py:312
  1223.2 9.3 gather_fusion.3
  1290.8 10.5 concatenate.30
  1306.9 8.7 convolution_bitcast_fusion
  1315.6 8.1 convolution_bitcast_fusion.1
  1364.0 32.4 %copy.299 = f32[2,384,6912]{1,0,2:T(2,128)} copy(f32[2,384,6912]{2,1,0:T(8,128)} %pad_maximum_fusion) | data formatting | bytes 42467328 | tf_op jit(solution)/shard_map/stack | solution.py:485
  1402.1 11.6 fusion.40
  1421.0 32.6 %reduce-scatter.6.cloned.1.call-done = f32[2,384,384]{2,1,0:T(8,128)} async-done(((f32[2,3072,384]{2,1,0:T(8,128)}), f32[2,384,384]{2,1,0:T(8,128)}) %reduce-scatter.6.cloned.1.call-update) | async-done | bytes 1179664 | tf_op jit(solution)/shard_map/reduce_scatter | solution.py:497
  1458.2 413.0 %all-reduce.5.cloned.1.call-done = f32[2,384,6912]{1,0,2:T(2,128)} async-done(((f32[2,384,6912]{1,0,2:T(2,128)}), f32[2,384,6912]{1,0,2:T(2,128)}) %all-reduce.5.cloned.1.call-update) | async-done | bytes 21233680
  1882.9 40.8 %psum.35 = f32[]{:T(128)} all-reduce(f32[]{:T(128)} %get-tuple-element.220), channel_id=1, replica_groups=mesh['group'=4,'expert'=4,'dp'=2] {'group','expert','dp'}, use_global_device_ids=true, to_apply=%region_25.26 | all-reduce | flops 1 | bytes 8 | tf_op jit(solution)/shard_map/psum | solution.py:455
  1928.6 69.3 %all-reduce.7.cloned.1.call-done = (bf16[2441,48]{1,0:T(8,128)(2,1)}, bf16[2,384,864]{1,2,0:T(8,128)(2,1)}, bf16[2,384,384]{2,1,0:T(8,128)(2,1)}, bf16[2,1,2,384,768]{4,3,2,1,0:T(8,128)(2,1)}) async-done(((bf16[2441,48]{1,0:T(8,128)(2,1)}, bf16[2,384,864]{1,2,0:T(8,128)(2,1)}, bf16[2,384,384]{2,1,0:T(8,128)(2,1)}, bf16[2,1,2,384,768]{4,3,2,1,0:T(8,128)(2,1)}), (bf16[2441,48]{1,0:T(8,128)(2,1)}, ...) | async-done | bytes 4510576 | tf_op jit(solution)/shard_map/psum | solution.py:517
  (632 shorter events, 414.5 us)
Async XLA Ops:
  7.2 33.8 %copy-start = (bf16[1024,16]{0,1:T(8,128)(2,1)S(1)}, bf16[1024,16]{0,1:T(8,128)(2,1)}, u32[]{:S(2)}) copy-start(bf16[1024,16]{0,1:T(8,128)(2,1)} %param.22) | copy-start | bytes 98308
  7.2 33.8 %all-gather.5.cloned.1.call-start = ((), (), s32[]{:S(2)}) async-start(), calls=%async_computation.11 | async-start | bytes 2211840 | tf_op jit(solution)/shard_map/all_gather | solution.py:405
  9.0 134.2 %all-gather.7.cloned.1.call-start = ((), (), s32[]{:S(2)}) async-start(), calls=%async_computation.12 | async-start | bytes 11943936 | tf_op jit(solution)/shard_map/all_gather | solution.py:406
  14.0 227.8 %all-gather.11.cloned.1.call-start = ((), (), s32[]{:S(2)}) async-start(), calls=%async_computation.14 | async-start | bytes 7077888 | tf_op jit(solution)/shard_map/all_gather | solution.py:409
  22.0 21.7 %copy-start.146 = (f32[4,128]{1,0:T(4,128)}, f32[4,128]{1,0:T(4,128)S(1)}, u32[]{:S(2)}) copy-start(f32[4,128]{1,0:T(4,128)S(1)} %get-tuple-element.203) | copy-start | bytes 6148
  22.0 21.7 %copy-start.148 = (f32[4,128]{1,0:T(4,128)}, f32[4,128]{1,0:T(4,128)S(1)}, u32[]{:S(2)}) copy-start(f32[4,128]{1,0:T(4,128)S(1)} %get-tuple-element.204) | copy-start | bytes 6148
  22.1 367.1 %copy-start.143 = (s32[2048,1]{0,1:T(1,128)}, s32[2048,1]{0,1:T(1,128)S(1)}, u32[]{:S(2)}) copy-start(s32[2048,1]{0,1:T(1,128)S(1)} %compare_select_fusion.1) | copy-start | bytes 24580
  23.3 165.6 %copy-start.21 = (f32[256,384]{1,0:T(8,128)}, f32[256,384]{1,0:T(8,128)S(1)}, u32[]{:S(2)}) copy-start(f32[256,384]{1,0:T(8,128)S(1)} %pad_maximum_fusion.3) | copy-start | bytes 1179652
  23.3 21.1 %copy-start.153 = (s32[4]{0:T(128)S(1)}, s32[4]{0:T(128)}, u32[]{:S(2)}) copy-start(s32[4]{0:T(128)} %param.25) | copy-start | bytes 52
  42.6 168.6 %copy-start.14 = (f32[1024,384]{1,0:T(8,128)}, f32[1024,384]{1,0:T(8,128)S(1)}, u32[]{:S(2)}) copy-start(f32[1024,384]{1,0:T(8,128)S(1)} %get-tuple-element.208) | copy-start | bytes 4718596
  42.6 146.4 %copy-start.117 = (f32[1024]{0:T(1024)}, f32[1024]{0:T(1024)S(1)}, u32[]{:S(2)}) copy-start(f32[1024]{0:T(1024)S(1)} %broadcast_multiply_fusion.7) | copy-start | bytes 12292
  44.0 120.9 %copy-start.126 = (f32[4,384]{1,0:T(4,128)}, f32[4,384]{1,0:T(4,128)S(1)}, u32[]{:S(2)}) copy-start(f32[4,384]{1,0:T(4,128)S(1)} %fusion.145) | copy-start | bytes 18436
  44.9 857.1 %copy-start.96 = (f32[4,384]{1,0:T(4,128)}, f32[4,384]{1,0:T(4,128)S(1)}, u32[]{:S(2)}) copy-start(f32[4,384]{1,0:T(4,128)S(1)} %convolution_add_fusion) | copy-start | bytes 18436
  188.9 22.3 %copy-start.128 = (f32[4,1,1,384]{3,0,1,2:T(4,128)}, f32[4,1,1,384]{3,0,1,2:T(4,128)S(1)}, u32[]{:S(2)}) copy-start(f32[4,1,1,384]{3,0,1,2:T(4,128)S(1)} %copy.431) | copy-start | bytes 18436
  214.3 279.3 %copy-start.3 = (f32[4,256,384]{2,1,0:T(8,128)}, f32[4,256,384]{2,1,0:T(8,128)S(1)}, u32[]{:S(2)}) copy-start(f32[4,256,384]{2,1,0:T(8,128)S(1)} %get-tuple-element.211) | copy-start | bytes 4718596
  215.9 197.4 %copy-start.24 = (bf16[4,256,384]{2,1,0:T(8,128)(2,1)}, bf16[4,256,384]{2,1,0:T(8,128)(2,1)S(1)}, u32[]{:S(2)}) copy-start(bf16[4,256,384]{2,1,0:T(8,128)(2,1)S(1)} %add_convert_fusion.4) | copy-start | bytes 2359300
  234.5 114.4 %all-to-all-start = ((bf16[4,1024,384]{2,1,0:T(8,128)(2,1)}), bf16[4,1024,384]{2,1,0:T(8,128)(2,1)}, u32[]{:S(2)}, u32[]{:S(2)}) async-start(bf16[4,1024,384]{2,1,0:T(8,128)(2,1)} %bitcast.555), calls=%async_computation | async-start | bytes 6291456 | tf_op jit(solution)/shard_map/all_to_all | solution.py:199
  239.5 245.5 %all-gather.9.cloned.1.call-start = ((), (), s32[]{:S(2)}) async-start(), calls=%async_computation.13 | async-start | bytes 5308416 | tf_op jit(solution)/shard_map/all_gather | solution.py:407
  348.9 19.8 copy-start.75
  379.6 75.6 %all-to-all-start.1 = ((bf16[4,1024,384]{2,1,0:T(8,128)(2,1)}), bf16[4,1024,384]{2,1,0:T(8,128)(2,1)}, u32[]{:S(2)}, u32[]{:S(2)}) async-start(bf16[4,1024,384]{2,1,0:T(8,128)(2,1)} %bitcast.583), calls=%async_computation.1 | async-start | bytes 6291456 | tf_op jit(solution)/shard_map/all_to_all | solution.py:214
  389.2 65.9 %copy-start.113 = (s32[2048]{0:T(1024)}, s32[2048]{0:T(1024)S(1)}, u32[]{:S(2)}) copy-start(s32[2048]{0:T(1024)S(1)} %broadcast_clamp_fusion.1) | copy-start | bytes 24580
  389.3 104.4 %copy-start.124 = (f32[4,1,1,384]{3,0,1,2:T(4,128)}, f32[4,1,1,384]{3,0,1,2:T(4,128)S(1)}, u32[]{:S(2)}) copy-start(f32[4,1,1,384]{3,0,1,2:T(4,128)S(1)} %copy.430) | copy-start | bytes 18436
  413.3 104.6 %copy-start.130 = (f32[4,1,1,384]{3,0,1,2:T(4,128)}, f32[4,1,1,384]{3,0,1,2:T(4,128)S(1)}, u32[]{:S(2)}) copy-start(f32[4,1,1,384]{3,0,1,2:T(4,128)S(1)} %copy.429) | copy-start | bytes 18436
  413.3 81.9 %copy-start.109 = (f32[4,1,1,384]{3,0,1,2:T(4,128)}, f32[4,1,1,384]{3,0,1,2:T(4,128)S(1)}, u32[]{:S(2)}) copy-start(f32[4,1,1,384]{3,0,1,2:T(4,128)S(1)} %copy.428) | copy-start | bytes 18436
  413.3 108.1 %copy-start.100 = (f32[4,384]{1,0:T(4,128)}, f32[4,384]{1,0:T(4,128)S(1)}, u32[]{:S(2)}) copy-start(f32[4,384]{1,0:T(4,128)S(1)} %get-tuple-element.237) | copy-start | bytes 18436
  494.8 23.1 %copy-start.12 = (f32[4,256,384]{2,1,0:T(8,128)}, f32[4,256,384]{2,1,0:T(8,128)S(1)}, u32[]{:S(2)}) copy-start(f32[4,256,384]{2,1,0:T(8,128)S(1)} %get-tuple-element.150) | copy-start | bytes 4718596
  537.0 72.9 %copy-start.77 = (bf16[1,2,384,1536]{3,2,1,0:T(8,128)(2,1)S(1)}, bf16[1,2,384,1536]{3,2,1,0:T(8,128)(2,1)}, u32[]{:S(2)}) copy-start(bf16[1,2,384,1536]{3,2,1,0:T(8,128)(2,1)} %get-tuple-element.159) | copy-start | bytes 7077892
  638.1 73.6 %all-to-all-start.3 = ((bf16[4,1024,384]{2,1,0:T(8,128)(2,1)}), bf16[4,1024,384]{2,1,0:T(8,128)(2,1)S(1)}, u32[]{:S(2)}, u32[]{:S(2)}) async-start(bf16[4,1024,384]{2,1,0:T(8,128)(2,1)} %bitcast.586), calls=%async_computation.3 | async-start | bytes 6291456 | tf_op jit(solution)/shard_map/all_to_all | solution.py:214
  781.5 74.4 %copy-start.78 = (bf16[1,2,384,1536]{3,2,1,0:T(8,128)(2,1)S(1)}, bf16[1,2,384,1536]{3,2,1,0:T(8,128)(2,1)}, u32[]{:S(2)}) copy-start(bf16[1,2,384,1536]{3,2,1,0:T(8,128)(2,1)} %get-tuple-element.159) | copy-start | bytes 7077892
  855.9 23.5 %copy-start.69 = (bf16[4,1024,384]{2,1,0:T(8,128)(2,1)}, bf16[4,1024,384]{2,1,0:T(8,128)(2,1)S(1)}, u32[]{:S(2)}) copy-start(bf16[4,1024,384]{2,1,0:T(8,128)(2,1)S(1)} %all_to_all.41) | copy-start | bytes 9437188
  890.3 73.5 %all-to-all-start.5 = ((bf16[4,1024,384]{2,1,0:T(8,128)(2,1)}), bf16[4,1024,384]{2,1,0:T(8,128)(2,1)S(1)}, u32[]{:S(2)}, u32[]{:S(2)}) async-start(bf16[4,1024,384]{2,1,0:T(8,128)(2,1)} %bitcast.585), calls=%async_computation.5 | async-start | bytes 6291456 | tf_op jit(solution)/shard_map/all_to_all | solution.py:312
  897.1 21.2 %copy-start.140 = (f32[4,256]{1,0:T(4,128)}, f32[4,256]{1,0:T(4,128)S(1)}, u32[]{:S(2)}) copy-start(f32[4,256]{1,0:T(4,128)S(1)} %add.522) | copy-start | bytes 12292
  1044.0 75.1 %all-to-all-start.6 = ((bf16[4,1024,384]{2,1,0:T(8,128)(2,1)}), bf16[4,1024,384]{2,1,0:T(8,128)(2,1)}, u32[]{:S(2)}, u32[]{:S(2)}) async-start(bf16[4,1024,384]{2,1,0:T(8,128)(2,1)} %bitcast.68), calls=%async_computation.6 | async-start | bytes 6291456 | tf_op jit(solution)/shard_map/all_to_all | solution.py:289
  1049.0 18.5 slice-start.6
  1049.0 18.5 slice-start.7
  1049.0 18.5 slice-start.11
  1067.5 51.7 %copy-start.76 = (bf16[1,2,384,1536]{3,2,1,0:T(8,128)(2,1)S(1)}, bf16[1,2,384,1536]{3,2,1,0:T(8,128)(2,1)}, u32[]{:S(2)}) copy-start(bf16[1,2,384,1536]{3,2,1,0:T(8,128)(2,1)} %get-tuple-element.160) | copy-start | bytes 7077892
  1149.3 74.0 %all-to-all-start.7 = ((bf16[4,1024,384]{2,1,0:T(8,128)(2,1)}), bf16[4,1024,384]{2,1,0:T(8,128)(2,1)S(1)}, u32[]{:S(2)}, u32[]{:S(2)}) async-start(bf16[4,1024,384]{2,1,0:T(8,128)(2,1)} %bitcast.584), calls=%async_computation.7 | async-start | bytes 6291456 | tf_op jit(solution)/shard_map/all_to_all | solution.py:312
  1153.1 249.0 %reduce-scatter.8.cloned.1.call-start = ((), (), s32[]{:S(2)}) async-start(), calls=%async_computation.16 | async-start | bytes 7077888 | tf_op jit(solution)/shard_map/reduce_scatter | solution.py:499
  1176.9 46.3 %copy-start.114 = (s32[2048]{0:T(1024)S(1)}, s32[2048]{0:T(1024)}, u32[]{:S(2)}) copy-start(s32[2048]{0:T(1024)} %copy-done.113) | copy-start | bytes 24580
  1176.9 236.8 %reduce-scatter.10.cloned.1.call-start = ((), (), s32[]{:S(2)}) async-start(), calls=%async_computation.17 | async-start | bytes 4423680
  1306.8 146.8 %reduce-scatter.6.cloned.1.call-start = ((), (), s32[]{:S(2)}) async-start(), calls=%async_computation.15 | async-start | bytes 10616832 | tf_op jit(solution)/shard_map/reduce_scatter | solution.py:497
  1328.0 543.2 %all-reduce.5.cloned.1.call-start = ((), (), s32[]{:S(2)}) async-start(), calls=%async_computation.18 | async-start | bytes 42467328
  1396.5 601.5 %all-reduce.7.cloned.1.call-start = ((), (), s32[]{:S(2)}) async-start(), calls=%async_computation.19 | async-start | bytes 9805824 | tf_op jit(solution)/shard_map/psum | solution.py:517
  1397.9 18.3 copy-start.34
  1416.2 37.5 %copy-start.35 = (f32[2,384,384]{2,1,0:T(8,128)S(1)}, f32[2,384,384]{2,1,0:T(8,128)}, u32[]{:S(2)}) copy-start(f32[2,384,384]{2,1,0:T(8,128)} %param.30) | copy-start | bytes 3538948
  1458.2 415.8 %copy-start.16 = (f32[2,384,864]{1,2,0:T(8,128)S(1)}, f32[2,384,864]{1,2,0:T(8,128)}, u32[]{:S(2)}) copy-start(f32[2,384,864]{1,2,0:T(8,128)} %param.29) | copy-start | bytes 7962628
  1998.0 18.6 slice-start.4
  (141 other events, 523.9 us)
Sparse Core Ops, SparseCore 0:
  10.3 30.7 all-gather.4
  43.2 99.9 all-gather.6
  145.4 12.7 all-gather.10
  242.3 94.2 all-gather.8
  1177.0 13.9 reduce-scatter.7
  1306.9 46.5 reduce-scatter.9
  1355.9 97.6 reduce-scatter.5
  1456.3 414.9 all-reduce.4
  1880.6 117.3 all-reduce.6
where the time goes:
time: 2040 us; the launch traced here: 2030 us
  waiting for transfers between devices  954 us (47%)
  matrix products  343 us (17%)
  local copies, waits for them, and re-layouts  324 us (16%)
  blocking collectives  188 us (9%)
  other arithmetic  178 us (9%)
  starting transfers between devices  27 us (1%)
    unnamed x11, waiting for transfers between devices  413 us
    unnamed x388, local copies, waits for them, and re-layouts  109 us
    all_to_all x1, waiting for transfers between devices, layer_forward(): lax.all_to_all(send_rows.reshape(expert_count, capacity, model_width), 'e...  102 us
    all_gather x1, waiting for transfers between devices, per_device(): lax.all_gather(to_half(layer_in), ('expert', 'dp'), axis=2, tiled=True)  98.3 us
    all_to_all x2, waiting for transfers between devices, layer_backward(): lax.all_to_all(source_major(grad_rows_in, lax.axis_size('expert')), 'expe...  91.8 us
    all_to_all x2, waiting for transfers between devices, layer_forward(): lax.all_to_all(source_major(out_exp, lax.axis_size('expert')), 'expert',...  88.5 us
    all_to_all x1, blocking collectives, layer_backward(): lax.all_to_all(send_grad.reshape(expert_count, capacity, model_width), 'e...  74.4 us
    all_to_all x1, blocking collectives, layer_forward(): lax.all_to_all(send_rows.reshape(expert_count, capacity, model_width), 'e...  72.9 us
  transfers between devices with their start and end apart: 15, of which 11 were waited for; matrix products, arithmetic and copies ran while one was open for 25% of the time, Pallas kernels for 0%

commit v1 on v0

--- a/solution.py
+++ b/solution.py
@@ -1,6 +1,10 @@
+import functools
+
 import jax
 import jax.numpy as jnp
 from jax import lax
+from jax.experimental import pallas as pl
+from jax.experimental.pallas import tpu as pltpu
 from jax.sharding import PartitionSpec as P
 
 D = 384
@@ -554,6 +558,674 @@
     )
 
 
+bf16 = jnp.bfloat16
+f32 = jnp.float32
+MIB = 1024 * 1024
+CHUNK = 768
+STEM_SIZES = (PATCH_DIM, FREQ, D, CLASSES + 1, 2 * D, PATCH_DIM)
+STEM_PADDED = tuple(-(-size // 128) * 128 for size in STEM_SIZES)
+STEM_AT = tuple(sum(STEM_PADDED[:place]) for place in range(len(STEM_PADDED)))
+STEM_LANES = sum(STEM_PADDED)
+
+
+def dot_nn(left_in, right_in):
+    return lax.dot_general(left_in, right_in, (((1,), (0,)), ((), ())), preferred_element_type=f32)
+
+
+def dot_nt(left_in, right_in):
+    return lax.dot_general(left_in, right_in, (((1,), (1,)), ((), ())), preferred_element_type=f32)
+
+
+def dot_tn(left_in, right_in):
+    return lax.dot_general(left_in, right_in, (((0,), (0,)), ((), ())), preferred_element_type=f32)
+
+
+def three_parts(rows):
+    high = rows.astype(bf16).astype(f32)
+    rest = rows - high
+    mid = rest.astype(bf16).astype(f32)
+    low = rest - mid
+    return jnp.concatenate([high, mid, low, jnp.zeros_like(low)], axis=0).astype(bf16)
+
+
+def three_sum(stacked):
+    return stacked[0:8] + stacked[8:16] + stacked[16:24]
+
+
+def full_nt(rows, weight):
+    return three_sum(dot_nt(three_parts(rows), weight))
+
+
+def full_nn(rows, weight):
+    return three_sum(dot_nn(three_parts(rows), weight))
+
+
+def silu_slope(values):
+    gate = 1.0 / (1.0 + jnp.exp(-values))
+    return gate * (1.0 + values * (1.0 - gate))
+
+
+def silu_of(values):
+    return values / (1.0 + jnp.exp(-values))
+
+
+def stem_piece(stem_ref, place):
+    return stem_ref[:, STEM_AT[place] : STEM_AT[place] + STEM_PADDED[place]]
+
+
+def cond_kernel(feat_ref, hot_ref, stem_ref, ada_a, ada_b, cond_ref, hid_ref, one_ref, two_ref, mods_ref, fin_ref):
+    pre_one = full_nt(feat_ref[...], stem_piece(stem_ref, 1))
+    hidden = silu_of(pre_one)
+    pre_two = full_nt(hidden, stem_piece(stem_ref, 2)) + dot_nt(hot_ref[...], stem_piece(stem_ref, 3))[0:8]
+    cond = silu_of(pre_two)
+    one_ref[...] = pre_one
+    two_ref[...] = pre_two
+    hid_ref[...] = hidden
+    cond_ref[...] = cond
+    parts = three_parts(cond)
+    for place in range(6):
+        rows = pl.ds(place * D, D)
+        mods_ref[0, :, rows] = three_sum(dot_nt(parts, ada_a[rows, :]))
+        mods_ref[1, :, rows] = three_sum(dot_nt(parts, ada_b[rows, :]))
+    fin_ref[...] = three_sum(dot_nn(parts, stem_piece(stem_ref, 4)))
+
+
+def cond_back_kernel(gm_a, gm_b, gf_ref, one_ref, two_ref, stem_ref, ada_a, ada_b, done_ref, dtwo_ref):
+    grad_cond = full_nt(gf_ref[...], stem_piece(stem_ref, 4))
+    grad_cond = grad_cond + full_nn(gm_a[...], ada_a[...]) + full_nn(gm_b[...], ada_b[...])
+    dtwo = grad_cond * silu_slope(two_ref[...])
+    dtwo_ref[...] = dtwo
+    dhid = full_nn(dtwo, stem_piece(stem_ref, 2))
+    done_ref[...] = dhid * silu_slope(one_ref[...])
+
+
+def norm_parts(values):
+    centre = values - jnp.mean(values, axis=-1, keepdims=True)
+    spread = jnp.mean(centre * centre, axis=-1, keepdims=True)
+    root = lax.rsqrt(spread + ln_eps)
+    return centre * root, root
+
+
+def norm_back(values, scale_in, gradient):
+    unit, root = norm_parts(values)
+    grad_unit = gradient * (1.0 + scale_in)
+    inner = jnp.mean(grad_unit * unit, axis=-1, keepdims=True)
+    grad_in = root * (grad_unit - jnp.mean(grad_unit, axis=-1, keepdims=True) - unit * inner)
+    return (
+        grad_in,
+        jnp.sum(gradient, axis=0, keepdims=True),
+        jnp.sum(gradient * unit, axis=0, keepdims=True),
+    )
+
+
+def mod_row(mods_ref, item, place):
+    return mods_ref[pl.ds(item, 1), place * D : (place + 1) * D]
+
+
+def head_masks():
+    lane = lax.broadcasted_iota(jnp.int32, (1, 128), 1)
+    return lane, [(lane // 64 == half).astype(f32).astype(bf16) for half in range(2)]
+
+
+def attn_fwd_kernel(x_ref, mods_ref, w_ref, normed_ref, qkv_ref, att_ref, branch_ref, mid_ref, n2_ref):
+    item = pl.program_id(0)
+    tokens = x_ref[...]
+    unit, _ = norm_parts(tokens)
+    normed = (unit * (1.0 + mod_row(mods_ref, item, 1)) + mod_row(mods_ref, item, 0)).astype(bf16)
+    normed_ref[...] = normed
+    qkv_ref[...] = dot_nt(normed, w_ref[0 : 3 * D, :]).astype(bf16)
+    lane, masks = head_masks()
+    for pair in range(HEADS // 2):
+        at = pair * 128
+        queries = qkv_ref[:, at : at + 128]
+        keys = qkv_ref[:, D + at : D + at + 128]
+        vals = qkv_ref[:, 2 * D + at : 2 * D + at + 128]
+        outs = []
+        for half in range(2):
+            scores = dot_nt(queries * masks[half], keys) * 0.125
+            powers = jnp.exp(scores - jnp.max(scores, axis=-1, keepdims=True))
+            probs = (powers * (1.0 / jnp.sum(powers, axis=-1, keepdims=True))).astype(bf16)
+            outs.append(dot_nn(probs, vals))
+        att_ref[:, at : at + 128] = jnp.where(lane < 64, outs[0], outs[1]).astype(bf16)
+    branch = dot_nt(att_ref[...], w_ref[3 * D : 4 * D, :])
+    branch_ref[...] = branch
+    middle = tokens + mod_row(mods_ref, item, 2) * branch
+    mid_ref[...] = middle
+    unit, _ = norm_parts(middle)
+    n2_ref[...] = (unit * (1.0 + mod_row(mods_ref, item, 4)) + mod_row(mods_ref, item, 3)).astype(bf16)
+
+
+def attn_bwd_kernel(
+    gn2_ref, g_ref, mid_ref, x_ref, normed_ref, qkv_ref, att_ref, branch_ref, mods_ref, gg_ref, w_ref,
+    gx_ref, gmods_ref, dw_ref, dqkv, acc,
+):
+    item = pl.program_id(0)
+
+    @pl.when(item == 0)
+    def _():
+        acc[...] = jnp.zeros_like(acc)
+        gmods_ref[...] = jnp.zeros_like(gmods_ref)
+
+    grad_mid, dshift, dscale = norm_back(mid_ref[...], mod_row(mods_ref, item, 4), gn2_ref[...])
+    grad_mid = grad_mid + g_ref[...]
+    dgate = jnp.sum(grad_mid * branch_ref[...], axis=0, keepdims=True)
+    gmods_ref[pl.ds(item, 1), 2 * D : 3 * D] = dgate
+    gmods_ref[pl.ds(item, 1), 3 * D : 4 * D] = dshift
+    gmods_ref[pl.ds(item, 1), 4 * D : 5 * D] = dscale
+    gmods_ref[pl.ds(item, 1), 5 * D : 6 * D] = gg_ref[pl.ds(item, 1), :]
+    grad_branch = (mod_row(mods_ref, item, 2) * grad_mid).astype(bf16)
+    acc[3 * D : 4 * D, :] += dot_tn(grad_branch, att_ref[...])
+    grad_att = dot_nn(grad_branch, w_ref[3 * D : 4 * D, :]).astype(bf16)
+    lane, masks = head_masks()
+    for pair in range(HEADS // 2):
+        at = pair * 128
+        queries = qkv_ref[:, at : at + 128]
+        keys = qkv_ref[:, D + at : D + at + 128]
+        vals = qkv_ref[:, 2 * D + at : 2 * D + at + 128]
+        grad_out = grad_att[:, at : at + 128]
+        parts = []
+        for half in range(2):
+            scores = dot_nt(queries * masks[half], keys) * 0.125
+            powers = jnp.exp(scores - jnp.max(scores, axis=-1, keepdims=True))
+            probs = powers * (1.0 / jnp.sum(powers, axis=-1, keepdims=True))
+            grad_vals = dot_tn(probs.astype(bf16), grad_out)
+            grad_probs = dot_nt(grad_out * masks[half], vals)
+            inner = jnp.sum(probs * grad_probs, axis=-1, keepdims=True)
+            grad_scores = (probs * (grad_probs - inner)).astype(bf16)
+            parts.append((dot_nn(grad_scores, keys) * 0.125, dot_tn(grad_scores, queries) * 0.125, grad_vals))
+        for place in range(3):
+            dqkv[:, place * D + at : place * D + at + 128] = jnp.where(
+                lane < 64, parts[0][place], parts[1][place]
+            ).astype(bf16)
+    acc[0 : 3 * D, :] += dot_tn(dqkv[...], normed_ref[...])
+    grad_normed = dot_nn(dqkv[...], w_ref[0 : 3 * D, :])
+    grad_in, dshift, dscale = norm_back(x_ref[...], mod_row(mods_ref, item, 1), grad_normed)
+    gx_ref[...] = grad_in + grad_mid
+    gmods_ref[pl.ds(item, 1), 0:D] = dshift
+    gmods_ref[pl.ds(item, 1), D : 2 * D] = dscale
+
+    @pl.when(item == pl.num_programs(0) - 1)
+    def _():
+        dw_ref[...] = acc[...].astype(bf16)
+
+
+def gelu_both(values):
+    outer = 0.7978845608028654
+    cubic = outer * 0.044715
+    square = values * values
+    angle = jnp.tanh(values * (square * cubic + outer))
+    half = 0.5 * values
+    active = half * angle + half
+    slope = half * (square * (3.0 * cubic) + outer) * (1.0 - angle * angle) + (0.5 * angle + 0.5)
+    return active.astype(bf16), slope.astype(bf16)
+
+
+def gate_column(g4_ref, rows, expert):
+    gates = g4_ref[rows, :]
+    lane = lax.broadcasted_iota(jnp.int32, gates.shape, 1)
+    return jnp.sum(jnp.where(lane == expert, gates, 0.0), axis=1, keepdims=True)
+
+
+def ffn_fwd_kernel(shared_steps, halves, n2_ref, mid_ref, mods_ref, g4_ref, up_ref, dn_ref, ex_ref, act_ref, dg_ref, mixed_ref, x_ref, acc, racc):
+    step = pl.program_id(0)
+    items = n2_ref.shape[0] // PATCHES
+
+    @pl.when(step < shared_steps)
+    def _():
+        for item in range(items):
+            rows = pl.ds(item * PATCHES, PATCHES)
+            active, slope = gelu_both(dot_nt(n2_ref[rows, :], up_ref[...]))
+            act_ref[0, rows, :] = active
+            dg_ref[0, rows, :] = slope
+            part = dot_nn(active, dn_ref[...])
+
+            @pl.when(step == 0)
+            def _():
+                acc[rows, :] = part
+
+            @pl.when(step > 0)
+            def _():
+                acc[rows, :] += part
+
+    @pl.when(step >= shared_steps)
+    def _():
+        expert, half = (step - shared_steps) // halves, (step - shared_steps) % halves
+        for item in range(items):
+            rows = pl.ds(item * PATCHES, PATCHES)
+            active, slope = gelu_both(dot_nn(n2_ref[rows, :], ex_ref[0, 0]))
+            act_ref[0, rows, :] = active
+            dg_ref[0, rows, :] = slope
+            part = dot_nt(active, ex_ref[0, 1])
+
+            @pl.when(half == 0)
+            def _():
+                racc[rows, :] = part
+
+            @pl.when(half > 0)
+            def _():
+                routed = (racc[rows, :] + part).astype(bf16).astype(f32)
+                acc[rows, :] += gate_column(g4_ref, rows, expert) * routed
+
+    @pl.when(step == pl.num_programs(0) - 1)
+    def _():
+        mixed_ref[...] = acc[...]
+        for item in range(items):
+            rows = pl.ds(item * PATCHES, PATCHES)
+            x_ref[rows, :] = mid_ref[rows, :] + mod_row(mods_ref, item, 5) * acc[rows, :]
+
+
+def ffn_bwd_kernel(
+    shared_steps, halves, g_ref, n2_ref, mods_ref, g4_ref, mixed_ref, act_ref, dg_ref, up_ref, dn_ref, ex_ref,
+    dup_ref, ddn_ref, dex_ref, gn2_ref, gg_ref, gmix, gs, gst, n2t, din, acc, racc,
+):
+    step = pl.program_id(0)
+    items = n2_ref.shape[0] // PATCHES
+
+    @pl.when(step == 0)
+    def _():
+        gg_ref[...] = jnp.zeros_like(gg_ref)
+        for item in range(items):
+            rows = pl.ds(item * PATCHES, PATCHES)
+            grad = g_ref[rows, :]
+            gg_ref[pl.ds(item, 1), :] = jnp.sum(grad * mixed_ref[rows, :], axis=0, keepdims=True)
+            grad = mod_row(mods_ref, item, 5) * grad
+            gmix[rows, :] = grad
+            gs[rows, :] = grad.astype(bf16)
+            gst[:, rows] = grad.astype(bf16).T
+            n2t[:, rows] = n2_ref[rows, :].T
+        acc[...] = jnp.zeros_like(acc)
+
+    @pl.when(step < shared_steps)
+    def _():
+        for item in range(items):
+            rows = pl.ds(item * PATCHES, PATCHES)
+            inner = (dot_nt(gs[rows, :], dn_ref[...]) * dg_ref[0, rows, :].astype(f32)).astype(bf16)
+            din[rows, :] = inner
+            acc[rows, :] += dot_nn(inner, up_ref[...])
+        dup_ref[...] = dot_nn(n2t[...], din[...]).astype(bf16).T
+        ddn_ref[...] = dot_nn(gst[...], act_ref[0]).astype(bf16).T
+
+    @pl.when(step >= shared_steps)
+    def _():
+        expert, half = (step - shared_steps) // halves, (step - shared_steps) % halves
+
+        @pl.when(half == 0)
+        def _():
+            for item in range(items):
+                rows = pl.ds(item * PATCHES, PATCHES)
+                grad = (gate_column(g4_ref, rows, expert) * gmix[rows, :]).astype(bf16)
+                gs[rows, :] = grad
+                gst[:, rows] = grad.T
+
+        for item in range(items):
+            rows = pl.ds(item * PATCHES, PATCHES)
+            inner = (dot_nn(gs[rows, :], ex_ref[0, 1]) * dg_ref[0, rows, :].astype(f32)).astype(bf16)
+            din[rows, :] = inner
+            part = dot_nt(inner, ex_ref[0, 0])
+
+            @pl.when(half == 0)
+            def _():
+                racc[rows, :] = part
+
+            @pl.when(half > 0)
+            def _():
+                acc[rows, :] += (racc[rows, :] + part).astype(bf16).astype(f32)
+
+        dex_ref[0, 0] = dot_nn(n2t[...], din[...]).astype(bf16)
+        dex_ref[0, 1] = dot_nn(gst[...], act_ref[0]).astype(bf16)
+
+    @pl.when(step == pl.num_programs(0) - 1)
+    def _():
+        gn2_ref[...] = acc[...]
+
+
+def final_kernel(x_ref, mods_ref, fo_ref, tgt_ref, gx_ref, gfm_ref, dfo_ref, loss_ref):
+    item = pl.program_id(0)
+
+    @pl.when(item == 0)
+    def _():
+        gfm_ref[...] = jnp.zeros_like(gfm_ref)
+        dfo_ref[...] = jnp.zeros_like(dfo_ref)
+        loss_ref[...] = jnp.zeros_like(loss_ref)
+
+    tokens = x_ref[...]
+    unit, _ = norm_parts(tokens)
+    scale = mod_row(mods_ref, item, 1)
+    normed = (unit * (1.0 + scale) + mod_row(mods_ref, item, 0)).astype(bf16)
+    err = dot_nt(fo_ref[...], normed) - tgt_ref[...]
+    loss_ref[...] += jnp.sum(err * err, axis=1, keepdims=True)
+    grad_pred = (2.0 * err).astype(bf16)
+    dfo_ref[...] += dot_nn(grad_pred, normed)
+    grad_in, dshift, dscale = norm_back(tokens, scale, dot_tn(grad_pred, fo_ref[...]))
+    gx_ref[...] = grad_in
+    gfm_ref[pl.ds(item, 1), 0:D] = dshift
+    gfm_ref[pl.ds(item, 1), D : 2 * D] = dscale
+
+
+def params(limit):
+    return pltpu.CompilerParams(vmem_limit_bytes=limit * MIB)
+
+
+def whole(shape):
+    return pl.BlockSpec(shape, lambda step: (0,) * len(shape))
+
+
+def rows_of(width):
+    return pl.BlockSpec((PATCHES, width), lambda step: (step, 0))
+
+
+def shape_of(shape, kind):
+    return jax.ShapeDtypeStruct(shape, kind)
+
+
+def cond_forward(feat, hot, stem_t, lin_a, lin_b):
+    ada = pl.BlockSpec((6 * D, D), lambda: (0, 0))
+    shapes = [(8, D)] * 4 + [(LAYERS, 8, 6 * D), (8, 2 * D)]
+    ada_at = [lax.slice_in_dim(lin, 4 * D, 10 * D, axis=0) for lin in (lin_a, lin_b)]
+    del ada
+    return pl.pallas_call(
+        cond_kernel,
+        out_shape=[shape_of(shape, f32) for shape in shapes],
+        compiler_params=params(40),
+        name="cond_forward",
+    )(feat, hot, stem_t, *ada_at), ada_at
+
+
+def cond_backward(gm_a, gm_b, gfm, pre_one, pre_two, stem_t, ada_at):
+    return pl.pallas_call(
+        cond_back_kernel,
+        out_shape=[shape_of((8, D), f32)] * 2,
+        compiler_params=params(40),
+        name="cond_backward",
+    )(gm_a, gm_b, gfm, pre_one, pre_two, stem_t, *ada_at)
+
+
+def attn_forward(tokens, mods, lin):
+    count = tokens.shape[0]
+    return pl.pallas_call(
+        attn_fwd_kernel,
+        grid=(count // PATCHES,),
+        in_specs=[rows_of(D), whole(mods.shape), whole((4 * D, D))],
+        out_specs=[rows_of(D), rows_of(3 * D), rows_of(D), rows_of(D), rows_of(D), rows_of(D)],
+        out_shape=[
+            shape_of((count, D), bf16),
+            shape_of((count, 3 * D), bf16),
+            shape_of((count, D), bf16),
+            shape_of((count, D), f32),
+            shape_of((count, D), f32),
+            shape_of((count, D), bf16),
+        ],
+        compiler_params=params(40),
+        name="attention_forward",
+    )(tokens, mods, lin)
+
+
+def attn_backward(gn2, grad, middle, tokens, normed, qkv, attended, branch, mods, grad_gate, lin):
+    count = tokens.shape[0]
+    return pl.pallas_call(
+        attn_bwd_kernel,
+        grid=(count // PATCHES,),
+        in_specs=[rows_of(D)] * 5
+        + [rows_of(3 * D), rows_of(D), rows_of(D), whole(mods.shape), whole(grad_gate.shape), whole((4 * D, D))],
+        out_specs=[rows_of(D), whole((8, 6 * D)), whole((4 * D, D))],
+        out_shape=[shape_of((count, D), f32), shape_of((8, 6 * D), f32), shape_of((4 * D, D), bf16)],
+        scratch_shapes=[pltpu.VMEM((PATCHES, 3 * D), bf16), pltpu.VMEM((4 * D, D), f32)],
+        compiler_params=params(50),
+        name="attention_backward",
+    )(gn2, grad, middle, tokens, normed, qkv, attended, branch, mods, grad_gate, lin)
+
+
+def weight_specs(shared_steps, lin_rows):
+    up_at = lin_rows // CHUNK - shared_steps
+    return [
+        pl.BlockSpec((CHUNK, D), lambda step: (up_at + jnp.minimum(step, shared_steps - 1), 0)),
+        pl.BlockSpec((CHUNK, D), lambda step: (jnp.minimum(step, shared_steps - 1), 0)),
+        pl.BlockSpec((1, 2, D, CHUNK), lambda step: (jnp.maximum(step - shared_steps, 0), 0, 0, 0)),
+    ]
+
+
+def ffn_forward(n2, middle, mods, g4, lin, lout, experts_w, halves):
+    count = n2.shape[0]
+    shared_steps = lout.shape[0] // CHUNK
+    steps = shared_steps + experts_w.shape[0]
+    wide = pl.BlockSpec((1, count, CHUNK), lambda step: (step, 0, 0))
+    return pl.pallas_call(
+        functools.partial(ffn_fwd_kernel, shared_steps, halves),
+        grid=(steps,),
+        in_specs=[whole(n2.shape), whole(middle.shape), whole(mods.shape), whole(g4.shape)]
+        + weight_specs(shared_steps, lin.shape[0]),
+        out_specs=[wide, wide, whole((count, D)), whole((count, D))],
+        out_shape=[
+            shape_of((steps, count, CHUNK), bf16),
+            shape_of((steps, count, CHUNK), bf16),
+            shape_of((count, D), f32),
+            shape_of((count, D), f32),
+        ],
+        scratch_shapes=[pltpu.VMEM((count, D), f32)] * 2,
+        compiler_params=params(56),
+        name="ffn_forward",
+    )(n2, middle, mods, g4, lin, lout, experts_w)
+
+
+def ffn_backward(grad, n2, mods, g4, mixed, active, slope, lin, lout, experts_w, halves):
+    count = n2.shape[0]
+    shared_steps = lout.shape[0] // CHUNK
+    steps = shared_steps + experts_w.shape[0]
+    wide = pl.BlockSpec((1, count, CHUNK), lambda step: (step, 0, 0))
+    specs = weight_specs(shared_steps, lin.shape[0])
+    return pl.pallas_call(
+        functools.partial(ffn_bwd_kernel, shared_steps, halves),
+        grid=(steps,),
+        in_specs=[whole(grad.shape), whole(n2.shape), whole(mods.shape), whole(g4.shape), whole(mixed.shape), wide, wide]
+        + specs,
+        out_specs=[specs[1], specs[1], specs[2], whole((count, D)), whole((8, D))],
+        out_shape=[
+            shape_of(lout.shape, bf16),
+            shape_of(lout.shape, bf16),
+            shape_of(experts_w.shape, bf16),
+            shape_of((count, D), f32),
+            shape_of((8, D), f32),
+        ],
+        scratch_shapes=[
+            pltpu.VMEM((count, D), f32),
+            pltpu.VMEM((count, D), bf16),
+            pltpu.VMEM((D, count), bf16),
+            pltpu.VMEM((D, count), bf16),
+            pltpu.VMEM((count, CHUNK), bf16),
+            pltpu.VMEM((count, D), f32),
+            pltpu.VMEM((count, D), f32),
+        ],
+        compiler_params=params(60),
+        name="ffn_backward",
+    )(grad, n2, mods, g4, mixed, active, slope, lin, lout, experts_w)
+
+
+def final_step(tokens, mods, fo_rows, target_t):
+    count = tokens.shape[0]
+    return pl.pallas_call(
+        final_kernel,
+        grid=(count // PATCHES,),
+        in_specs=[
+            rows_of(D),
+            whole(mods.shape),
+            whole(fo_rows.shape),
+            pl.BlockSpec((PATCH_DIM, PATCHES), lambda step: (0, step)),
+        ],
+        out_specs=[rows_of(D), whole((8, 2 * D)), whole((PATCH_DIM, D)), whole((PATCH_DIM, 1))],
+        out_shape=[
+            shape_of((count, D), f32),
+            shape_of((8, 2 * D), f32),
+            shape_of((PATCH_DIM, D), f32),
+            shape_of((PATCH_DIM, 1), f32),
+        ],
+        compiler_params=params(40),
+        name="final_step",
+    )(tokens, mods, fo_rows, target_t)
+
+
+def pad_rows(values):
+    return jnp.pad(values, ((0, 8 - values.shape[0]), (0, 0)))
+
+
+def stem_lanes(stem_t):
+    pieces, at = [], 0
+    for size, padded in zip(STEM_SIZES, STEM_PADDED):
+        pieces.append(jnp.pad(stem_t[:, at : at + size], ((0, 0), (0, padded - size))))
+        at = at + size
+    return jnp.concatenate(pieces, axis=1)
+
+
+SHARD = ("expert", "dp")
+
+
+def few_experts(
+    patches,
+    target_noise,
+    timesteps,
+    labels,
+    routes,
+    route_gates,
+    stem_weights,
+    layer_in,
+    layer_out,
+    experts,
+    stem_first,
+    layer_in_first,
+    layer_out_first,
+    experts_first,
+    stem_second,
+    layer_in_second,
+    layer_out_second,
+    experts_second,
+    stem_moment,
+    layer_in_moment,
+    layer_out_moment,
+    experts_moment,
+):
+    count = patches.shape[0]
+    items = timesteps.shape[0]
+    halves = lax.axis_size("dp")
+    sharers = lax.axis_size("expert") * halves
+    expert_count = lax.axis_size("expert") * experts.shape[1]
+    place = lax.axis_index("expert") * halves + lax.axis_index("dp")
+
+    stem_t = stem_weights.T
+    lin_t = jnp.swapaxes(layer_in, 1, 2)
+    stem_all = lax.all_gather(stem_lanes(to_half(stem_t)), SHARD, axis=0, tiled=True)
+    lin_all, lout_all, expert_all = [], [], []
+    for layer in range(LAYERS):
+        lin_all.append(lax.all_gather(to_half(lin_t[layer]), SHARD, axis=0, tiled=True))
+        lout_all.append(lax.all_gather(to_half(layer_out[layer]), SHARD, axis=0, tiled=True))
+        expert_all.append(lax.all_gather(to_half(experts[layer]), SHARD, axis=0, tiled=True))
+
+    feat = time_features(timesteps)
+    hot = label_table(labels)
+    hot_pad = jnp.pad(hot, ((0, 32 - items), (0, STEM_PADDED[3] - hot.shape[1]))).astype(bf16)
+    (cond, hidden, pre_one, pre_two, mods, fin_mods), ada_at = cond_forward(
+        pad_rows(feat), hot_pad, stem_all, lin_all[0], lin_all[1]
+    )
+    tokens = product_nt(patches, stem_all[:, :PATCH_DIM])
+    tokens = (tokens.reshape(items, -1, D) + positions_table()[None]).reshape(-1, D)
+    expert_ids = jnp.arange(expert_count, dtype=jnp.int32)
+    saved = []
+    for layer in range(LAYERS):
+        g4 = jnp.sum(
+            jnp.where(routes[layer][:, :, None] == expert_ids, route_gates[layer][:, :, None], 0.0), axis=1
+        )
+        normed, qkv, attended, branch, middle, n2 = attn_forward(tokens, mods[layer], lin_all[layer])
+        active, slope, mixed, result = ffn_forward(
+            n2, middle, mods[layer], g4, lin_all[layer], lout_all[layer], expert_all[layer], halves
+        )
+        saved.append((tokens, g4, normed, qkv, attended, branch, middle, n2, active, slope, mixed))
+        tokens = result
+    fo_rows = stem_all[:, STEM_AT[5] : STEM_AT[5] + PATCH_DIM].T
+    grad, grad_fin, grad_out_w, loss_rows = final_step(tokens, fin_mods, fo_rows, target_noise.T)
+    loss_total = lax.psum(jnp.sum(loss_rows), ("group", "expert", "dp"))
+
+    grad_mods = [None] * LAYERS
+    lin_sum, lout_sum, expert_sum = [None] * LAYERS, [None] * LAYERS, [None] * LAYERS
+    for layer in reversed(range(LAYERS)):
+        tokens, g4, normed, qkv, attended, branch, middle, n2, active, slope, mixed = saved[layer]
+        dup, ddn, dex, gn2, grad_gate = ffn_backward(
+            grad, n2, mods[layer], g4, mixed, active, slope, lin_all[layer], lout_all[layer], expert_all[layer], halves
+        )
+        grad, grad_mods[layer], dqkvo = attn_backward(
+            gn2, grad, middle, tokens, normed, qkv, attended, branch, mods[layer], grad_gate, lin_all[layer]
+        )
+        expert_sum[layer] = lax.psum_scatter(dex, SHARD, scatter_dimension=0, tiled=True)
+        lout_sum[layer] = lax.psum_scatter(ddn, SHARD, scatter_dimension=0, tiled=True)
+        dlin = jnp.concatenate([dqkvo, jnp.zeros((6 * D, D), bf16), dup], axis=0)
+        lin_sum[layer] = lax.psum_scatter(dlin, SHARD, scatter_dimension=0, tiled=True)
+    grad_patch = product_tn(patches, to_half(grad))
+    dpre_one, dpre_two = cond_backward(grad_mods[0], grad_mods[1], grad_fin, pre_one, pre_two, stem_all, ada_at)
+
+    factors = jnp.concatenate(
+        [cond[:items], hidden[:items], dpre_one[:items], dpre_two[:items], grad_fin[:items], grad_mods[0][:items], grad_mods[1][:items], feat],
+        axis=1,
+    )
+    width = factors.shape[1]
+    packed = jnp.concatenate([factors.reshape(-1), grad_patch.reshape(-1), grad_out_w.reshape(-1)])
+    gathered = lax.all_gather(packed, SHARD, axis=0, tiled=False)
+    ends = gathered[:, items * width :].reshape(sharers, 2, PATCH_DIM, D).sum(axis=0)
+    factors = gathered[:, : items * width].reshape(sharers * items, width)
+    hot_all = label_table(lax.all_gather(labels, SHARD, axis=0, tiled=True))
+    cond_f, hidden_f, done_f, dtwo_f, fin_f, gm_a, gm_b, feat_f = jnp.split(
+        factors, [D, 2 * D, 3 * D, 4 * D, 6 * D, 12 * D, 18 * D], axis=1
+    )
+    stem_cols = stem_weights.shape[1]
+    lin_cols = layer_in.shape[2]
+
+    def own(values):
+        return lax.dynamic_slice_in_dim(values, place * stem_cols, stem_cols, axis=1)
+
+    def outer(left_in, right_in):
+        return lax.dot_general(left_in, right_in, (((0,), (0,)), ((), ())), precision=highest)
+
+    stem_grad = jnp.concatenate(
+        [
+            own(ends[0]).T,
+            outer(own(done_f), feat_f),
+            outer(own(dtwo_f), hidden_f),
+            outer(own(dtwo_f), hot_all),
+            outer(own(cond_f), fin_f),
+            own(ends[1]).T,
+        ],
+        axis=1,
+    )
+    lin_grads = []
+    for layer, gm in ((0, gm_a), (1, gm_b)):
+        spread = jnp.pad(gm, ((0, 0), (4 * D, lin_cols * sharers - 10 * D)))
+        window = lax.dynamic_slice_in_dim(spread, place * lin_cols, lin_cols, axis=1)
+        lin_grads.append(lin_sum[layer].astype(f32) + outer(window, cond_f))
+    lin_grad = jnp.stack(lin_grads)
+    lout_grad = jnp.stack(lout_sum).astype(f32)
+    expert_grad = jnp.stack(expert_sum).astype(f32)
+
+    weights_all = (stem_t, lin_t, layer_out, experts)
+    gradients = (stem_grad, lin_grad, lout_grad, expert_grad)
+    firsts = (stem_first[0].T, jnp.swapaxes(layer_in_first[0], 1, 2), layer_out_first[0], experts_first[0])
+    seconds = (stem_second[0].T, jnp.swapaxes(layer_in_second[0], 1, 2), layer_out_second[0], experts_second[0])
+    moments = (stem_moment.T, jnp.swapaxes(layer_in_moment, 1, 2), layer_out_moment, experts_moment)
+    group_count = lax.axis_size("group")
+    new_weights, halves_out, first_out, second_out, new_moments = [], [], [], [], []
+    for at in range(4):
+        delta, first_new, second_new = adam_step(weights_all[at], gradients[at], firsts[at], seconds[at])
+        mean_delta = lax.psum(to_half(delta), "group").astype(f32) / group_count
+        moment_new = outer_mom * moments[at] + mean_delta
+        new_weight = weights_all[at] - outer_rate * (mean_delta + outer_mom * moment_new)
+        results = [new_weight, to_half(new_weight), first_new, second_new, moment_new]
+        if at == 0:
+            results = [value.T for value in results]
+        if at == 1:
+            results = [jnp.swapaxes(value, 1, 2) for value in results]
+        new_weights.append(results[0])
+        halves_out.append(results[1])
+        first_out.append(results[2][None])
+        second_out.append(results[3][None])
+        new_moments.append(results[4])
+    return (loss_total, *new_weights, *halves_out, *first_out, *second_out, *new_moments)
+
+
 def solution(mesh):
     placed = (
         P(("group", "expert", "dp"), None),
@@ -579,8 +1251,9 @@
         P(None, ("expert", "dp"), None),
         P(None, "expert", None, None, "dp"),
     )
+    step = few_experts if mesh.shape["expert"] <= 4 else per_device
     return jax.shard_map(
-        per_device,
+        step,
         mesh=mesh,
         in_specs=placed,
         out_specs=(

time: 2040 us -> 1210 us (0.59)
  matrix products: 343 us -> 10.6 us
  Pallas kernels: 0 us -> 291 us
  local copies, waits for them, and re-layouts: 324 us -> 45.7 us
  waiting for transfers between devices: 954 us -> 726 us
  blocking collectives: 188 us -> 44.9 us
  other arithmetic: 178 us -> 70.4 us
  starting transfers between devices: 27 us -> 0.59 us
    unnamed x11 -> x15, waiting for transfers between devices: 413 us -> 4.93 us
    reduce_scatter x2 -> x6, waiting for transfers between devices: 32.6 us -> 376 us  [the longest x2 192 us: few_experts(): lax.psum_scatter(dex, SHARD, scatter_dimension=0, tiled=True)]
    all_to_all x6 -> x0, waiting for transfers between devices: 323 us -> none  [the longest x1 102 us: layer_forward(): lax.all_to_all(send_rows.reshape(expert_count, capacity, model_width), 'e...]
    pallas_call x0 -> x11, Pallas kernels: none -> 291 us  [the longest x2 113 us: ffn_backward(): pl.pallas_call(functools.partial(ffn_bwd_kernel, shared_steps, halves), g...]
    dot_general x50 -> x6, matrix products: 261 us -> 7.65 us  [outer(): lax.dot_general(left_in, right_in, (((0,), (0,)), ((), ())), precision=hi...]
    all_gather x4 -> x8, waiting for transfers between devices: 116 us -> 287 us  [the longest x2 146 us: few_experts(): lax.all_gather(to_half(experts[layer]), SHARD, axis=0, tiled=True)]
    all_to_all x2 -> x0, blocking collectives: 147 us -> none  [the longest x1 74.4 us: layer_backward(): lax.all_to_all(send_grad.reshape(expert_count, capacity, model_width), 'e...]
    unnamed x388 -> x152, local copies, waits for them, and re-layouts: 109 us -> 30.9 us
  transfers between devices with their start and end apart: 15 -> 15, of which waited for: 11 -> 14; matrix products, arithmetic and copies ran while one was open for 25% -> 5% of each run, Pallas kernels for 0% -> 6%
where the time goes in v1:
time: 1210 us
  waiting for transfers between devices  726 us (60%)
  Pallas kernels  291 us (24%)
  other arithmetic  70.4 us (6%)
  local copies, waits for them, and re-layouts  45.7 us (4%)
  blocking collectives  44.9 us (4%)
  between operations  15.9 us (1%)
    reduce_scatter x2, waiting for transfers between devices, few_experts(): lax.psum_scatter(dex, SHARD, scatter_dimension=0, tiled=True)  192 us
    all_gather x2, waiting for transfers between devices, few_experts(): lax.all_gather(to_half(experts[layer]), SHARD, axis=0, tiled=True)  146 us
    reduce_scatter x2, waiting for transfers between devices, few_experts(): lax.psum_scatter(dlin, SHARD, scatter_dimension=0, tiled=True)  117 us
    pallas_call x2, Pallas kernels, ffn_backward(): pl.pallas_call(functools.partial(ffn_bwd_kernel, shared_steps, halves), g...  113 us
    all_gather x2, waiting for transfers between devices, few_experts(): lax.all_gather(to_half(lin_t[layer]), SHARD, axis=0, tiled=True)  112 us
    pallas_call x2, Pallas kernels, ffn_forward(): pl.pallas_call(functools.partial(ffn_fwd_kernel, shared_steps, halves), g...  107 us
    reduce_scatter x2, waiting for transfers between devices, few_experts(): lax.psum_scatter(ddn, SHARD, scatter_dimension=0, tiled=True)  67.9 us
    psum x1, waiting for transfers between devices, few_experts(): mean_delta = lax.psum(to_half(delta), 'group').astype(f32) / group_count  58.4 us
  transfers between devices with their start and end apart: 15, of which 14 were waited for; matrix products, arithmetic and copies ran while one was open for 5% of the time, Pallas kernels for 6%

profile of v1, /device:TPU:0, one launch (start us, length us, event | category | flops | bytes accessed | tf_op | source)
XLA Modules:
  0.0 1205.3 jit_solution(16530113328308452269)
XLA Ops:
  10.2 1.9 bitcast_convert_fusion
  15.1 2.6 convert.16
  17.7 1.6 fusion.76
  24.3 17.5 %all-gather.16.cloned.1.call-done.stem_ref = bf16[384,2688]{1,0:T(8,128)(2,1)} async-done(((bf16[48,2688]{1,0:T(8,128)(2,1)}), bf16[384,2688]{1,0:T(8,128)(2,1)}) %all-gather.16.cloned.1.call-update) | async-done | bytes 2064400 | tf_op jit(solution)/shard_map/all_gather | solution.py:1114
  44.1 56.0 %all-gather.18.cloned.1.call-done = bf16[1,6912,384]{2,1,0:T(8,128)(2,1)} async-done(((bf16[1,864,384]{2,1,0:T(8,128)(2,1)}), bf16[1,6912,384]{2,1,0:T(8,128)(2,1)}) %all-gather.18.cloned.1.call-update) | async-done | bytes 5308432 | tf_op jit(solution)/shard_map/all_gather | solution.py:1117
  100.2 1.7 slice_bitcast_fusion.1.ada_a
  101.8 55.9 %all-gather.20.cloned.1.call-done = bf16[1,6912,384]{2,1,0:T(8,128)(2,1)} async-done(((bf16[1,864,384]{2,1,0:T(8,128)(2,1)}), bf16[1,6912,384]{2,1,0:T(8,128)(2,1)}) %all-gather.20.cloned.1.call-update) | async-done | bytes 5308432 | tf_op jit(solution)/shard_map/all_gather | solution.py:1117
  157.8 1.8 slice_bitcast_fusion.ada_b
  159.9 2.0 cond_forward.1
  163.2 9.6 attention_forward.2
  179.2 11.0 all-gather.22.cloned.1.call-done
  190.2 92.0 %all-gather.24.cloned.1.call-done = bf16[8,1,2,384,768]{4,3,2,1,0:T(8,128)(2,1)} async-done(((bf16[1,1,2,384,768]{4,3,2,1,0:T(8,128)(2,1)}), bf16[8,1,2,384,768]{4,3,2,1,0:T(8,128)(2,1)}) %all-gather.24.cloned.1.call-update) | async-done | bytes 9437200 | tf_op jit(solution)/shard_map/all_gather | solution.py:1119
  282.2 53.2 %ffn_forward.2 = (bf16[12,1024,768]{2,1,0:T(8,128)(2,1)}, bf16[12,1024,768]{2,1,0:T(8,128)(2,1)}, f32[1024,384]{1,0:T(8,128)}, f32[1024,384]{1,0:T(8,128)}) custom-call(bf16[1024,384]{1,0:T(8,128)(2,1)} %copy-done.11, f32[1024,384]{1,0:T(8,128)} %copy-done.7, f32[8,2304]{1,0:T(8,128)} %copy-done.15, f32[1024,4]{1,0:T(8,128)} %copy.101.g4_ref, ...), custom_call_target="tpu_custom_call" | custom-call | tf_op jit(solution)/shard_map/ffn_forward/pallas_call | solution.py:992
  336.9 9.4 attention_forward.3
  352.6 53.8 %all-gather.28.cloned.1.call-done = bf16[8,1,2,384,768]{4,3,2,1,0:T(8,128)(2,1)} async-done(((bf16[1,1,2,384,768]{4,3,2,1,0:T(8,128)(2,1)}), bf16[8,1,2,384,768]{4,3,2,1,0:T(8,128)(2,1)}) %all-gather.28.cloned.1.call-update) | async-done | bytes 9437200 | tf_op jit(solution)/shard_map/all_gather | solution.py:1119
  406.5 53.5 %ffn_forward.3 = (bf16[12,1024,768]{2,1,0:T(8,128)(2,1)}, bf16[12,1024,768]{2,1,0:T(8,128)(2,1)}, f32[1024,384]{1,0:T(8,128)}, f32[1024,384]{1,0:T(8,128)}) custom-call(bf16[1024,384]{1,0:T(8,128)(2,1)} %copy-done.12, f32[1024,384]{1,0:T(8,128)} %copy-done.8, f32[8,2304]{1,0:T(8,128)} %copy-done.17, f32[1024,4]{1,0:T(8,128)} %copy.102.g4_ref, ...), custom_call_target="tpu_custom_call" | custom-call | tf_op jit(solution)/shard_map/ffn_forward/pallas_call | solution.py:992
  461.4 3.2 final_step.1
  465.8 56.8 %ffn_backward.2 = (bf16[3072,384]{1,0:T(8,128)(2,1)}, bf16[3072,384]{1,0:T(8,128)(2,1)}, bf16[8,2,384,768]{3,2,1,0:T(8,128)(2,1)}, f32[1024,384]{1,0:T(8,128)}, f32[8,384]{1,0:T(8,128)}) custom-call(f32[1024,384]{1,0:T(8,128)} %copy-done.10, bf16[1024,384]{1,0:T(8,128)(2,1)} %copy-done.12, f32[8,2304]{1,0:T(8,128)} %copy-done.17, f32[1024,4]{1,0:T(8,128)} %copy.102.g4_ref, ...), custom_call_target="tpu_custom_call" | custom-call | tf_op jit(solution)/shard_map/ffn_backward/pallas_call | solution.py:1016
  525.6 22.9 %attention_backward.2 = (f32[1024,384]{1,0:T(8,128)}, f32[8,2304]{1,0:T(8,128)S(1)}, bf16[1536,384]{1,0:T(8,128)(2,1)S(1)}) custom-call(f32[1024,384]{1,0:T(8,128)} %get-tuple-element.84.gn2_ref, f32[1024,384]{1,0:T(8,128)} %copy-done.10, f32[1024,384]{1,0:T(8,128)} %copy-done.8, f32[1024,384]{1,0:T(8,128)} %get-tuple-element.72.x_ref, ...), custom_call_target="tpu_custom_call" | custom-call | tf_op jit(solution)/shard_map/attention_backward/pallas_call | solution.py:965
  548.5 56.4 %ffn_backward.3 = (bf16[3072,384]{1,0:T(8,128)(2,1)}, bf16[3072,384]{1,0:T(8,128)(2,1)}, bf16[8,2,384,768]{3,2,1,0:T(8,128)(2,1)}, f32[1024,384]{1,0:T(8,128)}, f32[8,384]{1,0:T(8,128)}) custom-call(f32[1024,384]{1,0:T(8,128)} %get-tuple-element.90.g_ref, bf16[1024,384]{1,0:T(8,128)(2,1)} %copy-done.11, f32[8,2304]{1,0:T(8,128)} %copy-done.15, ...), custom_call_target="tpu_custom_call" | custom-call | tf_op jit(solution)/shard_map/ffn_backward/pallas_call | solution.py:1016
  607.9 23.1 %attention_backward.3 = (f32[1024,384]{1,0:T(8,128)}, f32[8,2304]{1,0:T(8,128)S(1)}, bf16[1536,384]{1,0:T(8,128)(2,1)S(1)}) custom-call(f32[1024,384]{1,0:T(8,128)} %get-tuple-element.94.gn2_ref, f32[1024,384]{1,0:T(8,128)} %get-tuple-element.90.g_ref, f32[1024,384]{1,0:T(8,128)} %copy-done.7, f32[1024,384]{1,0:T(8,128)} %copy-done.4, ...), custom_call_target="tpu_custom_call" | custom-call | tf_op jit(solution)/shard_map/attention_backward/pallas_call | solution.py:965
  632.0 1.6 convolution_bitcast_fusion
  633.7 1.5 copy-done.3
  635.1 1.6 copy-done.6
  640.2 10.0 pad_maximum_fusion
  653.8 6.6 all-reduce.6
  660.9 1.6 reshape.386
  667.0 2.7 fusion.45
  669.7 29.8 %reduce-scatter.13.cloned.1.call-done = bf16[384,384]{1,0:T(8,128)(2,1)} async-done(((bf16[3072,384]{1,0:T(8,128)(2,1)}), bf16[384,384]{1,0:T(8,128)(2,1)}) %reduce-scatter.13.cloned.1.call-update) | async-done | bytes 294928 | tf_op jit(solution)/shard_map/reduce_scatter | solution.py:1156
  699.5 38.1 %reduce-scatter.11.cloned.1.call-done = bf16[384,384]{1,0:T(8,128)(2,1)} async-done(((bf16[3072,384]{1,0:T(8,128)(2,1)}), bf16[384,384]{1,0:T(8,128)(2,1)}) %reduce-scatter.11.cloned.1.call-update) | async-done | bytes 294928 | tf_op jit(solution)/shard_map/reduce_scatter | solution.py:1156
  737.6 3.3 fusion.34
  740.9 59.0 %reduce-scatter.9.cloned.1.call-done = bf16[864,384]{1,0:T(8,128)(2,1)} async-done(((bf16[6912,384]{1,0:T(8,128)(2,1)}), bf16[864,384]{1,0:T(8,128)(2,1)}) %reduce-scatter.9.cloned.1.call-update) | async-done | bytes 663568 | tf_op jit(solution)/shard_map/reduce_scatter | solution.py:1158
  799.9 3.6 fusion.21
  803.5 57.5 %reduce-scatter.7.cloned.1.call-done = bf16[864,384]{1,0:T(8,128)(2,1)} async-done(((bf16[6912,384]{1,0:T(8,128)(2,1)}), bf16[864,384]{1,0:T(8,128)(2,1)}) %reduce-scatter.7.cloned.1.call-update) | async-done | bytes 663568 | tf_op jit(solution)/shard_map/reduce_scatter | solution.py:1158
  861.0 2.6 fusion.22
  863.7 6.1 fusion.42
  869.8 91.5 %reduce-scatter.17.cloned.1.call-done = bf16[1,2,384,768]{3,2,1,0:T(8,128)(2,1)} async-done(((bf16[8,2,384,768]{3,2,1,0:T(8,128)(2,1)}), bf16[1,2,384,768]{3,2,1,0:T(8,128)(2,1)}) %reduce-scatter.17.cloned.1.call-update) | async-done | bytes 1179664 | tf_op jit(solution)/shard_map/reduce_scatter | solution.py:1155
  961.2 100.1 %reduce-scatter.15.cloned.1.call-done = bf16[1,2,384,768]{3,2,1,0:T(8,128)(2,1)} async-done(((bf16[8,2,384,768]{3,2,1,0:T(8,128)(2,1)}), bf16[1,2,384,768]{3,2,1,0:T(8,128)(2,1)}) %reduce-scatter.15.cloned.1.call-update) | async-done | bytes 1179664 | tf_op jit(solution)/shard_map/reduce_scatter | solution.py:1155
  1061.3 9.0 fusion.14
  1070.9 38.3 %psum.35 = f32[]{:T(128)} all-reduce(f32[]{:T(128)} %reduce_sum.38), channel_id=1, replica_groups=mesh['group'=4,'expert'=4,'dp'=2] {'group','expert','dp'}, use_global_device_ids=true, to_apply=%region_3.4 | all-reduce | flops 1 | bytes 8 | tf_op jit(solution)/shard_map/psum | solution.py:1143
  1109.2 3.5 fusion.33
  1112.7 5.4 fusion.7
  1118.2 2.9 fusion.12
  1121.1 58.4 %all-reduce.10.cloned.1.call-done = (bf16[48,2441]{1,0:T(8,128)(2,1)}, bf16[2,864,384]{2,1,0:T(8,128)(2,1)}, bf16[2,384,384]{2,1,0:T(8,128)(2,1)}, bf16[2,1,2,384,768]{4,3,2,0,1:T(8,128)(2,1)}) async-done(((bf16[48,2441]{1,0:T(8,128)(2,1)}, bf16[2,864,384]{2,1,0:T(8,128)(2,1)}, bf16[2,384,384]{2,1,0:T(8,128)(2,1)}, bf16[2,1,2,384,768]{4,3,2,0,1:T(8,128)(2,1)}), (bf16[48,2441]{1,0:T(8,128)(2,1)}, ...) | async-done | bytes 4510576 | tf_op jit(solution)/shard_map/psum | solution.py:1213
  1179.6 2.6 convert_bitcast_fusion.3
  1182.2 5.5 convert_bitcast_fusion.2
  1187.7 1.9 fusion.75
  1190.2 8.1 convert_bitcast_fusion.1
  (238 shorter events, 50.7 us)
Async XLA Ops:
  7.2 35.6 %copy-start = (bf16[1024,16]{0,1:T(8,128)(2,1)S(1)}, bf16[1024,16]{0,1:T(8,128)(2,1)}, u32[]{:S(2)}) copy-start(bf16[1024,16]{0,1:T(8,128)(2,1)} %param.22) | copy-start | bytes 98308
  7.2 34.6 %all-gather.16.cloned.1.call-start = ((), (), s32[]{:S(2)}) async-start(), calls=%async_computation.6 | async-start | bytes 2322432 | tf_op jit(solution)/shard_map/all_gather | solution.py:1114
  10.1 90.1 %all-gather.18.cloned.1.call-start = ((), (), s32[]{:S(2)}) async-start(), calls=%async_computation.13 | async-start | bytes 5971968 | tf_op jit(solution)/shard_map/all_gather | solution.py:1117
  13.3 144.5 %all-gather.20.cloned.1.call-start = ((), (), s32[]{:S(2)}) async-start(), calls=%async_computation.14 | async-start | bytes 5971968 | tf_op jit(solution)/shard_map/all_gather | solution.py:1117
  14.0 176.2 %all-gather.22.cloned.1.call-start = ((), (), s32[]{:S(2)}) async-start(), calls=%async_computation.15 | async-start | bytes 2654208 | tf_op jit(solution)/shard_map/all_gather | solution.py:1118
  15.1 267.1 %all-gather.24.cloned.1.call-start = ((), (), s32[]{:S(2)}) async-start(), calls=%async_computation.16 | async-start | bytes 10616832 | tf_op jit(solution)/shard_map/all_gather | solution.py:1119
  19.2 3.7 copy-start.61
  19.3 333.4 %all-gather.26.cloned.1.call-start = ((), (), s32[]{:S(2)}) async-start(), calls=%async_computation.17 | async-start | bytes 2654208 | tf_op jit(solution)/shard_map/all_gather | solution.py:1118
  19.8 386.6 %all-gather.28.cloned.1.call-start = ((), (), s32[]{:S(2)}) async-start(), calls=%async_computation.18 | async-start | bytes 10616832 | tf_op jit(solution)/shard_map/all_gather | solution.py:1119
  20.6 640.3 %all-gather.30.cloned.1.call-start = ((), (), s32[]{:S(2)}) async-start(), calls=%async_computation.19 | async-start | bytes 1474560 | tf_op jit(solution)/shard_map/all_gather | solution.py:1168
  44.1 119.0 %copy-start.4 = (f32[1024,384]{1,0:T(8,128)}, f32[1024,384]{1,0:T(8,128)S(1)}, u32[]{:S(2)}) copy-start(f32[1024,384]{1,0:T(8,128)S(1)} %bitcast_add_fusion.2.x_ref) | copy-start | bytes 4718596
  157.8 2.1 copy-start.5
  163.1 9.6 copy-start.15
  163.1 172.3 %copy-start.17 = (f32[8,2304]{1,0:T(8,128)}, f32[8,2304]{1,0:T(8,128)S(1)}, u32[]{:S(2)}) copy-start(f32[8,2304]{1,0:T(8,128)S(1)} %get-tuple-element.236.mods_ref) | copy-start | bytes 221188
  406.5 53.5 %copy-start.32 = (f32[1024,16]{0,1:T(8,128)S(1)}, f32[1024,16]{0,1:T(8,128)}, u32[]{:S(2)}) copy-start(f32[1024,16]{0,1:T(8,128)} %param.23) | copy-start | bytes 196612
  406.5 53.5 %copy-start.34 = (f32[8,768]{1,0:T(8,128)S(1)}, f32[8,768]{1,0:T(8,128)}, u32[]{:S(2)}) copy-start(f32[8,768]{1,0:T(8,128)} %copy-done.33) | copy-start | bytes 73732
  465.8 56.9 %copy-start.18 = (f32[8,2304]{1,0:T(8,128)S(1)}, f32[8,2304]{1,0:T(8,128)}, u32[]{:S(2)}) copy-start(f32[8,2304]{1,0:T(8,128)} %copy-done.17) | copy-start | bytes 221188
  548.5 56.4 %copy-start.16 = (f32[8,2304]{1,0:T(8,128)S(1)}, f32[8,2304]{1,0:T(8,128)}, u32[]{:S(2)}) copy-start(f32[8,2304]{1,0:T(8,128)} %copy-done.15) | copy-start | bytes 221188
  607.9 25.8 %copy-start.38 = (f32[8,384]{1,0:T(8,128)S(1)}, f32[8,384]{1,0:T(8,128)}, u32[]{:S(2)}) copy-start(f32[8,384]{1,0:T(8,128)} %copy-done.37) | copy-start | bytes 36868
  638.7 60.8 %reduce-scatter.13.cloned.1.call-start = ((), (), s32[]{:S(2)}) async-start(), calls=%async_computation.10 | async-start | bytes 2654208 | tf_op jit(solution)/shard_map/reduce_scatter | solution.py:1156
  639.5 98.1 %reduce-scatter.11.cloned.1.call-start = ((), (), s32[]{:S(2)}) async-start(), calls=%async_computation.9 | async-start | bytes 2654208 | tf_op jit(solution)/shard_map/reduce_scatter | solution.py:1156
  640.1 159.9 %reduce-scatter.9.cloned.1.call-start = ((), (), s32[]{:S(2)}) async-start(), calls=%async_computation.8 | async-start | bytes 5971968 | tf_op jit(solution)/shard_map/reduce_scatter | solution.py:1158
  650.2 210.8 %reduce-scatter.7.cloned.1.call-start = ((), (), s32[]{:S(2)}) async-start(), calls=%async_computation.7 | async-start | bytes 5971968 | tf_op jit(solution)/shard_map/reduce_scatter | solution.py:1158
  650.8 310.4 %reduce-scatter.17.cloned.1.call-start = ((), (), s32[]{:S(2)}) async-start(), calls=%async_computation.12 | async-start | bytes 10616832 | tf_op jit(solution)/shard_map/reduce_scatter | solution.py:1155
  651.6 409.7 %reduce-scatter.15.cloned.1.call-start = ((), (), s32[]{:S(2)}) async-start(), calls=%async_computation.11 | async-start | bytes 10616832 | tf_op jit(solution)/shard_map/reduce_scatter | solution.py:1155
  652.1 527.4 %all-reduce.10.cloned.1.call-start = ((), (), s32[]{:S(2)}) async-start(), calls=%async_computation.20 | async-start | bytes 9043968 | tf_op jit(solution)/shard_map/psum | solution.py:1213
  662.8 4.2 copy-start.50
  665.7 71.9 %copy-start.46 = (f32[2,384,384]{2,1,0:T(8,128)S(1)}, f32[2,384,384]{2,1,0:T(8,128)}, u32[]{:S(2)}) copy-start(f32[2,384,384]{2,1,0:T(8,128)} %param.30) | copy-start | bytes 3538948
  665.7 71.9 %copy-start.49 = (f32[1,2,384,384]{3,2,1,0:T(8,128)S(1)}, f32[1,2,384,384]{3,2,1,0:T(8,128)}, u32[]{:S(2)}) copy-start(f32[1,2,384,384]{3,2,1,0:T(8,128)} %param.38) | copy-start | bytes 3538948
  740.9 122.8 %copy-start.39 = (f32[2,384,864]{1,2,0:T(8,128)S(1)}, f32[2,384,864]{1,2,0:T(8,128)}, u32[]{:S(2)}) copy-start(f32[2,384,864]{1,2,0:T(8,128)} %param.29) | copy-start | bytes 7962628
  861.0 2.7 copy-start.48
  1070.2 38.9 %copy-start.55 = (bf16[384,384]{1,0:T(8,128)(2,1)S(1)}, bf16[384,384]{1,0:T(8,128)(2,1)}, u32[]{:S(2)}) copy-start(bf16[384,384]{1,0:T(8,128)(2,1)} %reduce-scatter.13.cloned.1.call-done) | copy-start | bytes 884740
  1070.3 38.9 %copy-start.56 = (bf16[384,384]{1,0:T(8,128)(2,1)S(1)}, bf16[384,384]{1,0:T(8,128)(2,1)}, u32[]{:S(2)}) copy-start(bf16[384,384]{1,0:T(8,128)(2,1)} %reduce-scatter.11.cloned.1.call-done) | copy-start | bytes 884740
  1070.3 42.4 %copy-start.41 = (bf16[1,2,384,768]{3,2,1,0:T(8,128)(2,1)S(1)}, bf16[1,2,384,768]{3,2,1,0:T(8,128)(2,1)}, u32[]{:S(2)}) copy-start(bf16[1,2,384,768]{3,2,1,0:T(8,128)(2,1)} %reduce-scatter.17.cloned.1.call-done) | copy-start | bytes 3538948
  1070.3 42.4 %copy-start.43 = (bf16[1,2,384,768]{3,2,1,0:T(8,128)(2,1)S(1)}, bf16[1,2,384,768]{3,2,1,0:T(8,128)(2,1)}, u32[]{:S(2)}) copy-start(bf16[1,2,384,768]{3,2,1,0:T(8,128)(2,1)} %reduce-scatter.15.cloned.1.call-done) | copy-start | bytes 3538948
  1109.2 9.0 slice-start.2
  1112.7 5.5 slice-start.3
  1112.7 5.5 copy-start.42
  1112.7 5.4 copy-start.44
  1118.2 64.0 %copy-start.40 = (f32[2,384,864]{1,2,0:T(8,128)S(1)}, f32[2,384,864]{1,2,0:T(8,128)}, u32[]{:S(2)}) copy-start(f32[2,384,864]{1,2,0:T(8,128)} %param.29) | copy-start | bytes 7962628
  1118.2 71.5 %slice-start = ((s8[4718592]{0:T(1024)(128)(4,1)}), s8[524288]{0:T(1024)(128)(4,1)S(1)}, s32[]{:S(2)}) async-start(s8[4718592]{0:T(1024)(128)(4,1)} %bitcast.238), calls=%async_computation.21 | async-start | bytes 1048576
  1179.6 2.6 copy-start.53
  1182.1 5.6 copy-start.47
  1182.1 5.6 copy-start.54
  1182.2 5.6 copy-start.57
  1182.2 7.5 slice-start.1
  1187.7 2.5 copy-start.52
  1190.2 8.1 copy-start.1
  (36 other events, 42.6 us)
Sparse Core Ops, SparseCore 0:
  10.3 31.5 all-gather.15
  44.0 56.0 all-gather.17
  102.4 55.3 all-gather.19
  159.8 30.3 all-gather.21
  192.3 89.8 all-gather.23
  284.3 30.0 all-gather.25
  316.6 89.8 all-gather.27
  638.9 21.9 all-gather.29
  663.8 35.7 reduce-scatter.12
  702.3 35.3 reduce-scatter.10
  739.9 59.9 reduce-scatter.8
  802.1 58.8 reduce-scatter.6
  863.3 97.8 reduce-scatter.16
  963.4 97.8 reduce-scatter.14
  1070.4 109.1 all-reduce.9

commit v2 on v1

--- a/solution.py
+++ b/solution.py
@@ -746,7 +746,8 @@
 
     @pl.when(item == pl.num_programs(0) - 1)
     def _():
-        dw_ref[...] = acc[...].astype(bf16)
+        dw_ref[0 : 4 * D, :] = acc[...].astype(bf16)
+        dw_ref[4 * D :, :] = jnp.zeros_like(dw_ref[4 * D :, :])
 
 
 def gelu_both(values):
@@ -824,6 +825,7 @@
     @pl.when(step == 0)
     def _():
         gg_ref[...] = jnp.zeros_like(gg_ref)
+        dup_ref[0:D, :] = jnp.zeros((D, D), bf16)
         for item in range(items):
             rows = pl.ds(item * PATCHES, PATCHES)
             grad = g_ref[rows, :]
@@ -842,7 +844,8 @@
             inner = (dot_nt(gs[rows, :], dn_ref[...]) * dg_ref[0, rows, :].astype(f32)).astype(bf16)
             din[rows, :] = inner
             acc[rows, :] += dot_nn(inner, up_ref[...])
-        dup_ref[...] = dot_nn(n2t[...], din[...]).astype(bf16).T
+        at = dup_ref.shape[0] - shared_steps * CHUNK + step * CHUNK
+        dup_ref[pl.ds(pl.multiple_of(at, D), CHUNK), :] = dot_nn(n2t[...], din[...]).astype(bf16).T
         ddn_ref[...] = dot_nn(gst[...], act_ref[0]).astype(bf16).T
 
     @pl.when(step >= shared_steps)
@@ -904,6 +907,10 @@
 
 def params(limit):
     return pltpu.CompilerParams(vmem_limit_bytes=limit * MIB)
+
+
+def cost(multiplies, moved):
+    return pl.CostEstimate(flops=2 * multiplies, bytes_accessed=moved, transcendentals=0)
 
 
 def whole(shape):
@@ -956,21 +963,23 @@
             shape_of((count, D), bf16),
         ],
         compiler_params=params(40),
+        cost_estimate=cost(count * D * 4 * D * 9, 16 * count * D),
         name="attention_forward",
     )(tokens, mods, lin)
 
 
-def attn_backward(gn2, grad, middle, tokens, normed, qkv, attended, branch, mods, grad_gate, lin):
+def attn_backward(gn2, grad, middle, tokens, normed, qkv, attended, branch, mods, grad_gate, lin, out_rows):
     count = tokens.shape[0]
     return pl.pallas_call(
         attn_bwd_kernel,
         grid=(count // PATCHES,),
         in_specs=[rows_of(D)] * 5
         + [rows_of(3 * D), rows_of(D), rows_of(D), whole(mods.shape), whole(grad_gate.shape), whole((4 * D, D))],
-        out_specs=[rows_of(D), whole((8, 6 * D)), whole((4 * D, D))],
-        out_shape=[shape_of((count, D), f32), shape_of((8, 6 * D), f32), shape_of((4 * D, D), bf16)],
+        out_specs=[rows_of(D), whole((8, 6 * D)), whole((out_rows, D))],
+        out_shape=[shape_of((count, D), f32), shape_of((8, 6 * D), f32), shape_of((out_rows, D), bf16)],
         scratch_shapes=[pltpu.VMEM((PATCHES, 3 * D), bf16), pltpu.VMEM((4 * D, D), f32)],
         compiler_params=params(50),
+        cost_estimate=cost(count * D * 4 * D * 22, 16 * count * D),
         name="attention_backward",
     )(gn2, grad, middle, tokens, normed, qkv, attended, branch, mods, grad_gate, lin)
 
@@ -1003,6 +1012,7 @@
         ],
         scratch_shapes=[pltpu.VMEM((count, D), f32)] * 2,
         compiler_params=params(56),
+        cost_estimate=cost(4 * steps * count * D * CHUNK * 2, 8 * steps * count * CHUNK),
         name="ffn_forward",
     )(n2, middle, mods, g4, lin, lout, experts_w)
 
@@ -1018,9 +1028,9 @@
         grid=(steps,),
         in_specs=[whole(grad.shape), whole(n2.shape), whole(mods.shape), whole(g4.shape), whole(mixed.shape), wide, wide]
         + specs,
-        out_specs=[specs[1], specs[1], specs[2], whole((count, D)), whole((8, D))],
+        out_specs=[whole((lout.shape[0] + D, D)), specs[1], specs[2], whole((count, D)), whole((8, D))],
         out_shape=[
-            shape_of(lout.shape, bf16),
+            shape_of((lout.shape[0] + D, D), bf16),
             shape_of(lout.shape, bf16),
             shape_of(experts_w.shape, bf16),
             shape_of((count, D), f32),
@@ -1036,6 +1046,7 @@
             pltpu.VMEM((count, D), f32),
         ],
         compiler_params=params(60),
+        cost_estimate=cost(4 * steps * count * D * CHUNK * 4 // 2, 8 * steps * count * CHUNK),
         name="ffn_backward",
     )(grad, n2, mods, g4, mixed, active, slope, lin, lout, experts_w)
 
@@ -1073,6 +1084,316 @@
         pieces.append(jnp.pad(stem_t[:, at : at + size], ((0, 0), (0, padded - size))))
         at = at + size
     return jnp.concatenate(pieces, axis=1)
+
+
+MESH_ID = pl.DeviceIdType.MESH
+TILE = 48
+
+
+def plane_partners():
+    group = lax.axis_index("group")
+    return {"group": group + 1 - 2 * lax.rem(group, 2)}, {"group": lax.rem(group + 2, 4)}
+
+
+def greet(partners, line_at, line_size):
+    barrier = pltpu.get_barrier_semaphore()
+    for partner in partners:
+        pl.semaphore_signal(barrier, inc=1, device_id=partner, device_id_type=MESH_ID)
+
+    @pl.when(line_at > 0)
+    def _():
+        pl.semaphore_signal(barrier, inc=1, device_id={"expert": line_at - 1}, device_id_type=MESH_ID)
+
+    @pl.when(line_at < line_size - 1)
+    def _():
+        pl.semaphore_signal(barrier, inc=1, device_id={"expert": line_at + 1}, device_id_type=MESH_ID)
+
+    ends = jnp.where(line_at == 0, 1, 0) + jnp.where(line_at == line_size - 1, 1, 0)
+    pl.semaphore_wait(barrier, len(partners) + 2 - ends)
+
+
+def row_tiles(rows, body):
+    def step(index, carry):
+        body(pl.ds(pl.multiple_of(index * TILE, TILE), TILE))
+        return carry
+
+    lax.fori_loop(0, rows // TILE, step, 0)
+
+
+def adam_delta(weight, gradient, first, second):
+    return adam_step(weight, gradient, first, second)[0]
+
+
+def reduce_units():
+    units = []
+    for matrix in range(2):
+        for half in range(2):
+            units.append((0, matrix, half * D // 2, D // 2, CHUNK, ()))
+    for half in range(2):
+        units.append((1, 0, half * 432, 432, D, (1,)))
+    units.append((2, 0, 0, D, D, ()))
+    return units
+
+
+def reduce_kernel(
+    layer, dex, dqkvo, dup, ddn, extra, ex_w, ex_f, ex_s, li_w, li_f, li_s, lo_w, lo_f, lo_s,
+    g_ex, g_li, g_lo, m_ex, m_li, m_lo, *scratch,
+):
+    units = reduce_units()
+    number = len(units)
+    banks = [scratch[at * number : (at + 1) * number] for at in range(9)]
+    chip, local, came, delta, swapped, swapped_two, weight, first, second = banks
+    extra_buf = scratch[9 * number]
+    core_send, core_recv, line_send, line_recv, load_sem, plane_send, plane_recv, out_sem = scratch[9 * number + 1 :]
+    at = lax.axis_index("expert")
+    core = lax.axis_index("dp")
+    sibling = {"dp": 1 - core}
+    side_x, side_y = plane_partners()
+    greet([sibling, side_x, side_y], at, 4)
+
+    def pieces(unit, which):
+        kind, matrix, row, rows, _, _ = units[unit]
+        if kind == 0:
+            return [(dex.at[:, which, matrix, pl.ds(row, rows)], slice(0, 4))]
+        if kind == 2:
+            return [(ddn.at[:, which, pl.ds(row, rows)], slice(0, 4))]
+        return [
+            (dqkvo.at[which, pl.ds(row, rows)], 0),
+            (dup.at[0, which, pl.ds(row, rows)], 2),
+            (dup.at[1, which, pl.ds(row, rows)], 3),
+        ]
+
+    def dest(bank, unit, where):
+        return bank[unit].at[pl.ds(0, 4)] if isinstance(where, slice) else bank[unit].at[where]
+
+    given, loads = [], []
+    for unit in range(number):
+        given.append([])
+        for place, (source, where) in enumerate(pieces(unit, 1 - core)):
+            copy = pltpu.make_async_remote_copy(
+                source, dest(chip, unit, where), core_send.at[unit, place], core_recv.at[unit, place],
+                device_id=sibling, device_id_type=MESH_ID,
+            )
+            copy.start()
+            given[unit].append(copy)
+        loads.append([])
+        for place, (source, where) in enumerate(pieces(unit, core)):
+            copy = pltpu.make_async_copy(source, dest(local, unit, where), load_sem.at[unit, place])
+            copy.start()
+            loads[unit].append(copy)
+    state_loads = []
+    for unit, (kind, matrix, row, rows, _, _) in enumerate(units):
+        if kind == 0:
+            sources = [ex_w.at[layer, 0, matrix], ex_f.at[0, layer, 0, matrix], ex_s.at[0, layer, 0, matrix]]
+        elif kind == 1:
+            sources = [li_w.at[layer], li_f.at[layer], li_s.at[layer]]
+        else:
+            sources = [lo_w.at[layer], lo_f.at[0, layer], lo_s.at[0, layer]]
+        state_loads.append([])
+        for place, (source, bank) in enumerate(zip(sources, (weight, first, second))):
+            copy = pltpu.make_async_copy(source.at[pl.ds(row, rows)], bank[unit], load_sem.at[unit, 3 + place])
+            copy.start()
+            state_loads[unit].append(copy)
+    extra_load = pltpu.make_async_copy(extra, extra_buf, load_sem.at[number, 0])
+    extra_load.start()
+
+    def line_copy(unit, owner, step, place):
+        slot = 4 if step == -1 and owner == place - 1 else owner
+        return pltpu.make_async_remote_copy(
+            chip[unit].at[owner], came[unit].at[slot], line_send.at[unit, owner], line_recv.at[unit, slot],
+            device_id={"expert": at + step}, device_id_type=MESH_ID,
+        )
+
+    def arrived(unit, slot):
+        pltpu.make_async_remote_copy(
+            came[unit].at[slot], came[unit].at[slot], line_send.at[unit, 0], line_recv.at[unit, slot],
+            device_id=sibling, device_id_type=MESH_ID,
+        ).wait_recv()
+
+    routes_of = {0: [(3, 1), (2, 1), (1, 1)], 1: [(3, 1), (2, 1), (0, -1)], 2: [(0, -1), (1, -1), (3, 1)], 3: [(0, -1), (1, -1), (2, -1)]}
+    finals = {0: [4], 1: [1, 4], 2: [2, 4], 3: [3]}
+
+    for unit, (kind, matrix, row, rows, _, absent) in enumerate(units):
+        for copy in given[unit]:
+            copy.wait_recv()
+        for copy in loads[unit]:
+            copy.wait()
+        for owner in range(4):
+            if owner in absent:
+                chip[unit][owner] = jnp.zeros(chip[unit].shape[1:], bf16)
+                continue
+
+            def add(tile, owner=owner, unit=unit):
+                total = chip[unit][owner, tile, :].astype(f32) + local[unit][owner, tile, :].astype(f32)
+                chip[unit][owner, tile, :] = total.astype(bf16)
+
+            row_tiles(rows, add)
+        for end in (0, 3):
+
+            @pl.when(at == end)
+            def _(unit=unit, end=end, absent=absent):
+                for owner, step in routes_of[end]:
+                    if owner not in absent:
+                        line_copy(unit, owner, step, end).start()
+                came[unit][0 if end == 0 else 4] = jnp.zeros(chip[unit].shape[1:], bf16)
+
+        for owner in absent:
+
+            @pl.when(at == owner)
+            def _(unit=unit, owner=owner):
+                came[unit][owner] = jnp.zeros(chip[unit].shape[1:], bf16)
+                came[unit][4] = jnp.zeros(chip[unit].shape[1:], bf16)
+
+    def forward(unit):
+        rows, absent = units[unit][3], units[unit][5]
+        for middle in (1, 2):
+
+            @pl.when(at == middle)
+            def _(middle=middle):
+                for owner, step in routes_of[middle]:
+                    if owner in absent:
+                        continue
+                    arrived(unit, owner)
+
+                    def add(tile, owner=owner):
+                        total = chip[unit][owner, tile, :].astype(f32) + came[unit][owner, tile, :].astype(f32)
+                        chip[unit][owner, tile, :] = total.astype(bf16)
+
+                    row_tiles(rows, add)
+                    line_copy(unit, owner, step, middle).start()
+
+    def plane_copies(unit, second_step):
+        rows = units[unit][3]
+        middle = rows // 32 * 16
+        sides = (side_y, side_x) if second_step else (side_x, side_y)
+        landing = swapped_two if second_step else swapped
+        copies = []
+        for half, (begin, size) in enumerate(((0, middle), (middle, rows - middle))):
+            part = pl.ds(begin, size)
+            copies.append(
+                pltpu.make_async_remote_copy(
+                    delta[unit].at[part], landing[unit].at[part], plane_send.at[unit, 2 * second_step + half],
+                    plane_recv.at[unit, 2 * second_step + half], device_id=sides[half], device_id_type=MESH_ID,
+                )
+            )
+        return copies
+
+    def out_copy(unit, means):
+        kind, matrix, row, rows, _, _ = units[unit]
+        target = ((g_ex.at[matrix], g_li, g_lo), (m_ex.at[matrix], m_li, m_lo))[means][kind]
+        source = first[unit] if means else weight[unit]
+        return pltpu.make_async_copy(source, target.at[pl.ds(row, rows)], out_sem.at[unit, means])
+
+    firsts, seconds = {}, {}
+
+    def finish(unit):
+        kind, matrix, row, rows, _, absent = units[unit]
+        for place in range(4):
+
+            @pl.when(at == place)
+            def _(place=place):
+                if place not in absent:
+                    for slot in finals[place]:
+                        arrived(unit, slot)
+
+        for copy in state_loads[unit]:
+            copy.wait()
+        if kind == 1 and row == 0:
+            extra_load.wait()
+
+        def body(tile):
+            grad = chip[unit][at, tile, :].astype(f32) + came[unit][at, tile, :].astype(f32)
+            grad = grad + came[unit][4, tile, :].astype(f32)
+            if kind == 1:
+                grad = grad + extra_buf[pl.ds(row + tile.start, TILE), :]
+            change = adam_delta(weight[unit][tile, :], grad, first[unit][tile, :], second[unit][tile, :])
+            delta[unit][tile, :] = change.astype(bf16)
+            weight[unit][tile, :] = grad
+
+        row_tiles(rows, body)
+        out_copy(unit, 0).start()
+        firsts[unit] = plane_copies(unit, 0)
+        for copy in firsts[unit]:
+            copy.start()
+
+    def exchange(unit):
+        for copy in firsts[unit]:
+            copy.wait()
+
+        def body(tile):
+            total = delta[unit][tile, :].astype(f32) + swapped[unit][tile, :].astype(f32)
+            delta[unit][tile, :] = total.astype(bf16)
+
+        row_tiles(units[unit][3], body)
+        seconds[unit] = plane_copies(unit, 1)
+        for copy in seconds[unit]:
+            copy.start()
+
+    def close(unit):
+        for copy in seconds[unit]:
+            copy.wait_recv()
+
+        def body(tile):
+            first[unit][tile, :] = delta[unit][tile, :].astype(f32) + swapped_two[unit][tile, :].astype(f32)
+
+        row_tiles(units[unit][3], body)
+        out_copy(unit, 1).start()
+
+    for turn in range(number + 3):
+        for lag, action in enumerate((forward, finish, exchange, close)):
+            if 0 <= turn - lag < number:
+                action(turn - lag)
+
+    for unit in range(number):
+        for copy in given[unit]:
+            copy.wait_send()
+        for copy in seconds[unit]:
+            copy.wait_send()
+        out_copy(unit, 0).wait()
+        out_copy(unit, 1).wait()
+        for place in range(4):
+
+            @pl.when(at == place)
+            def _(place=place, unit=unit):
+                for owner, step in routes_of[place]:
+                    if owner not in units[unit][5]:
+                        line_copy(unit, owner, step, place).wait_send()
+
+
+def reduce_layer(layer, dex, dqkvo, dup, ddn, extra, states):
+    units = reduce_units()
+    scratch = []
+    for lead, kind in (((4,), bf16), ((4,), bf16), ((5,), bf16), ((), bf16), ((), bf16), ((), bf16), ((), f32), ((), f32), ((), f32)):
+        scratch += [pltpu.VMEM(lead + (unit[3], unit[4]), kind) for unit in units]
+    number = len(units)
+    scratch.append(pltpu.VMEM(extra.shape, f32))
+    dma = pltpu.SemaphoreType.DMA
+    scratch += [dma((number, 3)), dma((number, 3)), dma((number, 4)), dma((number, 5)), dma((number + 1, 6))]
+    scratch += [dma((number, 4)), dma((number, 4)), dma((number, 2))]
+    anywhere = pl.BlockSpec(memory_space=pl.ANY)
+    shapes = [(2, D, CHUNK), extra.shape, (D, D)] * 2
+    return pl.pallas_call(
+        functools.partial(reduce_kernel, layer),
+        out_shape=[shape_of(shape, f32) for shape in shapes],
+        in_specs=[anywhere] * (5 + len(states)),
+        out_specs=[anywhere] * 6,
+        scratch_shapes=scratch,
+        compiler_params=pltpu.CompilerParams(
+            vmem_limit_bytes=62 * MIB, collective_id=1 + layer, has_side_effects=True
+        ),
+        name="reduce_layer",
+    )(dex, dqkvo, dup, ddn, extra, *states)
+
+
+def plane_sum(delta):
+    middle = delta.shape[0] // 2
+    swaps = [[(i, i ^ bit) for i in range(4)] for bit in (1, 2)]
+    totals = []
+    for half, order in ((delta[:middle], (0, 1)), (delta[middle:], (1, 0))):
+        for axis in order:
+            half = to_half(half.astype(f32) + lax.ppermute(half, "group", swaps[axis]).astype(f32))
+        totals.append(half.astype(f32))
+    return jnp.concatenate(totals, axis=0)
 
 
 SHARD = ("expert", "dp")
@@ -1142,26 +1463,45 @@
     grad, grad_fin, grad_out_w, loss_rows = final_step(tokens, fin_mods, fo_rows, target_noise.T)
     loss_total = lax.psum(jnp.sum(loss_rows), ("group", "expert", "dp"))
 
-    grad_mods = [None] * LAYERS
-    lin_sum, lout_sum, expert_sum = [None] * LAYERS, [None] * LAYERS, [None] * LAYERS
+    stem_cols = stem_weights.shape[1]
+    lin_cols = layer_in.shape[2]
+
+    def outer(left_in, right_in):
+        return lax.dot_general(left_in, right_in, (((0,), (0,)), ((), ())), precision=highest)
+
+    def flip(values):
+        return jnp.swapaxes(values, -1, -2)
+
+    states = (experts, experts_first, experts_second, lin_t, flip(layer_in_first[0]), flip(layer_in_second[0]))
+    states = states + (layer_out, layer_out_first, layer_out_second)
+    grad_mods, reduced = [None] * LAYERS, [None] * LAYERS
     for layer in reversed(range(LAYERS)):
         tokens, g4, normed, qkv, attended, branch, middle, n2, active, slope, mixed = saved[layer]
         dup, ddn, dex, gn2, grad_gate = ffn_backward(
             grad, n2, mods[layer], g4, mixed, active, slope, lin_all[layer], lout_all[layer], expert_all[layer], halves
         )
         grad, grad_mods[layer], dqkvo = attn_backward(
-            gn2, grad, middle, tokens, normed, qkv, attended, branch, mods[layer], grad_gate, lin_all[layer]
+            gn2, grad, middle, tokens, normed, qkv, attended, branch, mods[layer], grad_gate, lin_all[layer],
+            halves * lin_cols,
         )
-        expert_sum[layer] = lax.psum_scatter(dex, SHARD, scatter_dimension=0, tiled=True)
-        lout_sum[layer] = lax.psum_scatter(ddn, SHARD, scatter_dimension=0, tiled=True)
-        dlin = jnp.concatenate([dqkvo, jnp.zeros((6 * D, D), bf16), dup], axis=0)
-        lin_sum[layer] = lax.psum_scatter(dlin, SHARD, scatter_dimension=0, tiled=True)
+        factors = jnp.concatenate([cond[:items], grad_mods[layer][:items]], axis=1)
+        factors = lax.all_gather(factors, SHARD, axis=0, tiled=True)
+        spread = jnp.pad(factors[:, D:], ((0, 0), (4 * D, lin_cols * sharers - 10 * D)))
+        window = lax.dynamic_slice_in_dim(spread, place * lin_cols, lin_cols, axis=1)
+        reduced[layer] = reduce_layer(
+            layer,
+            dex.reshape((-1, halves) + dex.shape[1:]),
+            dqkvo.reshape(halves, lin_cols, D),
+            dup.reshape(-1, halves, lin_cols, D),
+            ddn.reshape(-1, halves, layer_out.shape[1], D),
+            outer(window, factors[:, :D]),
+            states,
+        )
     grad_patch = product_tn(patches, to_half(grad))
     dpre_one, dpre_two = cond_backward(grad_mods[0], grad_mods[1], grad_fin, pre_one, pre_two, stem_all, ada_at)
 
     factors = jnp.concatenate(
-        [cond[:items], hidden[:items], dpre_one[:items], dpre_two[:items], grad_fin[:items], grad_mods[0][:items], grad_mods[1][:items], feat],
-        axis=1,
+        [cond[:items], hidden[:items], dpre_one[:items], dpre_two[:items], grad_fin[:items], feat], axis=1
     )
     width = factors.shape[1]
     packed = jnp.concatenate([factors.reshape(-1), grad_patch.reshape(-1), grad_out_w.reshape(-1)])
@@ -1169,17 +1509,10 @@
     ends = gathered[:, items * width :].reshape(sharers, 2, PATCH_DIM, D).sum(axis=0)
     factors = gathered[:, : items * width].reshape(sharers * items, width)
     hot_all = label_table(lax.all_gather(labels, SHARD, axis=0, tiled=True))
-    cond_f, hidden_f, done_f, dtwo_f, fin_f, gm_a, gm_b, feat_f = jnp.split(
-        factors, [D, 2 * D, 3 * D, 4 * D, 6 * D, 12 * D, 18 * D], axis=1
-    )
-    stem_cols = stem_weights.shape[1]
-    lin_cols = layer_in.shape[2]
+    cond_f, hidden_f, done_f, dtwo_f, fin_f, feat_f = jnp.split(factors, [D, 2 * D, 3 * D, 4 * D, 6 * D], axis=1)
 
     def own(values):
         return lax.dynamic_slice_in_dim(values, place * stem_cols, stem_cols, axis=1)
-
-    def outer(left_in, right_in):
-        return lax.dot_general(left_in, right_in, (((0,), (0,)), ((), ())), precision=highest)
 
     stem_grad = jnp.concatenate(
         [
@@ -1192,38 +1525,36 @@
         ],
         axis=1,
     )
-    lin_grads = []
-    for layer, gm in ((0, gm_a), (1, gm_b)):
-        spread = jnp.pad(gm, ((0, 0), (4 * D, lin_cols * sharers - 10 * D)))
-        window = lax.dynamic_slice_in_dim(spread, place * lin_cols, lin_cols, axis=1)
-        lin_grads.append(lin_sum[layer].astype(f32) + outer(window, cond_f))
-    lin_grad = jnp.stack(lin_grads)
-    lout_grad = jnp.stack(lout_sum).astype(f32)
-    expert_grad = jnp.stack(expert_sum).astype(f32)
-
-    weights_all = (stem_t, lin_t, layer_out, experts)
-    gradients = (stem_grad, lin_grad, lout_grad, expert_grad)
-    firsts = (stem_first[0].T, jnp.swapaxes(layer_in_first[0], 1, 2), layer_out_first[0], experts_first[0])
-    seconds = (stem_second[0].T, jnp.swapaxes(layer_in_second[0], 1, 2), layer_out_second[0], experts_second[0])
-    moments = (stem_moment.T, jnp.swapaxes(layer_in_moment, 1, 2), layer_out_moment, experts_moment)
     group_count = lax.axis_size("group")
-    new_weights, halves_out, first_out, second_out, new_moments = [], [], [], [], []
-    for at in range(4):
-        delta, first_new, second_new = adam_step(weights_all[at], gradients[at], firsts[at], seconds[at])
-        mean_delta = lax.psum(to_half(delta), "group").astype(f32) / group_count
-        moment_new = outer_mom * moments[at] + mean_delta
-        new_weight = weights_all[at] - outer_rate * (mean_delta + outer_mom * moment_new)
-        results = [new_weight, to_half(new_weight), first_new, second_new, moment_new]
-        if at == 0:
-            results = [value.T for value in results]
-        if at == 1:
-            results = [jnp.swapaxes(value, 1, 2) for value in results]
-        new_weights.append(results[0])
-        halves_out.append(results[1])
-        first_out.append(results[2][None])
-        second_out.append(results[3][None])
-        new_moments.append(results[4])
-    return (loss_total, *new_weights, *halves_out, *first_out, *second_out, *new_moments)
+
+    def update(weight, gradient, first, second, moment, total):
+        delta, first_new, second_new = adam_step(weight, gradient, first, second)
+        if total is None:
+            total = plane_sum(to_half(delta))
+        mean_delta = total / group_count
+        moment_new = outer_mom * moment + mean_delta
+        new_weight = weight - outer_rate * (mean_delta + outer_mom * moment_new)
+        return new_weight, to_half(new_weight), first_new[None], second_new[None], moment_new
+
+    def update_layers(at, weight, first, second, moment):
+        parts = [
+            update(weight[layer], reduced[layer][at], first[layer], second[layer], moment[layer], reduced[layer][3 + at])
+            for layer in range(LAYERS)
+        ]
+        return [jnp.stack([parts[0][out], parts[1][out]], axis=1 if out in (2, 3) else 0) for out in range(5)]
+
+    stem_out = [flip(v) for v in update(stem_t, stem_grad, stem_first[0].T, stem_second[0].T, stem_moment.T, None)]
+    lin_out = update_layers(1, lin_t, flip(layer_in_first[0]), flip(layer_in_second[0]), flip(layer_in_moment))
+    lin_out = [flip(v) for v in lin_out]
+    lout_out = update_layers(2, layer_out, layer_out_first[0], layer_out_second[0], layer_out_moment)
+    pairs = [v.reshape((LAYERS,) + v.shape[-3:]) for v in (experts, experts_first, experts_second, experts_moment)]
+    expert_out = update_layers(0, *pairs)
+    likes = (experts, experts, experts_first, experts_second, experts)
+    expert_out = [v.reshape(like.shape) for v, like in zip(expert_out, likes)]
+    results = []
+    for at in range(5):
+        results += [stem_out[at], lin_out[at], lout_out[at], expert_out[at]]
+    return (loss_total, *results)
 
 
 def solution(mesh):

time: 1210 us -> 1100 us (0.909)
  waiting for transfers between devices: 726 us -> 281 us
  Pallas kernels: 291 us -> 587 us
  blocking collectives: 44.9 us -> 94.6 us
  other arithmetic: 70.4 us -> 45.9 us
    reduce_scatter x6 -> x0, waiting for transfers between devices: 376 us -> none  [the longest x2 192 us: few_experts(): lax.psum_scatter(dex, SHARD, scatter_dimension=0, tiled=True)]
    pallas_call x0 -> x2, Pallas kernels: none -> 295 us  [reduce_layer(): pl.pallas_call(functools.partial(reduce_kernel, layer), out_shape=[shape_...]
    psum x1 -> x0, waiting for transfers between devices: 58.4 us -> none  [few_experts(): mean_delta = lax.psum(to_half(delta), 'group').astype(f32) / group_count]
    all_gather x0 -> x3, blocking collectives: none -> 44.6 us  [the longest x2 28.7 us: few_experts(): factors = lax.all_gather(factors, SHARD, axis=0, tiled=True)]
    another operation x3 -> x11, other arithmetic: 4.53 us -> 18.7 us  [update_layers(): jnp.stack([parts[0][out], parts[1][out]], axis=1 if out in (2, 3) else 0)]
    convert_element_type x4, other arithmetic: 15.2 us -> 2.09 us  [to_half(): return values.astype(jnp.bfloat16)]
    all_gather x1, waiting for transfers between devices: 17.5 us -> 5.25 us  [few_experts(): lax.all_gather(stem_lanes(to_half(stem_t)), SHARD, axis=0, tiled=True)]
    unnamed x152 -> x170, local copies, waits for them, and re-layouts: 30.9 us -> 34.8 us
  transfers between devices with their start and end apart: 15 -> 11, of which waited for: 14 -> 8; matrix products, arithmetic and copies ran while one was open for 5% -> 6% of each run, Pallas kernels for 6% -> 34%
where the time goes in v2:
time: 1100 us; the launch traced here: 1090 us
  Pallas kernels  587 us (53%)
  waiting for transfers between devices  281 us (26%)
  blocking collectives  94.6 us (9%)
  local copies, waits for them, and re-layouts  52.2 us (5%)
  other arithmetic  45.9 us (4%)
  between operations  15.9 us (1%)
    pallas_call x2, Pallas kernels, reduce_layer(): pl.pallas_call(functools.partial(reduce_kernel, layer), out_shape=[shape_...  295 us
    all_gather x2, waiting for transfers between devices, few_experts(): lax.all_gather(to_half(experts[layer]), SHARD, axis=0, tiled=True)  147 us
    pallas_call x2, Pallas kernels, ffn_backward(): pl.pallas_call(functools.partial(ffn_bwd_kernel, shared_steps, halves), g...  114 us
    all_gather x2, waiting for transfers between devices, few_experts(): lax.all_gather(to_half(lin_t[layer]), SHARD, axis=0, tiled=True)  112 us
    pallas_call x2, Pallas kernels, ffn_forward(): pl.pallas_call(functools.partial(ffn_fwd_kernel, shared_steps, halves), g...  107 us
    pallas_call x2, Pallas kernels, attn_backward(): pl.pallas_call(attn_bwd_kernel, grid=(count // PATCHES,), in_specs=[rows_...  46.2 us
    psum x1, blocking collectives, few_experts(): loss_total = lax.psum(jnp.sum(loss_rows), ('group', 'expert', 'dp'))  38.7 us
    unnamed x170, local copies, waits for them, and re-layouts  34.8 us
  transfers between devices with their start and end apart: 11, of which 8 were waited for; matrix products, arithmetic and copies ran while one was open for 6% of the time, Pallas kernels for 34%

profile of v2, /device:TPU:0, one launch (start us, length us, event | category | flops | bytes accessed | tf_op | source)
XLA Modules:
  0.0 1091.5 jit_solution(17091782713864759407)
XLA Ops:
  10.2 2.9 fusion.25
  14.9 4.0 fusion.82
  24.0 11.3 %all-reduce.6 = s32[32]{0:T(128)} all-reduce(s32[32]{0:T(128)S(1)} %dynamic-update-slice), channel_id=1, replica_groups=mesh['group'=4,'expert'=4,'dp'=2] {'expert','dp'}, use_global_device_ids=true, to_apply=%add.6 | all-reduce | flops 32 | bytes 256
  36.8 5.2 all-gather.13.cloned.1.call-done.stem_ref
  44.3 56.0 %all-gather.15.cloned.1.call-done.w_ref.up_ref = bf16[6912,384]{1,0:T(8,128)(2,1)} async-done(((bf16[864,384]{1,0:T(8,128)(2,1)}), bf16[6912,384]{1,0:T(8,128)(2,1)}) %all-gather.15.cloned.1.call-update) | async-done | bytes 5308432 | tf_op jit(solution)/shard_map/all_gather | solution.py:1438
  100.3 1.7 slice.280.ada_a
  102.0 55.9 %all-gather.17.cloned.1.call-done.w_ref.up_ref = bf16[6912,384]{1,0:T(8,128)(2,1)} async-done(((bf16[864,384]{1,0:T(8,128)(2,1)}), bf16[6912,384]{1,0:T(8,128)(2,1)}) %all-gather.17.cloned.1.call-update) | async-done | bytes 5308432 | tf_op jit(solution)/shard_map/all_gather | solution.py:1438
  157.9 1.8 slice.282.ada_b
  160.1 2.0 cond_forward.1
  163.9 9.6 attention_forward.2
  179.9 10.5 all-gather.19.cloned.1.call-done.dn_ref
  190.4 91.9 %all-gather.23.cloned.1.call-done = bf16[8,1,2,384,768]{4,3,2,1,0:T(8,128)(2,1)} async-done(((bf16[1,1,2,384,768]{4,3,2,1,0:T(8,128)(2,1)}), bf16[8,1,2,384,768]{4,3,2,1,0:T(8,128)(2,1)}) %all-gather.23.cloned.1.call-update) | async-done | bytes 9437200 | tf_op jit(solution)/shard_map/all_gather | solution.py:1440
  282.4 53.2 %ffn_forward.2 = (bf16[12,1024,768]{2,1,0:T(8,128)(2,1)}, bf16[12,1024,768]{2,1,0:T(8,128)(2,1)}, f32[1024,384]{1,0:T(8,128)}, f32[1024,384]{1,0:T(8,128)}) custom-call(bf16[1024,384]{1,0:T(8,128)(2,1)} %copy-done.30, f32[1024,384]{1,0:T(8,128)} %copy-done.22, f32[8,2304]{1,0:T(8,128)} %copy-done.9, f32[1024,4]{1,0:T(8,128)} %copy.81.g4_ref, ...), custom_call_target="tpu_custom_call" | custom-call | flops 57982058496 | bytes 75497472 | tf_op jit(solution)/shard_map/ffn_forward/pallas_call | solution.py:1001
  337.1 9.4 attention_forward.3
  351.9 54.7 %all-gather.25.cloned.1.call-done = bf16[8,1,2,384,768]{4,3,2,1,0:T(8,128)(2,1)} async-done(((bf16[1,1,2,384,768]{4,3,2,1,0:T(8,128)(2,1)}), bf16[8,1,2,384,768]{4,3,2,1,0:T(8,128)(2,1)}) %all-gather.25.cloned.1.call-update) | async-done | bytes 9437200 | tf_op jit(solution)/shard_map/all_gather | solution.py:1440
  406.6 53.4 %ffn_forward.3 = (bf16[12,1024,768]{2,1,0:T(8,128)(2,1)}, bf16[12,1024,768]{2,1,0:T(8,128)(2,1)}, f32[1024,384]{1,0:T(8,128)}, f32[1024,384]{1,0:T(8,128)}) custom-call(bf16[1024,384]{1,0:T(8,128)(2,1)} %copy-done.33, f32[1024,384]{1,0:T(8,128)} %copy-done.25, f32[8,2304]{1,0:T(8,128)} %copy-done.11, f32[1024,4]{1,0:T(8,128)} %copy.82.g4_ref, ...), custom_call_target="tpu_custom_call" | custom-call | flops 57982058496 | bytes 75497472 | tf_op jit(solution)/shard_map/ffn_forward/pallas_call | solution.py:1001
  461.5 3.2 final_step.1
  466.5 57.4 %ffn_backward.2 = (bf16[3456,384]{1,0:T(8,128)(2,1)}, bf16[3072,384]{1,0:T(8,128)(2,1)}, bf16[8,2,384,768]{3,2,1,0:T(8,128)(2,1)}, f32[1024,384]{1,0:T(8,128)}, f32[8,384]{1,0:T(8,128)}) custom-call(f32[1024,384]{1,0:T(8,128)} %copy-done.18, bf16[1024,384]{1,0:T(8,128)(2,1)} %copy-done.33, f32[8,2304]{1,0:T(8,128)} %copy-done.11, f32[1024,4]{1,0:T(8,128)} %copy.82.g4_ref, ...), custom_call_target="tpu_custom_call" | custom-call | flops 57982058496 | bytes 75497472 | tf_op jit(solution)/shard_map/ffn_backward/pallas_call | solution.py:1026
  525.7 22.9 %attention_backward.2 = (f32[1024,384]{1,0:T(8,128)}, f32[8,2304]{1,0:T(8,128)S(1)}, bf16[1728,384]{1,0:T(8,128)(2,1)S(1)}) custom-call(f32[1024,384]{1,0:T(8,128)} %get-tuple-element.96.gn2_ref, f32[1024,384]{1,0:T(8,128)} %copy-done.18, f32[1024,384]{1,0:T(8,128)} %copy-done.25, f32[1024,384]{1,0:T(8,128)} %get-tuple-element.84.x_ref, ...), custom_call_target="tpu_custom_call" | custom-call | flops 26575110144 | bytes 6291456 | tf_op jit(solution)/shard_map/attention_backward/pallas_call | solution.py:973
  549.7 57.1 %ffn_backward.3 = (bf16[3456,384]{1,0:T(8,128)(2,1)}, bf16[3072,384]{1,0:T(8,128)(2,1)}, bf16[8,2,384,768]{3,2,1,0:T(8,128)(2,1)}, f32[1024,384]{1,0:T(8,128)}, f32[8,384]{1,0:T(8,128)}) custom-call(f32[1024,384]{1,0:T(8,128)} %get-tuple-element.102.g_ref, bf16[1024,384]{1,0:T(8,128)(2,1)} %copy-done.30, f32[8,2304]{1,0:T(8,128)} %copy-done.9, ...), custom_call_target="tpu_custom_call" | custom-call | flops 57982058496 | bytes 75497472 | tf_op jit(solution)/shard_map/ffn_backward/pallas_call | solution.py:1026
  608.7 23.3 %attention_backward.3 = (f32[1024,384]{1,0:T(8,128)}, f32[8,2304]{1,0:T(8,128)S(1)}, bf16[1728,384]{1,0:T(8,128)(2,1)S(1)}) custom-call(f32[1024,384]{1,0:T(8,128)} %get-tuple-element.106.gn2_ref, f32[1024,384]{1,0:T(8,128)} %get-tuple-element.102.g_ref, f32[1024,384]{1,0:T(8,128)} %copy-done.22, f32[1024,384]{1,0:T(8,128)} %copy-done.6, ...), custom_call_target="tpu_custom_call" | custom-call | flops 26575110144 | bytes 6291456 | tf_op jit(solution)/shard_map/attention_backward/pallas_call | solution.py:973
  633.0 1.6 convolution_bitcast_fusion
  634.7 1.5 copy-done.2
  636.1 1.6 copy-done.4
  639.1 15.9 %all-gather.2 = f32[180224]{0:T(1024)S(1)} all-gather(f32[22528]{0:T(1024)S(1)} %pad_maximum_fusion.7), channel_id=4, replica_groups=mesh['group'=4,'expert'=4,'dp'=2] {'expert','dp'}, dimensions={0}, use_global_device_ids=true | all-gather | bytes 811008 | tf_op jit(solution)/shard_map/all_gather | solution.py:1508
  655.9 38.7 %psum.7 = f32[]{:T(128)} all-reduce(f32[]{:T(128)} %reduce_sum.38), channel_id=1, replica_groups=mesh['group'=4,'expert'=4,'dp'=2] {'group','expert','dp'}, use_global_device_ids=true, to_apply=%region_3.4 | all-reduce | flops 1 | bytes 8 | tf_op jit(solution)/shard_map/psum | solution.py:1464
  698.8 2.3 collective-permute-start
  701.9 14.3 %all-gather.3 = f32[8,4,2688]{2,1,0:T(4,128)S(1)} all-gather(f32[1,4,2688]{2,1,0:T(4,128)S(1)} %get-tuple-element.296), channel_id=1, replica_groups=mesh['group'=4,'expert'=4,'dp'=2] {'expert','dp'}, dimensions={0}, use_global_device_ids=true | all-gather | bytes 387072 | tf_op jit(solution)/shard_map/all_gather | solution.py:1488
  716.4 14.4 %all-gather.4 = f32[8,4,2688]{2,1,0:T(4,128)S(1)} all-gather(f32[1,4,2688]{2,1,0:T(4,128)S(1)} %get-tuple-element.297), channel_id=1, replica_groups=mesh['group'=4,'expert'=4,'dp'=2] {'expert','dp'}, dimensions={0}, use_global_device_ids=true | all-gather | bytes 387072 | tf_op jit(solution)/shard_map/all_gather | solution.py:1488
  730.9 2.5 fusion.45.extra
  733.4 2.5 fusion.46.extra
  735.9 147.0 %reduce_layer.2 = (f32[2,384,768]{2,1,0:T(8,128)}, f32[864,384]{1,0:T(8,128)}, f32[384,384]{1,0:T(8,128)}, f32[2,384,768]{2,1,0:T(8,128)}, f32[864,384]{1,0:T(8,128)}, /*index=5*/f32[384,384]{1,0:T(8,128)}) custom-call(bf16[4,2,2,384,768]{4,3,2,1,0:T(8,128)(2,1)} %bitcast.371, bf16[2,864,384]{2,1,0:T(8,128)(2,1)} %bitcast.352, ...), custom_call_target="tpu_custom_call" | custom-call | tf_op jit(solution)/shard_map/reduce_layer/pallas_call | solution.py:1375
  882.9 147.8 %reduce_layer.3 = (f32[2,384,768]{2,1,0:T(8,128)}, f32[864,384]{1,0:T(8,128)}, f32[384,384]{1,0:T(8,128)}, f32[2,384,768]{2,1,0:T(8,128)}, f32[864,384]{1,0:T(8,128)}, /*index=5*/f32[384,384]{1,0:T(8,128)}) custom-call(bf16[4,2,2,384,768]{4,3,2,1,0:T(8,128)(2,1)} %bitcast.370, bf16[2,864,384]{2,1,0:T(8,128)(2,1)} %bitcast.351, ...), custom_call_target="tpu_custom_call" | custom-call | tf_op jit(solution)/shard_map/reduce_layer/pallas_call | solution.py:1375
  1030.8 4.1 convert_bitcast_fusion.3
  1034.9 1.7 maximum_bitcast_fusion.4
  1041.2 3.2 convert_bitcast_fusion.1
  1044.4 2.5 maximum_bitcast_fusion
  1048.1 1.6 maximum_bitcast_fusion.8
  1052.2 1.7 maximum_bitcast_fusion.5
  1058.8 2.8 fusion.5
  1061.7 2.5 maximum_bitcast_fusion.1
  1064.2 1.7 maximum_bitcast_fusion.6
  1066.9 2.5 maximum_bitcast_fusion.2
  1069.4 1.7 maximum_bitcast_fusion.7
  1071.1 2.5 maximum_bitcast_fusion.3
  1075.7 1.8 collective-permute-start.3
  1078.7 2.4 collective-permute-done.3
  1081.2 2.1 collective-permute-done.1
  (262 shorter events, 63.4 us)
Async XLA Ops:
  7.2 35.8 %copy-start = (bf16[1024,16]{0,1:T(8,128)(2,1)S(1)}, bf16[1024,16]{0,1:T(8,128)(2,1)}, u32[]{:S(2)}) copy-start(bf16[1024,16]{0,1:T(8,128)(2,1)} %param.22) | copy-start | bytes 98308
  7.2 34.8 %all-gather.13.cloned.1.call-start = ((), (), s32[]{:S(2)}) async-start(), calls=%async_computation | async-start | bytes 2322432 | tf_op jit(solution)/shard_map/all_gather | solution.py:1435
  9.2 4.7 copy-start.38
  10.1 90.2 %all-gather.15.cloned.1.call-start = ((), (), s32[]{:S(2)}) async-start(), calls=%async_computation.1 | async-start | bytes 5971968 | tf_op jit(solution)/shard_map/all_gather | solution.py:1438
  13.1 144.8 %all-gather.17.cloned.1.call-start = ((), (), s32[]{:S(2)}) async-start(), calls=%async_computation.2 | async-start | bytes 5971968 | tf_op jit(solution)/shard_map/all_gather | solution.py:1438
  13.8 176.6 %all-gather.19.cloned.1.call-start = ((), (), s32[]{:S(2)}) async-start(), calls=%async_computation.3 | async-start | bytes 2654208 | tf_op jit(solution)/shard_map/all_gather | solution.py:1439
  14.8 267.6 %all-gather.23.cloned.1.call-start = ((), (), s32[]{:S(2)}) async-start(), calls=%async_computation.5 | async-start | bytes 10616832 | tf_op jit(solution)/shard_map/all_gather | solution.py:1440
  18.9 3.6 copy-start.72
  18.9 4.8 copy-start.70
  18.9 333.0 %all-gather.21.cloned.1.call-start = ((), (), s32[]{:S(2)}) async-start(), calls=%async_computation.4 | async-start | bytes 2654208 | tf_op jit(solution)/shard_map/all_gather | solution.py:1439
  19.5 387.1 %all-gather.25.cloned.1.call-start = ((), (), s32[]{:S(2)}) async-start(), calls=%async_computation.6 | async-start | bytes 10616832 | tf_op jit(solution)/shard_map/all_gather | solution.py:1440
  20.3 16.2 %copy-start.65 = (f32[4]{0:T(128)}, f32[4]{0:T(128)S(1)}, u32[]{:S(2)}) copy-start(f32[4]{0:T(128)S(1)} %convert_element_type.149) | copy-start | bytes 52
  44.3 119.6 %copy-start.6 = (f32[1024,384]{1,0:T(8,128)}, f32[1024,384]{1,0:T(8,128)S(1)}, u32[]{:S(2)}) copy-start(f32[1024,384]{1,0:T(8,128)S(1)} %bitcast_add_fusion.4.x_ref) | copy-start | bytes 4718596
  163.9 9.6 copy-start.9
  163.9 171.7 %copy-start.11 = (f32[8,2304]{1,0:T(8,128)}, f32[8,2304]{1,0:T(8,128)S(1)}, u32[]{:S(2)}) copy-start(f32[8,2304]{1,0:T(8,128)S(1)} %get-tuple-element.286.mods_ref) | copy-start | bytes 221188
  406.6 53.5 %copy-start.13 = (f32[1024,16]{0,1:T(8,128)S(1)}, f32[1024,16]{0,1:T(8,128)}, u32[]{:S(2)}) copy-start(f32[1024,16]{0,1:T(8,128)} %param.23) | copy-start | bytes 196612
  406.6 53.5 %copy-start.15 = (f32[8,768]{1,0:T(8,128)S(1)}, f32[8,768]{1,0:T(8,128)}, u32[]{:S(2)}) copy-start(f32[8,768]{1,0:T(8,128)} %copy-done.14) | copy-start | bytes 73732
  466.5 57.4 %copy-start.12 = (f32[8,2304]{1,0:T(8,128)S(1)}, f32[8,2304]{1,0:T(8,128)}, u32[]{:S(2)}) copy-start(f32[8,2304]{1,0:T(8,128)} %copy-done.11) | copy-start | bytes 221188
  549.7 57.1 %copy-start.10 = (f32[8,2304]{1,0:T(8,128)S(1)}, f32[8,2304]{1,0:T(8,128)}, u32[]{:S(2)}) copy-start(f32[8,2304]{1,0:T(8,128)} %copy-done.9) | copy-start | bytes 221188
  549.7 57.1 %copy-start.27 = (bf16[1024,384]{1,0:T(8,128)(2,1)S(1)}, bf16[1024,384]{1,0:T(8,128)(2,1)}, u32[]{:S(2)}) copy-start(bf16[1024,384]{1,0:T(8,128)(2,1)} %copy-done.26) | copy-start | bytes 2359300
  608.6 26.0 %copy-start.17 = (f32[8,384]{1,0:T(8,128)S(1)}, f32[8,384]{1,0:T(8,128)}, u32[]{:S(2)}) copy-start(f32[8,384]{1,0:T(8,128)} %copy-done.16) | copy-start | bytes 36868
  639.1 56.5 %copy-start.69 = (s32[32]{0:T(128)S(1)}, s32[32]{0:T(128)}, u32[]{:S(2)}) copy-start(s32[32]{0:T(128)} %all-reduce.6) | copy-start | bytes 388
  655.1 41.7 %copy-start.42 = (f32[2441,48]{0,1:T(8,128)S(1)}, f32[2441,48]{0,1:T(8,128)}, u32[]{:S(2)}) copy-start(f32[2441,48]{0,1:T(8,128)} %param.28) | copy-start | bytes 1406020
  655.1 41.7 %copy-start.56 = (f32[1,2441,48]{1,2,0:T(8,128)S(1)}, f32[1,2441,48]{1,2,0:T(8,128)}, u32[]{:S(2)}) copy-start(f32[1,2441,48]{1,2,0:T(8,128)} %param.36) | copy-start | bytes 1406020
  655.1 41.7 %copy-start.57 = (f32[1,2441,48]{1,2,0:T(8,128)S(1)}, f32[1,2441,48]{1,2,0:T(8,128)}, u32[]{:S(2)}) copy-start(f32[1,2441,48]{1,2,0:T(8,128)} %param.32) | copy-start | bytes 1406020
  696.5 5.4 copy-start.62
  698.8 375.9 %collective-permute-start = (bf16[24,2441]{1,0:T(8,128)(2,1)}, bf16[24,2441]{1,0:T(8,128)(2,1)S(1)}, u32[]{:S(2)}, u32[]{:S(2)}) collective-permute-start(bf16[24,2441]{1,0:T(8,128)(2,1)} %get-tuple-element.284), channel_id=1, source_target_pairs={{0,8},{8,0},{16,24},{24,16},{1,9},{9,1},{17,25},{25,17},{2,10},{10... | collective-permute-start | bytes 351512 | tf_op jit(solution)/shard_map/ppermute | solution.py:1394
  701.1 373.7 %collective-permute-start.2 = (bf16[24,2441]{1,0:T(8,128)(2,1)}, bf16[24,2441]{1,0:T(8,128)(2,1)}, u32[]{:S(2)}, u32[]{:S(2)}) collective-permute-start(bf16[24,2441]{1,0:T(8,128)(2,1)} %get-tuple-element.285), channel_id=1, source_target_pairs={{0,16},{8,24},{16,0},{24,8},{1,17},{9,25},{17,1},{25,9},{2,18},{10... | collective-permute-start | bytes 351512 | tf_op jit(solution)/shard_map/ppermute | solution.py:1394
  1030.8 5.9 copy-start.55
  1034.9 2.6 copy-start.50
  1034.9 2.7 copy-start.54
  1034.9 4.9 copy-start.45
  1036.6 3.3 slice-start
  1044.4 5.3 copy-start.49
  1046.9 2.8 copy-start.37
  1048.1 2.9 copy-start.36
  1048.1 3.2 copy-start.48
  1051.3 2.6 copy-start.52
  1051.4 2.6 copy-start.53
  1052.2 4.2 slice-start.2
  1052.2 5.6 slice-start.4
  1053.9 3.9 slice-start.3
  1053.9 3.9 slice-start.5
  1055.3 3.5 copy-start.43
  1073.6 3.9 copy-start.51
  1073.6 9.7 copy-start.58
  1075.7 5.4 collective-permute-start.3
  1078.4 4.9 collective-permute-start.1
  (42 other events, 56.5 us)
Sparse Core Ops, SparseCore 0:
  10.3 31.6 all-gather.12
  44.2 56.0 all-gather.14
  102.5 55.3 all-gather.16
  160.0 30.3 all-gather.18
  192.5 89.8 all-gather.22
  284.4 30.0 all-gather.20
  316.8 89.8 all-gather.24

commit v3 on v2

--- a/solution.py
+++ b/solution.py
@@ -7,6 +7,7 @@
 from jax.experimental.pallas import tpu as pltpu
 from jax.sharding import PartitionSpec as P
 
+GROUP, LINE, CORE = "group", "expert", "dp"
 D = 384
 HEADS = 6
 IMG = 32
@@ -181,7 +182,7 @@
     item_count = cond_act.shape[0]
     model_width = tokens.shape[1]
     local_count = expert_w.shape[0]
-    expert_count = lax.axis_size("expert") * local_count
+    expert_count = lax.axis_size(LINE) * local_count
     capacity = 4 * tokens.shape[0] // expert_count
     mods = jnp.dot(
         cond_act, lin[:, 4 * model_width : 10 * model_width].astype(jnp.float32), precision=highest
@@ -202,7 +203,7 @@
     send_rows = send_rows.at[slot_index].set(jnp.repeat(normed_two, 2, axis=0))
     received = lax.all_to_all(
         send_rows.reshape(expert_count, capacity, model_width),
-        "expert",
+        LINE,
         split_axis=0,
         concat_axis=0,
         tiled=True,
@@ -216,8 +217,8 @@
         jnp.einsum("erf,edf->erd", active_exp, expert_w[:, 1], preferred_element_type=jnp.float32)
     )
     returned = lax.all_to_all(
-        source_major(out_exp, lax.axis_size("expert")),
-        "expert",
+        source_major(out_exp, lax.axis_size(LINE)),
+        LINE,
         split_axis=0,
         concat_axis=0,
         tiled=True,
@@ -272,7 +273,7 @@
     item_count = cond_act.shape[0]
     model_width = tokens.shape[1]
     local_count = expert_w.shape[0]
-    expert_count = lax.axis_size("expert") * local_count
+    expert_count = lax.axis_size(LINE) * local_count
     capacity = 4 * tokens.shape[0] // expert_count
     grad_shaped = grad_tokens.reshape(item_count, -1, model_width)
     grad_gate_two = jnp.sum(
@@ -292,7 +293,7 @@
     )
     received = lax.all_to_all(
         send_grad.reshape(expert_count, capacity, model_width),
-        "expert",
+        LINE,
         split_axis=0,
         concat_axis=0,
         tiled=True,
@@ -314,8 +315,8 @@
         )
     )
     back_rows = lax.all_to_all(
-        source_major(grad_rows_in, lax.axis_size("expert")),
-        "expert",
+        source_major(grad_rows_in, lax.axis_size(LINE)),
+        LINE,
         split_axis=0,
         concat_axis=0,
         tiled=True,
@@ -406,11 +407,11 @@
     experts_moment,
 ):
     stem_all, lin_all, lout_all = (
-        lax.all_gather(to_half(stem_weights), ("expert", "dp"), axis=1, tiled=True),
-        lax.all_gather(to_half(layer_in), ("expert", "dp"), axis=2, tiled=True),
-        lax.all_gather(to_half(layer_out), ("expert", "dp"), axis=1, tiled=True),
-    )
-    expert_all = lax.all_gather(to_half(experts), "dp", axis=4, tiled=True)
+        lax.all_gather(to_half(stem_weights), (LINE, CORE), axis=1, tiled=True),
+        lax.all_gather(to_half(layer_in), (LINE, CORE), axis=2, tiled=True),
+        lax.all_gather(to_half(layer_out), (LINE, CORE), axis=1, tiled=True),
+    )
+    expert_all = lax.all_gather(to_half(experts), CORE, axis=4, tiled=True)
     model_width = stem_all.shape[1]
     item_count = timesteps.shape[0]
     patch_w, time_one, time_two, table_w, final_ada, final_out = split_stem(stem_all)
@@ -456,7 +457,7 @@
     final_normed = to_half(final_pre.reshape(-1, model_width))
     predicted = product_nt(final_normed, final_out)
     residual_err = predicted - target_noise
-    loss_total = lax.psum(jnp.sum(residual_err * residual_err), ("group", "expert", "dp"))
+    loss_total = lax.psum(jnp.sum(residual_err * residual_err), (GROUP, LINE, CORE))
     grad_pred = to_half(2.0 * residual_err)
     grad_final_out = product_tn(grad_pred, final_normed)
     grad_final_normed = product(grad_pred, final_out)
@@ -496,12 +497,12 @@
         axis=0,
     )
     stem_sum, lin_sum, lout_sum = (
-        lax.psum_scatter(grad_stem, ("expert", "dp"), scatter_dimension=1, tiled=True),
-        lax.psum_scatter(lin_stack, ("expert", "dp"), scatter_dimension=2, tiled=True),
-        lax.psum_scatter(lout_stack, ("expert", "dp"), scatter_dimension=1, tiled=True),
+        lax.psum_scatter(grad_stem, (LINE, CORE), scatter_dimension=1, tiled=True),
+        lax.psum_scatter(lin_stack, (LINE, CORE), scatter_dimension=2, tiled=True),
+        lax.psum_scatter(lout_stack, (LINE, CORE), scatter_dimension=1, tiled=True),
     )
     expert_sum = lax.psum_scatter(
-        expert_stack.astype(jnp.bfloat16), "dp", scatter_dimension=4, tiled=True
+        expert_stack.astype(jnp.bfloat16), CORE, scatter_dimension=4, tiled=True
     ).astype(jnp.float32)
     weights_all = (stem_weights, layer_in, layer_out, experts)
     gradients = (stem_sum, lin_sum, lout_sum, expert_sum)
@@ -518,12 +519,12 @@
         for array_idx in range(4)
     ]
     delta_all = (
-        lax.psum(stepped[0][0].astype(jnp.bfloat16), "group").astype(jnp.float32),
-        lax.psum(stepped[1][0].astype(jnp.bfloat16), "group").astype(jnp.float32),
-        lax.psum(stepped[2][0].astype(jnp.bfloat16), "group").astype(jnp.float32),
-        lax.psum(stepped[3][0].astype(jnp.bfloat16), "group").astype(jnp.float32),
-    )
-    group_count = lax.axis_size("group")
+        lax.psum(stepped[0][0].astype(jnp.bfloat16), GROUP).astype(jnp.float32),
+        lax.psum(stepped[1][0].astype(jnp.bfloat16), GROUP).astype(jnp.float32),
+        lax.psum(stepped[2][0].astype(jnp.bfloat16), GROUP).astype(jnp.float32),
+        lax.psum(stepped[3][0].astype(jnp.bfloat16), GROUP).astype(jnp.float32),
+    )
+    group_count = lax.axis_size(GROUP)
     new_weights = []
     new_moments = []
     for array_idx in range(4):
@@ -562,10 +563,12 @@
 f32 = jnp.float32
 MIB = 1024 * 1024
 CHUNK = 768
+FWD_ROWS = 256
+BWD_ROWS = 256
 STEM_SIZES = (PATCH_DIM, FREQ, D, CLASSES + 1, 2 * D, PATCH_DIM)
 STEM_PADDED = tuple(-(-size // 128) * 128 for size in STEM_SIZES)
 STEM_AT = tuple(sum(STEM_PADDED[:place]) for place in range(len(STEM_PADDED)))
-STEM_LANES = sum(STEM_PADDED)
+STEM_LANES = -(-sum(STEM_PADDED) // 1024) * 1024
 
 
 def dot_nn(left_in, right_in):
@@ -613,30 +616,35 @@
     return stem_ref[:, STEM_AT[place] : STEM_AT[place] + STEM_PADDED[place]]
 
 
-def cond_kernel(feat_ref, hot_ref, stem_ref, ada_a, ada_b, cond_ref, hid_ref, one_ref, two_ref, mods_ref, fin_ref):
-    pre_one = full_nt(feat_ref[...], stem_piece(stem_ref, 1))
-    hidden = silu_of(pre_one)
-    pre_two = full_nt(hidden, stem_piece(stem_ref, 2)) + dot_nt(hot_ref[...], stem_piece(stem_ref, 3))[0:8]
-    cond = silu_of(pre_two)
-    one_ref[...] = pre_one
-    two_ref[...] = pre_two
-    hid_ref[...] = hidden
-    cond_ref[...] = cond
-    parts = three_parts(cond)
-    for place in range(6):
-        rows = pl.ds(place * D, D)
-        mods_ref[0, :, rows] = three_sum(dot_nt(parts, ada_a[rows, :]))
-        mods_ref[1, :, rows] = three_sum(dot_nt(parts, ada_b[rows, :]))
-    fin_ref[...] = three_sum(dot_nn(parts, stem_piece(stem_ref, 4)))
-
-
-def cond_back_kernel(gm_a, gm_b, gf_ref, one_ref, two_ref, stem_ref, ada_a, ada_b, done_ref, dtwo_ref):
-    grad_cond = full_nt(gf_ref[...], stem_piece(stem_ref, 4))
-    grad_cond = grad_cond + full_nn(gm_a[...], ada_a[...]) + full_nn(gm_b[...], ada_b[...])
-    dtwo = grad_cond * silu_slope(two_ref[...])
-    dtwo_ref[...] = dtwo
-    dhid = full_nn(dtwo, stem_piece(stem_ref, 2))
-    done_ref[...] = dhid * silu_slope(one_ref[...])
+def cond_kernel(feat_ref, hot_ref, stem_ref, ada_ref, cond_ref, hid_ref, one_ref, two_ref, mods_ref, fin_ref):
+    @pl.when(pl.program_id(0) == 0)
+    def _():
+        pre_one = full_nt(feat_ref[...], stem_piece(stem_ref, 1))
+        hidden = silu_of(pre_one)
+        pre_two = full_nt(hidden, stem_piece(stem_ref, 2)) + dot_nt(hot_ref[...], stem_piece(stem_ref, 3))[0:8]
+        cond = silu_of(pre_two)
+        one_ref[...] = pre_one
+        two_ref[...] = pre_two
+        hid_ref[...] = hidden
+        cond_ref[...] = cond
+        fin_ref[...] = full_nn(cond, stem_piece(stem_ref, 4))
+
+    for layer in range(LAYERS):
+        mods_ref[layer] = full_nt(cond_ref[...], ada_ref[layer])
+
+
+def cond_back_kernel(gm_a, gm_b, gf_ref, one_ref, two_ref, stem_ref, ada_ref, done_ref, dtwo_ref):
+    @pl.when(pl.program_id(0) == 0)
+    def _():
+        dtwo_ref[...] = full_nt(gf_ref[...], stem_piece(stem_ref, 4))
+
+    dtwo_ref[...] += full_nn(gm_a[...], ada_ref[0]) + full_nn(gm_b[...], ada_ref[1])
+
+    @pl.when(pl.program_id(0) == pl.num_programs(0) - 1)
+    def _():
+        dtwo = dtwo_ref[...] * silu_slope(two_ref[...])
+        dtwo_ref[...] = dtwo
+        done_ref[...] = full_nn(dtwo, stem_piece(stem_ref, 2)) * silu_slope(one_ref[...])
 
 
 def norm_parts(values):
@@ -756,9 +764,9 @@
     square = values * values
     angle = jnp.tanh(values * (square * cubic + outer))
     half = 0.5 * values
-    active = half * angle + half
-    slope = half * (square * (3.0 * cubic) + outer) * (1.0 - angle * angle) + (0.5 * angle + 0.5)
-    return active.astype(bf16), slope.astype(bf16)
+    above = 1.0 + angle
+    slope = above * (half * (square * (3.0 * cubic) + outer) * (1.0 - angle) + 0.5)
+    return (half * above).astype(bf16), slope.astype(bf16)
 
 
 def gate_column(g4_ref, rows, expert):
@@ -767,45 +775,45 @@
     return jnp.sum(jnp.where(lane == expert, gates, 0.0), axis=1, keepdims=True)
 
 
-def ffn_fwd_kernel(shared_steps, halves, n2_ref, mid_ref, mods_ref, g4_ref, up_ref, dn_ref, ex_ref, act_ref, dg_ref, mixed_ref, x_ref, acc, racc):
+def ffn_fwd_kernel(shared_steps, halves, gathers, n2_ref, mid_ref, mods_ref, g4_ref, up_ref, dn_ref, ex_ref, *rest):
     step = pl.program_id(0)
+    given, (act_ref, dg_ref, mixed_ref, x_ref) = rest[:gathers], rest[gathers : gathers + 4]
+    taken, (acc, racc), sems = rest[gathers + 4 : 2 * gathers + 4], rest[2 * gathers + 4 : 2 * gathers + 6], rest[2 * gathers + 6 :]
+    if gathers:
+        gather_beside(step, pl.num_programs(0) - 1, given, taken, sems)
     items = n2_ref.shape[0] // PATCHES
 
+    @pl.when(step == 0)
+    def _():
+        acc[...] = jnp.zeros_like(acc)
+        racc[...] = jnp.zeros_like(racc)
+
     @pl.when(step < shared_steps)
+    def _():
+        for block in range(n2_ref.shape[0] // FWD_ROWS):
+            rows = pl.ds(block * FWD_ROWS, FWD_ROWS)
+            active, slope = gelu_both(dot_nt(n2_ref[rows, :], up_ref[...]))
+            act_ref[0, rows, :] = active
+            dg_ref[0, rows, :] = slope
+            acc[rows, :] += dot_nn(active, dn_ref[...])
+
+    @pl.when(step >= shared_steps)
+    def _():
+        for block in range(n2_ref.shape[0] // FWD_ROWS):
+            rows = pl.ds(block * FWD_ROWS, FWD_ROWS)
+            active, slope = gelu_both(dot_nn(n2_ref[rows, :], ex_ref[0, 0]))
+            act_ref[0, rows, :] = active
+            dg_ref[0, rows, :] = slope
+            racc[rows, :] += dot_nt(active, ex_ref[0, 1])
+
+    expert, half = (step - shared_steps) // halves, (step - shared_steps) % halves
+
+    @pl.when((step >= shared_steps) & (half == halves - 1))
     def _():
         for item in range(items):
             rows = pl.ds(item * PATCHES, PATCHES)
-            active, slope = gelu_both(dot_nt(n2_ref[rows, :], up_ref[...]))
-            act_ref[0, rows, :] = active
-            dg_ref[0, rows, :] = slope
-            part = dot_nn(active, dn_ref[...])
-
-            @pl.when(step == 0)
-            def _():
-                acc[rows, :] = part
-
-            @pl.when(step > 0)
-            def _():
-                acc[rows, :] += part
-
-    @pl.when(step >= shared_steps)
-    def _():
-        expert, half = (step - shared_steps) // halves, (step - shared_steps) % halves
-        for item in range(items):
-            rows = pl.ds(item * PATCHES, PATCHES)
-            active, slope = gelu_both(dot_nn(n2_ref[rows, :], ex_ref[0, 0]))
-            act_ref[0, rows, :] = active
-            dg_ref[0, rows, :] = slope
-            part = dot_nt(active, ex_ref[0, 1])
-
-            @pl.when(half == 0)
-            def _():
-                racc[rows, :] = part
-
-            @pl.when(half > 0)
-            def _():
-                routed = (racc[rows, :] + part).astype(bf16).astype(f32)
-                acc[rows, :] += gate_column(g4_ref, rows, expert) * routed
+            acc[rows, :] += gate_column(g4_ref, rows, expert) * racc[rows, :].astype(bf16).astype(f32)
+            racc[rows, :] = jnp.zeros((PATCHES, D), f32)
 
     @pl.when(step == pl.num_programs(0) - 1)
     def _():
@@ -836,11 +844,12 @@
             gst[:, rows] = grad.astype(bf16).T
             n2t[:, rows] = n2_ref[rows, :].T
         acc[...] = jnp.zeros_like(acc)
+        racc[...] = jnp.zeros_like(racc)
 
     @pl.when(step < shared_steps)
     def _():
-        for item in range(items):
-            rows = pl.ds(item * PATCHES, PATCHES)
+        for block in range(n2_ref.shape[0] // BWD_ROWS):
+            rows = pl.ds(block * BWD_ROWS, BWD_ROWS)
             inner = (dot_nt(gs[rows, :], dn_ref[...]) * dg_ref[0, rows, :].astype(f32)).astype(bf16)
             din[rows, :] = inner
             acc[rows, :] += dot_nn(inner, up_ref[...])
@@ -860,22 +869,19 @@
                 gs[rows, :] = grad
                 gst[:, rows] = grad.T
 
-        for item in range(items):
-            rows = pl.ds(item * PATCHES, PATCHES)
+        for block in range(n2_ref.shape[0] // BWD_ROWS):
+            rows = pl.ds(block * BWD_ROWS, BWD_ROWS)
             inner = (dot_nn(gs[rows, :], ex_ref[0, 1]) * dg_ref[0, rows, :].astype(f32)).astype(bf16)
             din[rows, :] = inner
-            part = dot_nt(inner, ex_ref[0, 0])
-
-            @pl.when(half == 0)
-            def _():
-                racc[rows, :] = part
-
-            @pl.when(half > 0)
-            def _():
-                acc[rows, :] += (racc[rows, :] + part).astype(bf16).astype(f32)
+            racc[rows, :] += dot_nt(inner, ex_ref[0, 0])
 
         dex_ref[0, 0] = dot_nn(n2t[...], din[...]).astype(bf16)
         dex_ref[0, 1] = dot_nn(gst[...], act_ref[0]).astype(bf16)
+
+        @pl.when(half == halves - 1)
+        def _():
+            acc[...] += racc[...].astype(bf16).astype(f32)
+            racc[...] = jnp.zeros_like(racc)
 
     @pl.when(step == pl.num_programs(0) - 1)
     def _():
@@ -925,34 +931,48 @@
     return jax.ShapeDtypeStruct(shape, kind)
 
 
-def cond_forward(feat, hot, stem_t, lin_a, lin_b):
-    ada = pl.BlockSpec((6 * D, D), lambda: (0, 0))
+ADA_STEPS = 6 * D // CHUNK
+ADA_AT = 4 * D // CHUNK
+
+
+def cond_forward(feat, hot, stem_t, lin):
     shapes = [(8, D)] * 4 + [(LAYERS, 8, 6 * D), (8, 2 * D)]
-    ada_at = [lax.slice_in_dim(lin, 4 * D, 10 * D, axis=0) for lin in (lin_a, lin_b)]
-    del ada
     return pl.pallas_call(
         cond_kernel,
+        grid=(ADA_STEPS,),
+        in_specs=[
+            whole(feat.shape),
+            whole(hot.shape),
+            whole(stem_t.shape),
+            pl.BlockSpec((LAYERS, CHUNK, D), lambda step: (0, ADA_AT + step, 0)),
+        ],
+        out_specs=[whole((8, D))] * 4 + [pl.BlockSpec((LAYERS, 8, CHUNK), lambda step: (0, 0, step)), whole((8, 2 * D))],
         out_shape=[shape_of(shape, f32) for shape in shapes],
-        compiler_params=params(40),
+        compiler_params=params(60),
         name="cond_forward",
-    )(feat, hot, stem_t, *ada_at), ada_at
-
-
-def cond_backward(gm_a, gm_b, gfm, pre_one, pre_two, stem_t, ada_at):
+    )(feat, hot, stem_t, lin)
+
+
+def cond_backward(gm_a, gm_b, gfm, pre_one, pre_two, stem_t, lin):
+    columns = pl.BlockSpec((8, CHUNK), lambda step: (0, step))
     return pl.pallas_call(
         cond_back_kernel,
+        grid=(ADA_STEPS,),
+        in_specs=[columns, columns, whole(gfm.shape), whole((8, D)), whole((8, D)), whole(stem_t.shape)]
+        + [pl.BlockSpec((LAYERS, CHUNK, D), lambda step: (0, ADA_AT + step, 0))],
+        out_specs=[whole((8, D))] * 2,
         out_shape=[shape_of((8, D), f32)] * 2,
-        compiler_params=params(40),
+        compiler_params=params(60),
         name="cond_backward",
-    )(gm_a, gm_b, gfm, pre_one, pre_two, stem_t, *ada_at)
-
-
-def attn_forward(tokens, mods, lin):
+    )(gm_a, gm_b, gfm, pre_one, pre_two, stem_t, lin)
+
+
+def attn_forward(layer, tokens, mods, lin):
     count = tokens.shape[0]
     return pl.pallas_call(
         attn_fwd_kernel,
         grid=(count // PATCHES,),
-        in_specs=[rows_of(D), whole(mods.shape), whole((4 * D, D))],
+        in_specs=[rows_of(D), whole(mods.shape), attn_weights(layer)],
         out_specs=[rows_of(D), rows_of(3 * D), rows_of(D), rows_of(D), rows_of(D), rows_of(D)],
         out_shape=[
             shape_of((count, D), bf16),
@@ -962,67 +982,75 @@
             shape_of((count, D), f32),
             shape_of((count, D), bf16),
         ],
-        compiler_params=params(40),
+        compiler_params=params(60),
         cost_estimate=cost(count * D * 4 * D * 9, 16 * count * D),
         name="attention_forward",
     )(tokens, mods, lin)
 
 
-def attn_backward(gn2, grad, middle, tokens, normed, qkv, attended, branch, mods, grad_gate, lin, out_rows):
+def attn_weights(layer):
+    return pl.BlockSpec((None, 4 * D, D), lambda step: (layer, 0, 0))
+
+
+def attn_backward(layer, gn2, grad, middle, tokens, normed, qkv, attended, branch, mods, grad_gate, lin, out_rows):
     count = tokens.shape[0]
     return pl.pallas_call(
         attn_bwd_kernel,
         grid=(count // PATCHES,),
         in_specs=[rows_of(D)] * 5
-        + [rows_of(3 * D), rows_of(D), rows_of(D), whole(mods.shape), whole(grad_gate.shape), whole((4 * D, D))],
+        + [rows_of(3 * D), rows_of(D), rows_of(D), whole(mods.shape), whole(grad_gate.shape), attn_weights(layer)],
         out_specs=[rows_of(D), whole((8, 6 * D)), whole((out_rows, D))],
         out_shape=[shape_of((count, D), f32), shape_of((8, 6 * D), f32), shape_of((out_rows, D), bf16)],
         scratch_shapes=[pltpu.VMEM((PATCHES, 3 * D), bf16), pltpu.VMEM((4 * D, D), f32)],
-        compiler_params=params(50),
+        compiler_params=params(60),
         cost_estimate=cost(count * D * 4 * D * 22, 16 * count * D),
         name="attention_backward",
     )(gn2, grad, middle, tokens, normed, qkv, attended, branch, mods, grad_gate, lin)
 
 
-def weight_specs(shared_steps, lin_rows):
+def weight_specs(layer, shared_steps, lin_rows):
     up_at = lin_rows // CHUNK - shared_steps
     return [
-        pl.BlockSpec((CHUNK, D), lambda step: (up_at + jnp.minimum(step, shared_steps - 1), 0)),
+        pl.BlockSpec((None, CHUNK, D), lambda step: (layer, up_at + jnp.minimum(step, shared_steps - 1), 0)),
         pl.BlockSpec((CHUNK, D), lambda step: (jnp.minimum(step, shared_steps - 1), 0)),
         pl.BlockSpec((1, 2, D, CHUNK), lambda step: (jnp.maximum(step - shared_steps, 0), 0, 0, 0)),
     ]
 
 
-def ffn_forward(n2, middle, mods, g4, lin, lout, experts_w, halves):
+def ffn_forward(layer, n2, middle, mods, g4, lin, lout, experts_w, halves, beside=()):
     count = n2.shape[0]
     shared_steps = lout.shape[0] // CHUNK
     steps = shared_steps + experts_w.shape[0]
     wide = pl.BlockSpec((1, count, CHUNK), lambda step: (step, 0, 0))
+    anywhere = [pl.BlockSpec(memory_space=pl.ANY)] * len(beside)
+    remote = pltpu.CompilerParams(vmem_limit_bytes=60 * MIB, collective_id=7, has_side_effects=True)
     return pl.pallas_call(
-        functools.partial(ffn_fwd_kernel, shared_steps, halves),
+        functools.partial(ffn_fwd_kernel, shared_steps, halves, len(beside)),
         grid=(steps,),
         in_specs=[whole(n2.shape), whole(middle.shape), whole(mods.shape), whole(g4.shape)]
-        + weight_specs(shared_steps, lin.shape[0]),
-        out_specs=[wide, wide, whole((count, D)), whole((count, D))],
+        + weight_specs(layer, shared_steps, lin.shape[1])
+        + anywhere,
+        out_specs=[wide, wide, whole((count, D)), whole((count, D))] + anywhere,
         out_shape=[
             shape_of((steps, count, CHUNK), bf16),
             shape_of((steps, count, CHUNK), bf16),
             shape_of((count, D), f32),
             shape_of((count, D), f32),
-        ],
-        scratch_shapes=[pltpu.VMEM((count, D), f32)] * 2,
-        compiler_params=params(56),
+        ]
+        + [shape_of((8,) + part.shape, bf16) for part in beside],
+        scratch_shapes=[pltpu.VMEM((count, D), f32)] * 2 + (gather_semaphores(4) if beside else []),
+        compiler_params=remote if beside else params(60),
         cost_estimate=cost(4 * steps * count * D * CHUNK * 2, 8 * steps * count * CHUNK),
         name="ffn_forward",
-    )(n2, middle, mods, g4, lin, lout, experts_w)
-
-
-def ffn_backward(grad, n2, mods, g4, mixed, active, slope, lin, lout, experts_w, halves):
+    )(n2, middle, mods, g4, lin, lout, experts_w, *beside)
+
+
+def ffn_backward(layer, grad, n2, mods, g4, mixed, active, slope, lin, lout, experts_w, halves):
     count = n2.shape[0]
     shared_steps = lout.shape[0] // CHUNK
     steps = shared_steps + experts_w.shape[0]
     wide = pl.BlockSpec((1, count, CHUNK), lambda step: (step, 0, 0))
-    specs = weight_specs(shared_steps, lin.shape[0])
+    specs = weight_specs(layer, shared_steps, lin.shape[1])
     return pl.pallas_call(
         functools.partial(ffn_bwd_kernel, shared_steps, halves),
         grid=(steps,),
@@ -1069,9 +1097,42 @@
             shape_of((PATCH_DIM, D), f32),
             shape_of((PATCH_DIM, 1), f32),
         ],
-        compiler_params=params(40),
+        compiler_params=params(60),
         name="final_step",
     )(tokens, mods, fo_rows, target_t)
+
+
+def update_kernel(groups, grad_a, grad_b, total_a, total_b, w_ref, f_ref, s_ref, m_ref, new_ref, half_ref, fn_ref, sn_ref, mn_ref):
+    for layer, (grad_ref, total_ref) in enumerate(((grad_a, total_a), (grad_b, total_b))):
+
+        @pl.when(pl.program_id(0) == layer)
+        def _(grad_ref=grad_ref, total_ref=total_ref):
+            gradient = grad_ref[...]
+            fn_ref[0] = beta_one * f_ref[0] + (1.0 - beta_one) * gradient
+            sn_ref[0] = beta_two * s_ref[0] + (1.0 - beta_two) * gradient * gradient
+            mean_delta = total_ref[...] / groups
+            moment_new = outer_mom * m_ref[0] + mean_delta
+            weight = w_ref[0] - outer_rate * (mean_delta + outer_mom * moment_new)
+            mn_ref[0] = moment_new
+            new_ref[0] = weight
+            half_ref[0] = weight.astype(bf16)
+
+
+def update_arrays(tile, grads, totals, weight, first, second, moment):
+    layers, rows, width = weight.shape
+    tiles = rows // tile
+    state = pl.BlockSpec((1, tile, width), lambda layer, step: (layer, step, 0))
+    early = pl.BlockSpec((tile, width), lambda layer, step: (jnp.where(layer == 0, step, tiles - 1), 0))
+    late = pl.BlockSpec((tile, width), lambda layer, step: (jnp.where(layer == 0, 0, step), 0))
+    return pl.pallas_call(
+        functools.partial(update_kernel, lax.axis_size(GROUP)),
+        grid=(layers, tiles),
+        in_specs=[early, late, early, late] + [state] * 4,
+        out_specs=[state] * 5,
+        out_shape=[shape_of(weight.shape, kind) for kind in (f32, bf16, f32, f32, f32)],
+        compiler_params=params(60),
+        name="update_arrays",
+    )(*grads, *totals, weight, first, second, moment)
 
 
 def pad_rows(values):
@@ -1083,6 +1144,7 @@
     for size, padded in zip(STEM_SIZES, STEM_PADDED):
         pieces.append(jnp.pad(stem_t[:, at : at + size], ((0, 0), (0, padded - size))))
         at = at + size
+    pieces.append(jnp.zeros((stem_t.shape[0], STEM_LANES - sum(STEM_PADDED)), stem_t.dtype))
     return jnp.concatenate(pieces, axis=1)
 
 
@@ -1091,8 +1153,8 @@
 
 
 def plane_partners():
-    group = lax.axis_index("group")
-    return {"group": group + 1 - 2 * lax.rem(group, 2)}, {"group": lax.rem(group + 2, 4)}
+    group = lax.axis_index(GROUP)
+    return {GROUP: group + 1 - 2 * lax.rem(group, 2)}, {GROUP: lax.rem(group + 2, 4)}
 
 
 def greet(partners, line_at, line_size):
@@ -1102,11 +1164,11 @@
 
     @pl.when(line_at > 0)
     def _():
-        pl.semaphore_signal(barrier, inc=1, device_id={"expert": line_at - 1}, device_id_type=MESH_ID)
+        pl.semaphore_signal(barrier, inc=1, device_id={LINE: line_at - 1}, device_id_type=MESH_ID)
 
     @pl.when(line_at < line_size - 1)
     def _():
-        pl.semaphore_signal(barrier, inc=1, device_id={"expert": line_at + 1}, device_id_type=MESH_ID)
+        pl.semaphore_signal(barrier, inc=1, device_id={LINE: line_at + 1}, device_id_type=MESH_ID)
 
     ends = jnp.where(line_at == 0, 1, 0) + jnp.where(line_at == line_size - 1, 1, 0)
     pl.semaphore_wait(barrier, len(partners) + 2 - ends)
@@ -1136,18 +1198,21 @@
 
 
 def reduce_kernel(
-    layer, dex, dqkvo, dup, ddn, extra, ex_w, ex_f, ex_s, li_w, li_f, li_s, lo_w, lo_f, lo_s,
-    g_ex, g_li, g_lo, m_ex, m_li, m_lo, *scratch,
+    layer, with_stem, dex, dqkvo, dup, ddn, extra, ex_w, ex_f, ex_s, li_w, li_f, li_s, lo_w, lo_f, lo_s, *rest
 ):
+    if with_stem:
+        stem_in, *rest, stem_sem, stem_send, stem_recv, stem_a, stem_b, stem_c, stem_d = rest
+        stem_out = rest.pop(6)
+    g_ex, g_li, g_lo, m_ex, m_li, m_lo, *scratch = rest
     units = reduce_units()
     number = len(units)
     banks = [scratch[at * number : (at + 1) * number] for at in range(9)]
     chip, local, came, delta, swapped, swapped_two, weight, first, second = banks
     extra_buf = scratch[9 * number]
     core_send, core_recv, line_send, line_recv, load_sem, plane_send, plane_recv, out_sem = scratch[9 * number + 1 :]
-    at = lax.axis_index("expert")
-    core = lax.axis_index("dp")
-    sibling = {"dp": 1 - core}
+    at = lax.axis_index(LINE)
+    core = lax.axis_index(CORE)
+    sibling = {CORE: 1 - core}
     side_x, side_y = plane_partners()
     greet([sibling, side_x, side_y], at, 4)
 
@@ -1165,6 +1230,39 @@
 
     def dest(bank, unit, where):
         return bank[unit].at[pl.ds(0, 4)] if isinstance(where, slice) else bank[unit].at[where]
+
+    if with_stem:
+        load = pltpu.make_async_copy(stem_in, stem_a, stem_sem.at[0])
+        load.start()
+        load.wait()
+
+    def stem_copies(second_step):
+        landing, sides = ((stem_b, (side_x, side_y)), (stem_c, (side_y, side_x)))[second_step]
+        return [
+            pltpu.make_async_remote_copy(
+                stem_a.at[pl.ds(begin, size)], landing.at[pl.ds(begin, size)], stem_send.at[2 * second_step + half],
+                stem_recv.at[2 * second_step + half], device_id=sides[half], device_id_type=MESH_ID,
+            )
+            for half, (begin, size) in enumerate(((0, 16), (16, 32)))
+        ]
+
+    def stem_turn(turn):
+        if not with_stem or turn > 2:
+            return
+        if turn == 0:
+            for copy in stem_copies(0):
+                copy.start()
+        elif turn == 1:
+            for copy in stem_copies(0):
+                copy.wait()
+            stem_a[...] = (stem_a[...].astype(f32) + stem_b[...].astype(f32)).astype(bf16)
+            for copy in stem_copies(1):
+                copy.start()
+        else:
+            for copy in stem_copies(1):
+                copy.wait()
+            stem_d[...] = stem_a[...].astype(f32) + stem_c[...].astype(f32)
+            pltpu.make_async_copy(stem_d, stem_out, stem_sem.at[1]).start()
 
     given, loads = [], []
     for unit in range(number):
@@ -1201,7 +1299,7 @@
         slot = 4 if step == -1 and owner == place - 1 else owner
         return pltpu.make_async_remote_copy(
             chip[unit].at[owner], came[unit].at[slot], line_send.at[unit, owner], line_recv.at[unit, slot],
-            device_id={"expert": at + step}, device_id_type=MESH_ID,
+            device_id={LINE: at + step}, device_id_type=MESH_ID,
         )
 
     def arrived(unit, slot):
@@ -1340,10 +1438,13 @@
         out_copy(unit, 1).start()
 
     for turn in range(number + 3):
+        stem_turn(turn)
         for lag, action in enumerate((forward, finish, exchange, close)):
             if 0 <= turn - lag < number:
                 action(turn - lag)
 
+    if with_stem:
+        pltpu.make_async_copy(stem_d, stem_out, stem_sem.at[1]).wait()
     for unit in range(number):
         for copy in given[unit]:
             copy.wait_send()
@@ -1360,7 +1461,7 @@
                         line_copy(unit, owner, step, place).wait_send()
 
 
-def reduce_layer(layer, dex, dqkvo, dup, ddn, extra, states):
+def reduce_layer(layer, dex, dqkvo, dup, ddn, extra, states, stem_delta=None):
     units = reduce_units()
     scratch = []
     for lead, kind in (((4,), bf16), ((4,), bf16), ((5,), bf16), ((), bf16), ((), bf16), ((), bf16), ((), f32), ((), f32), ((), f32)):
@@ -1372,31 +1473,326 @@
     scratch += [dma((number, 4)), dma((number, 4)), dma((number, 2))]
     anywhere = pl.BlockSpec(memory_space=pl.ANY)
     shapes = [(2, D, CHUNK), extra.shape, (D, D)] * 2
+    stems = [] if stem_delta is None else [stem_delta]
+    for delta in stems:
+        shapes.append(delta.shape)
+        scratch += [dma((2,)), dma((4,)), dma((4,))] + [pltpu.VMEM(delta.shape, bf16)] * 3
+        scratch.append(pltpu.VMEM(delta.shape, f32))
     return pl.pallas_call(
-        functools.partial(reduce_kernel, layer),
+        functools.partial(reduce_kernel, layer, bool(stems)),
         out_shape=[shape_of(shape, f32) for shape in shapes],
-        in_specs=[anywhere] * (5 + len(states)),
-        out_specs=[anywhere] * 6,
+        in_specs=[anywhere] * (5 + len(states) + len(stems)),
+        out_specs=[anywhere] * len(shapes),
         scratch_shapes=scratch,
         compiler_params=pltpu.CompilerParams(
             vmem_limit_bytes=62 * MIB, collective_id=1 + layer, has_side_effects=True
         ),
         name="reduce_layer",
-    )(dex, dqkvo, dup, ddn, extra, *states)
-
-
-def plane_sum(delta):
-    middle = delta.shape[0] // 2
-    swaps = [[(i, i ^ bit) for i in range(4)] for bit in (1, 2)]
-    totals = []
-    for half, order in ((delta[:middle], (0, 1)), (delta[middle:], (1, 0))):
-        for axis in order:
-            half = to_half(half.astype(f32) + lax.ppermute(half, "group", swaps[axis]).astype(f32))
-        totals.append(half.astype(f32))
-    return jnp.concatenate(totals, axis=0)
-
-
-SHARD = ("expert", "dp")
+    )(dex, dqkvo, dup, ddn, extra, *states, *stems)
+
+
+def shard_part(kind, ref, quarter, half=None):
+    if kind == "stem":
+        begin, size = quarter * (STEM_LANES // 4), STEM_LANES // 4
+        if half is not None:
+            begin, size = begin + half * (size // 2), size // 2
+        return ref.at[:, pl.ds(pl.multiple_of(begin, 128), size)]
+    if kind == "lin":
+        begin, size = lax.rem(quarter, 2) * 432, 432
+        if half is not None:
+            begin, size = begin + half * 208, (208, 224)[half]
+        return ref.at[quarter // 2, pl.ds(pl.multiple_of(begin, 16), size)]
+    begin, size = quarter * (D // 4), D // 4
+    if half is not None:
+        begin, size = begin + half * (size // 2), size // 2
+    return ref.at[pl.ds(pl.multiple_of(begin, 16), size)]
+
+
+class WeightGather:
+    def __init__(self, kinds, sources, targets, sends, recvs, cores_send, cores_recv, own_sem):
+        self.kinds, self.sources, self.targets = kinds, sources, targets
+        self.sends, self.recvs = sends, recvs
+        self.cores_send, self.cores_recv, self.own_sem = cores_send, cores_recv, own_sem
+        self.at, self.core, self.group = lax.axis_index(LINE), lax.axis_index(CORE), lax.axis_index(GROUP)
+        self.sibling = {CORE: 1 - self.core}
+        self.side_x, self.side_y = plane_partners()
+        self.group_x = self.group + 1 - 2 * lax.rem(self.group, 2)
+        self.group_y = lax.rem(self.group + 2, 4)
+        near = jnp.where(self.at == 3, 3, 1)
+        far = jnp.where(self.at == 0, 3, jnp.where(self.at == 3, 1, 2))
+        self.order = (near, 6 - near - far, far)
+
+    def enter(self):
+        greet([self.sibling, self.side_x, self.side_y], self.at, 4)
+
+    def whole_part(self, unit, owner, core):
+        target = self.targets[unit]
+        if self.kinds[unit] == "lin":
+            return target.at[:, owner * 2 + core]
+        return target.at[owner * 2 + core]
+
+    def copy(self, unit, source, target, slot, kind, device):
+        return pltpu.make_async_remote_copy(
+            source, target, self.sends.at[unit, slot, kind], self.recvs.at[unit, slot, kind],
+            device_id=device, device_id_type=MESH_ID,
+        )
+
+    def line_copy(self, unit, owner, to_slot, send_slot, step, own):
+        target = shard_part(self.kinds[unit], self.whole_part(unit, owner, self.core), self.group)
+        source = shard_part(self.kinds[unit], self.sources[unit], self.group) if own else target
+        return pltpu.make_async_remote_copy(
+            source, target, self.sends.at[unit, send_slot, 0], self.recvs.at[unit, to_slot - 1, 0],
+            device_id={LINE: self.at + step}, device_id_type=MESH_ID,
+        )
+
+    def owner_of(self, slot):
+        return lax.rem(self.at + slot, 4)
+
+    def part(self, unit, slot, quarter, half=None):
+        return shard_part(self.kinds[unit], self.whole_part(unit, self.owner_of(slot), self.core), quarter, half)
+
+    def core_copy(self, unit, slot, own=False):
+        source = self.sources[unit] if own else self.whole_part(unit, self.owner_of(slot), self.core)
+        return pltpu.make_async_remote_copy(
+            source, self.whole_part(unit, self.owner_of(slot), self.core),
+            self.cores_send.at[unit, slot], self.cores_recv.at[unit, slot],
+            device_id=self.sibling, device_id_type=MESH_ID,
+        )
+
+    def own_copy(self, unit):
+        return pltpu.make_async_copy(
+            self.sources[unit], self.whole_part(unit, self.at, self.core), self.own_sem.at[unit]
+        )
+
+    def own_line(self, unit, act):
+        for step, slot, send_slot, there in ((1, 3, 3, self.at < 3), (-1, 1, 4, self.at > 0)):
+
+            @pl.when(there)
+            def _(step=step, slot=slot, send_slot=send_slot):
+                act(self.line_copy(unit, self.at, slot, send_slot, step, True))
+
+    def begin(self, unit):
+        self.own_line(unit, lambda copy: copy.start())
+        self.core_copy(unit, 0, True).start()
+        self.own_copy(unit).start()
+
+    def forwards(self, unit, slot, act):
+        left = self.at + slot >= 4
+        for step, to_slot, there in ((1, slot - 1, left & (self.at < 3)), (-1, slot + 1, (self.at + slot < 4) & (self.at > 0))):
+
+            @pl.when(there)
+            def _(step=step, to_slot=to_slot):
+                act(self.line_copy(unit, self.owner_of(slot), to_slot, slot - 1, step, False))
+
+    def plane_copies(self, unit, slot):
+        mine = self.part(unit, slot, self.group)
+        return [self.copy(unit, mine, mine, slot - 1, 1, self.side_x), self.copy(unit, mine, mine, slot - 1, 2, self.side_y)]
+
+    def plane_arrivals(self, unit, slot):
+        parts = [self.part(unit, slot, self.group_x), self.part(unit, slot, self.group_y)]
+        return [self.copy(unit, parts[0], parts[0], slot - 1, 1, self.side_x), self.copy(unit, parts[1], parts[1], slot - 1, 2, self.side_y)]
+
+    def corner_copies(self, unit, slot):
+        parts = [self.part(unit, slot, self.group_x, 0), self.part(unit, slot, self.group_y, 1)]
+        return [self.copy(unit, parts[0], parts[0], slot - 1, 3, self.side_y), self.copy(unit, parts[1], parts[1], slot - 1, 4, self.side_x)]
+
+    def corner_arrivals(self, unit, slot):
+        corner = 3 - self.group
+        parts = [self.part(unit, slot, corner, 0), self.part(unit, slot, corner, 1)]
+        return [self.copy(unit, parts[0], parts[0], slot - 1, 3, self.side_y), self.copy(unit, parts[1], parts[1], slot - 1, 4, self.side_x)]
+
+    def along_line(self, unit):
+        for slot in self.order:
+            mine = self.part(unit, slot, self.group)
+            self.copy(unit, mine, mine, slot - 1, 0, self.sibling).wait_recv()
+            self.forwards(unit, slot, lambda copy: copy.start())
+            for copy in self.plane_copies(unit, slot):
+                copy.start()
+
+    def in_plane(self, unit):
+        for slot in self.order:
+            for copy in self.plane_arrivals(unit, slot):
+                copy.wait_recv()
+            for copy in self.corner_copies(unit, slot):
+                copy.start()
+
+    def to_sibling(self, unit):
+        for slot in self.order:
+            for copy in self.corner_arrivals(unit, slot):
+                copy.wait_recv()
+            self.core_copy(unit, slot).start()
+
+    def end(self, unit):
+        self.own_copy(unit).wait()
+        self.own_line(unit, lambda copy: copy.wait_send())
+        for slot in range(4):
+            self.core_copy(unit, slot, slot == 0).wait_send()
+            other = self.whole_part(unit, self.owner_of(slot), 1 - self.core)
+            pltpu.make_async_remote_copy(
+                other, other, self.cores_send.at[unit, slot], self.cores_recv.at[unit, slot],
+                device_id=self.sibling, device_id_type=MESH_ID,
+            ).wait_recv()
+        for slot in (1, 2, 3):
+            self.forwards(unit, slot, lambda copy: copy.wait_send())
+            for copy in self.plane_copies(unit, slot) + self.corner_copies(unit, slot):
+                copy.wait_send()
+
+
+def gather_semaphores(number):
+    dma = pltpu.SemaphoreType.DMA
+    return [dma((number, 5, 5)), dma((number, 3, 5)), dma((number, 4)), dma((number, 4)), dma((number,))]
+
+
+def gather_kernel(kinds, split, *refs):
+    count = len(split)
+    arrays_in, arrays_out, sems = refs[:count], refs[count : 2 * count], refs[2 * count :]
+    sources, targets = [], []
+    for given, target, parts in zip(arrays_in, arrays_out, split):
+        for part in parts:
+            sources.append(given if part is None else given.at[part])
+            targets.append(target if part is None else target.at[(slice(None),) + part])
+    work = WeightGather(kinds, sources, targets, *sems)
+    work.enter()
+    number = len(kinds)
+    work.begin(0)
+    work.begin(1)
+    for turn in range(number + 2):
+        for lag, action in enumerate((work.along_line, work.in_plane, work.to_sibling)):
+            if 0 <= turn - lag < number:
+                action(turn - lag)
+            if lag == 0 and turn + 2 < number:
+                work.begin(turn + 2)
+    for unit in range(number):
+        work.end(unit)
+
+
+def gather_beside(step, last, given, taken, sems):
+    parts = [(matrix, slice(None), pl.ds(begin, D)) for matrix in range(2) for begin in (0, D)]
+    sources = [given[0].at[part] for part in parts]
+    targets = [taken[0].at[(slice(None),) + part] for part in parts]
+    work = WeightGather(["rows"] * 4, sources, targets, *sems)
+    line, plane, pair = work.along_line, work.in_plane, work.to_sibling
+    schedule = {
+        0: [(work.begin, 0), (work.begin, 1)],
+        2: [(line, 0), (work.begin, 2)],
+        4: [(line, 1), (plane, 0), (work.begin, 3)],
+        6: [(line, 2), (plane, 1), (pair, 0)],
+        8: [(line, 3), (plane, 2), (pair, 1)],
+        10: [(plane, 3), (pair, 2)],
+        11: [(pair, 3)] + [(work.end, unit) for unit in range(4)],
+    }
+    for when, actions in schedule.items():
+
+        @pl.when(step == (last if when == 11 else when))
+        def _(when=when, actions=actions):
+            if when == 0:
+                work.enter()
+            for action, unit in actions:
+                action(unit)
+
+
+def gather_weights(stem, lin, louts, experts_in):
+    lanes = [pl.ds(begin, 128) for begin in range(0, D, 128)]
+    every = slice(None)
+    arrays = [stem, lin] + list(louts) + list(experts_in)
+    kinds = ["stem"] + ["lin"] * len(lanes) + ["rows"] * (len(louts) + 4 * len(experts_in))
+    split = [[None], [(every, every, part) for part in lanes]] + [[None]] * len(louts)
+    split += [[(matrix, every, pl.ds(begin, D)) for matrix in range(2) for begin in (0, D)]] * len(experts_in)
+    shapes = [(8,) + stem.shape, (lin.shape[0], 8) + lin.shape[1:]]
+    shapes += [(8,) + part.shape for part in arrays[2:]]
+    anywhere = pl.BlockSpec(memory_space=pl.ANY)
+    return pl.pallas_call(
+        functools.partial(gather_kernel, kinds, split),
+        out_shape=[shape_of(shape, bf16) for shape in shapes],
+        in_specs=[anywhere] * len(arrays),
+        out_specs=[anywhere] * len(arrays),
+        scratch_shapes=gather_semaphores(len(kinds)),
+        compiler_params=pltpu.CompilerParams(collective_id=5, has_side_effects=True),
+        name="gather_weights",
+    )(*arrays)
+
+
+def exchange_kernel(packed, loss, all_packed, total, from_x, from_y, losses, held, send, recv, core_send, core_recv, plane_send, plane_recv, own_sem):
+    at, core = lax.axis_index(LINE), lax.axis_index(CORE)
+    side_x, side_y = plane_partners()
+    sibling = {CORE: 1 - core}
+    barrier = pltpu.get_barrier_semaphore()
+    others = [{LINE: lax.rem(at + step, 4)} for step in (1, 2, 3)]
+    for partner in others + [sibling, side_x, side_y]:
+        pl.semaphore_signal(barrier, inc=1, device_id=partner, device_id_type=MESH_ID)
+    pl.semaphore_wait(barrier, 6)
+
+    def slots(owner, which):
+        return all_packed.at[owner * 2 + which], losses.at[owner * 2 + which]
+
+    own = [pltpu.make_async_copy(source, target, own_sem.at[place]) for place, (source, target) in enumerate(zip((packed, loss), slots(at, core)))]
+    for copy in own:
+        copy.start()
+
+    def line(step, place):
+        source, target = ((packed, loss)[place], slots(at, core)[place])
+        return pltpu.make_async_remote_copy(
+            source, target, send.at[step - 1, place], recv.at[step - 1, place],
+            device_id=others[step - 1], device_id_type=MESH_ID,
+        )
+
+    def across(step, place):
+        owner = lax.rem(at + 4 - step, 4)
+        source = (packed, loss)[place] if step == 0 else slots(owner, core)[place]
+        return pltpu.make_async_remote_copy(
+            source, slots(owner, core)[place], core_send.at[step, place], core_recv.at[step, place],
+            device_id=sibling, device_id_type=MESH_ID,
+        )
+
+    def arrival(step, place, which, sem):
+        here = slots(lax.rem(at + 4 - step, 4), which)[place]
+        return pltpu.make_async_remote_copy(
+            here, here, core_send.at[step, place], sem, device_id=sibling, device_id_type=MESH_ID
+        )
+
+    for place in (1, 0):
+        for step in (2, 3, 1):
+            line(step, place).start()
+        across(0, place).start()
+    for place in (1, 0):
+        for step in (1, 3, 2):
+            arrival(step, place, core, recv.at[step - 1, place]).wait_recv()
+            across(step, place).start()
+        for step in range(4):
+            arrival(step, place, 1 - core, core_recv.at[step, place]).wait_recv()
+        if place == 1:
+            own[1].wait()
+            held[...] = jnp.sum(losses[...], axis=0)
+            first = pltpu.make_async_remote_copy(held, from_x, plane_send.at[0], plane_recv.at[0], device_id=side_x, device_id_type=MESH_ID)
+            first.start()
+    first.wait()
+    held[...] += from_x[...]
+    second = pltpu.make_async_remote_copy(held, from_y, plane_send.at[1], plane_recv.at[1], device_id=side_y, device_id_type=MESH_ID)
+    second.start()
+    second.wait()
+    total[...] = held[...] + from_y[...]
+    own[0].wait()
+    for place in range(2):
+        for step in (1, 2, 3):
+            line(step, place).wait_send()
+        for step in range(4):
+            across(step, place).wait_send()
+
+
+def exchange_small(packed, loss):
+    dma = pltpu.SemaphoreType.DMA
+    vmem = pl.BlockSpec(memory_space=pltpu.VMEM)
+    return pl.pallas_call(
+        exchange_kernel,
+        out_shape=[shape_of((8,) + packed.shape, packed.dtype), shape_of(loss.shape, f32)],
+        in_specs=[vmem, vmem],
+        out_specs=[vmem, vmem],
+        scratch_shapes=[pltpu.VMEM(loss.shape, f32)] * 2
+        + [pltpu.VMEM((8,) + loss.shape, f32), pltpu.VMEM(loss.shape, f32)]
+        + [dma((3, 2)), dma((3, 2)), dma((4, 2)), dma((4, 2)), dma((2,)), dma((2,)), dma((2,))],
+        compiler_params=pltpu.CompilerParams(collective_id=6, has_side_effects=True, vmem_limit_bytes=16 * MIB),
+        name="exchange_small",
+    )(packed, loss)
 
 
 def few_experts(
@@ -1425,26 +1821,25 @@
 ):
     count = patches.shape[0]
     items = timesteps.shape[0]
-    halves = lax.axis_size("dp")
-    sharers = lax.axis_size("expert") * halves
-    expert_count = lax.axis_size("expert") * experts.shape[1]
-    place = lax.axis_index("expert") * halves + lax.axis_index("dp")
+    halves = lax.axis_size(CORE)
+    sharers = lax.axis_size(LINE) * halves
+    expert_count = lax.axis_size(LINE) * experts.shape[1]
+    place = lax.axis_index(LINE) * halves + lax.axis_index(CORE)
 
     stem_t = stem_weights.T
     lin_t = jnp.swapaxes(layer_in, 1, 2)
-    stem_all = lax.all_gather(stem_lanes(to_half(stem_t)), SHARD, axis=0, tiled=True)
-    lin_all, lout_all, expert_all = [], [], []
-    for layer in range(LAYERS):
-        lin_all.append(lax.all_gather(to_half(lin_t[layer]), SHARD, axis=0, tiled=True))
-        lout_all.append(lax.all_gather(to_half(layer_out[layer]), SHARD, axis=0, tiled=True))
-        expert_all.append(lax.all_gather(to_half(experts[layer]), SHARD, axis=0, tiled=True))
+    louts = [to_half(layer_out[layer]) for layer in range(LAYERS)]
+    pairs = [to_half(experts[layer, 0]) for layer in range(LAYERS)]
+    gathered = gather_weights(stem_lanes(to_half(stem_t)), to_half(lin_t), louts, pairs[:1])
+    stem_all = gathered[0].reshape(D, STEM_LANES)
+    lin_all = gathered[1].reshape(LAYERS, -1, D)
+    lout_all = [gathered[2 + layer].reshape(-1, D) for layer in range(LAYERS)]
+    expert_all = [gathered[2 + LAYERS]]
 
     feat = time_features(timesteps)
     hot = label_table(labels)
     hot_pad = jnp.pad(hot, ((0, 32 - items), (0, STEM_PADDED[3] - hot.shape[1]))).astype(bf16)
-    (cond, hidden, pre_one, pre_two, mods, fin_mods), ada_at = cond_forward(
-        pad_rows(feat), hot_pad, stem_all, lin_all[0], lin_all[1]
-    )
+    cond, hidden, pre_one, pre_two, mods, fin_mods = cond_forward(pad_rows(feat), hot_pad, stem_all, lin_all)
     tokens = product_nt(patches, stem_all[:, :PATCH_DIM])
     tokens = (tokens.reshape(items, -1, D) + positions_table()[None]).reshape(-1, D)
     expert_ids = jnp.arange(expert_count, dtype=jnp.int32)
@@ -1453,64 +1848,65 @@
         g4 = jnp.sum(
             jnp.where(routes[layer][:, :, None] == expert_ids, route_gates[layer][:, :, None], 0.0), axis=1
         )
-        normed, qkv, attended, branch, middle, n2 = attn_forward(tokens, mods[layer], lin_all[layer])
-        active, slope, mixed, result = ffn_forward(
-            n2, middle, mods[layer], g4, lin_all[layer], lout_all[layer], expert_all[layer], halves
+        normed, qkv, attended, branch, middle, n2 = attn_forward(layer, tokens, mods[layer], lin_all)
+        beside = (pairs[layer + 1],) if layer + 1 < LAYERS else ()
+        active, slope, mixed, result, *arrived = ffn_forward(
+            layer, n2, middle, mods[layer], g4, lin_all, lout_all[layer], expert_all[layer], halves, beside
         )
+        if beside:
+            expert_all.append(arrived[0])
         saved.append((tokens, g4, normed, qkv, attended, branch, middle, n2, active, slope, mixed))
         tokens = result
     fo_rows = stem_all[:, STEM_AT[5] : STEM_AT[5] + PATCH_DIM].T
     grad, grad_fin, grad_out_w, loss_rows = final_step(tokens, fin_mods, fo_rows, target_noise.T)
-    loss_total = lax.psum(jnp.sum(loss_rows), ("group", "expert", "dp"))
 
     stem_cols = stem_weights.shape[1]
     lin_cols = layer_in.shape[2]
 
     def outer(left_in, right_in):
-        return lax.dot_general(left_in, right_in, (((0,), (0,)), ((), ())), precision=highest)
+        return lax.dot_general(left_in, right_in, (((0,), (0,)), ((), ())), preferred_element_type=f32)
 
     def flip(values):
         return jnp.swapaxes(values, -1, -2)
 
     states = (experts, experts_first, experts_second, lin_t, flip(layer_in_first[0]), flip(layer_in_second[0]))
     states = states + (layer_out, layer_out_first, layer_out_second)
-    grad_mods, reduced = [None] * LAYERS, [None] * LAYERS
+    grad_mods, reduced, outgoing = [None] * LAYERS, [None] * LAYERS, [None] * LAYERS
     for layer in reversed(range(LAYERS)):
         tokens, g4, normed, qkv, attended, branch, middle, n2, active, slope, mixed = saved[layer]
         dup, ddn, dex, gn2, grad_gate = ffn_backward(
-            grad, n2, mods[layer], g4, mixed, active, slope, lin_all[layer], lout_all[layer], expert_all[layer], halves
+            layer, grad, n2, mods[layer], g4, mixed, active, slope, lin_all, lout_all[layer], expert_all[layer], halves
         )
         grad, grad_mods[layer], dqkvo = attn_backward(
-            gn2, grad, middle, tokens, normed, qkv, attended, branch, mods[layer], grad_gate, lin_all[layer],
+            layer, gn2, grad, middle, tokens, normed, qkv, attended, branch, mods[layer], grad_gate, lin_all,
             halves * lin_cols,
         )
-        factors = jnp.concatenate([cond[:items], grad_mods[layer][:items]], axis=1)
-        factors = lax.all_gather(factors, SHARD, axis=0, tiled=True)
-        spread = jnp.pad(factors[:, D:], ((0, 0), (4 * D, lin_cols * sharers - 10 * D)))
-        window = lax.dynamic_slice_in_dim(spread, place * lin_cols, lin_cols, axis=1)
-        reduced[layer] = reduce_layer(
-            layer,
-            dex.reshape((-1, halves) + dex.shape[1:]),
-            dqkvo.reshape(halves, lin_cols, D),
-            dup.reshape(-1, halves, lin_cols, D),
-            ddn.reshape(-1, halves, layer_out.shape[1], D),
-            outer(window, factors[:, :D]),
-            states,
-        )
+        outgoing[layer] = (dex, dqkvo, dup, ddn)
     grad_patch = product_tn(patches, to_half(grad))
-    dpre_one, dpre_two = cond_backward(grad_mods[0], grad_mods[1], grad_fin, pre_one, pre_two, stem_all, ada_at)
-
+    dpre_one, dpre_two = cond_backward(grad_mods[0], grad_mods[1], grad_fin, pre_one, pre_two, stem_all, lin_all)
+
+    names = jnp.stack([labels // 32, labels % 32], axis=1).astype(f32)
     factors = jnp.concatenate(
-        [cond[:items], hidden[:items], dpre_one[:items], dpre_two[:items], grad_fin[:items], feat], axis=1
-    )
+        [cond[:items], grad_mods[0][:items], grad_mods[1][:items], hidden[:items], dpre_one[:items], dpre_two[:items]]
+        + [grad_fin[:items], feat, jnp.pad(names, ((0, 0), (0, 126)))],
+        axis=1,
+    ).astype(bf16)
     width = factors.shape[1]
-    packed = jnp.concatenate([factors.reshape(-1), grad_patch.reshape(-1), grad_out_w.reshape(-1)])
-    gathered = lax.all_gather(packed, SHARD, axis=0, tiled=False)
-    ends = gathered[:, items * width :].reshape(sharers, 2, PATCH_DIM, D).sum(axis=0)
+    ends = jnp.concatenate([grad_patch, grad_out_w], axis=0).astype(bf16)
+    packed = jnp.concatenate([factors.reshape(-1), ends.reshape(-1)])
+    lanes = -(-packed.size // (16 * 128)) * 128
+    packed = jnp.pad(packed, (0, 16 * lanes - packed.size)).reshape(16, lanes)
+    loss = jnp.pad(loss_rows.reshape(1, PATCH_DIM), ((0, 7), (0, 128 - PATCH_DIM)))
+    gathered, loss_all = exchange_small(packed, loss)
+    loss_total = jnp.sum(loss_all)
+    gathered = gathered.reshape(sharers, -1)
     factors = gathered[:, : items * width].reshape(sharers * items, width)
-    hot_all = label_table(lax.all_gather(labels, SHARD, axis=0, tiled=True))
-    cond_f, hidden_f, done_f, dtwo_f, fin_f, feat_f = jnp.split(factors, [D, 2 * D, 3 * D, 4 * D, 6 * D], axis=1)
-
+    ends = gathered[:, items * width : items * width + 2 * PATCH_DIM * D].reshape(sharers, 2, PATCH_DIM, D)
+    ends = jnp.sum(ends.astype(f32), axis=0)
+    cond_f, gm_a, gm_b, hidden_f, done_f, dtwo_f, fin_f, feat_f, names = jnp.split(
+        factors, [D, 7 * D, 13 * D, 14 * D, 15 * D, 16 * D, 18 * D, 18 * D + FREQ], axis=1
+    )
+    hot_all = label_table((names[:, 0].astype(f32) * 32 + names[:, 1].astype(f32)).astype(jnp.int32)).astype(bf16)
     def own(values):
         return lax.dynamic_slice_in_dim(values, place * stem_cols, stem_cols, axis=1)
 
@@ -1525,30 +1921,42 @@
         ],
         axis=1,
     )
-    group_count = lax.axis_size("group")
-
-    def update(weight, gradient, first, second, moment, total):
-        delta, first_new, second_new = adam_step(weight, gradient, first, second)
-        if total is None:
-            total = plane_sum(to_half(delta))
-        mean_delta = total / group_count
-        moment_new = outer_mom * moment + mean_delta
-        new_weight = weight - outer_rate * (mean_delta + outer_mom * moment_new)
-        return new_weight, to_half(new_weight), first_new[None], second_new[None], moment_new
-
-    def update_layers(at, weight, first, second, moment):
-        parts = [
-            update(weight[layer], reduced[layer][at], first[layer], second[layer], moment[layer], reduced[layer][3 + at])
-            for layer in range(LAYERS)
-        ]
-        return [jnp.stack([parts[0][out], parts[1][out]], axis=1 if out in (2, 3) else 0) for out in range(5)]
-
-    stem_out = [flip(v) for v in update(stem_t, stem_grad, stem_first[0].T, stem_second[0].T, stem_moment.T, None)]
-    lin_out = update_layers(1, lin_t, flip(layer_in_first[0]), flip(layer_in_second[0]), flip(layer_in_moment))
-    lin_out = [flip(v) for v in lin_out]
-    lout_out = update_layers(2, layer_out, layer_out_first[0], layer_out_second[0], layer_out_moment)
-    pairs = [v.reshape((LAYERS,) + v.shape[-3:]) for v in (experts, experts_first, experts_second, experts_moment)]
-    expert_out = update_layers(0, *pairs)
+    stem_stepped = adam_step(stem_t, stem_grad, stem_first[0].T, stem_second[0].T)
+    stem_delta = jnp.pad(to_half(stem_stepped[0]), ((0, 0), (0, -stem_t.shape[1] % 128)))
+    for layer, gm in ((1, gm_b), (0, gm_a)):
+        spread = jnp.pad(gm, ((0, 0), (4 * D, lin_cols * sharers - 10 * D)))
+        window = lax.dynamic_slice_in_dim(spread, place * lin_cols, lin_cols, axis=1)
+        dex, dqkvo, dup, ddn = outgoing[layer]
+        reduced[layer] = reduce_layer(
+            layer,
+            dex.reshape((-1, halves) + dex.shape[1:]),
+            dqkvo.reshape(halves, lin_cols, D),
+            dup.reshape(-1, halves, lin_cols, D),
+            ddn.reshape(-1, halves, layer_out.shape[1], D),
+            outer(window, cond_f),
+            states,
+            stem_delta if layer == 1 else None,
+        )
+    stem_total = reduced[1][6]
+    group_count = lax.axis_size(GROUP)
+
+    mean_delta = stem_total[:, : stem_t.shape[1]] / group_count
+    moment_new = outer_mom * stem_moment.T + mean_delta
+    new_weight = stem_t - outer_rate * (mean_delta + outer_mom * moment_new)
+    stem_out = [flip(v) for v in (new_weight, to_half(new_weight), stem_stepped[1][None], stem_stepped[2][None], moment_new)]
+
+    def both(at, rows, tile, weight, first, second, moment):
+        grads = [reduced[layer][at].reshape(rows, -1) for layer in range(LAYERS)]
+        totals = [reduced[layer][3 + at].reshape(rows, -1) for layer in range(LAYERS)]
+        shaped = [v.reshape(LAYERS, rows, -1) for v in (weight, first, second, moment)]
+        return update_arrays(tile, grads, totals, *shaped)
+
+    lin_out = both(1, lin_cols, 432, lin_t, flip(layer_in_first), flip(layer_in_second), flip(layer_in_moment))
+    lin_out = [flip(v.reshape((1,) * (at in (2, 3)) + v.shape)) for at, v in enumerate(lin_out)]
+    lout_rows = layer_out.shape[1]
+    lout_out = both(2, lout_rows, lout_rows // 2, layer_out, layer_out_first, layer_out_second, layer_out_moment)
+    lout_out = [v.reshape((1,) * (at in (2, 3)) + v.shape) for at, v in enumerate(lout_out)]
+    expert_out = both(0, 2 * D, D // 2, experts, experts_first, experts_second, experts_moment)
     likes = (experts, experts, experts_first, experts_second, experts)
     expert_out = [v.reshape(like.shape) for v, like in zip(expert_out, likes)]
     results = []
@@ -1559,56 +1967,56 @@
 
 def solution(mesh):
     placed = (
-        P(("group", "expert", "dp"), None),
-        P(("group", "expert", "dp"), None),
-        P(("group", "expert", "dp")),
-        P(("group", "expert", "dp")),
-        P(None, ("group", "expert", "dp"), None),
-        P(None, ("group", "expert", "dp"), None),
-        P(None, ("expert", "dp")),
-        P(None, None, ("expert", "dp")),
-        P(None, ("expert", "dp"), None),
-        P(None, "expert", None, None, "dp"),
-        P("group", None, ("expert", "dp")),
-        P("group", None, None, ("expert", "dp")),
-        P("group", None, ("expert", "dp"), None),
-        P("group", None, "expert", None, None, "dp"),
-        P("group", None, ("expert", "dp")),
-        P("group", None, None, ("expert", "dp")),
-        P("group", None, ("expert", "dp"), None),
-        P("group", None, "expert", None, None, "dp"),
-        P(None, ("expert", "dp")),
-        P(None, None, ("expert", "dp")),
-        P(None, ("expert", "dp"), None),
-        P(None, "expert", None, None, "dp"),
-    )
-    step = few_experts if mesh.shape["expert"] <= 4 else per_device
+        P((GROUP, LINE, CORE), None),
+        P((GROUP, LINE, CORE), None),
+        P((GROUP, LINE, CORE)),
+        P((GROUP, LINE, CORE)),
+        P(None, (GROUP, LINE, CORE), None),
+        P(None, (GROUP, LINE, CORE), None),
+        P(None, (LINE, CORE)),
+        P(None, None, (LINE, CORE)),
+        P(None, (LINE, CORE), None),
+        P(None, LINE, None, None, CORE),
+        P(GROUP, None, (LINE, CORE)),
+        P(GROUP, None, None, (LINE, CORE)),
+        P(GROUP, None, (LINE, CORE), None),
+        P(GROUP, None, LINE, None, None, CORE),
+        P(GROUP, None, (LINE, CORE)),
+        P(GROUP, None, None, (LINE, CORE)),
+        P(GROUP, None, (LINE, CORE), None),
+        P(GROUP, None, LINE, None, None, CORE),
+        P(None, (LINE, CORE)),
+        P(None, None, (LINE, CORE)),
+        P(None, (LINE, CORE), None),
+        P(None, LINE, None, None, CORE),
+    )
+    step = few_experts if mesh.shape[LINE] <= 4 else per_device
     return jax.shard_map(
         step,
         mesh=mesh,
         in_specs=placed,
         out_specs=(
             P(),
-            P(None, ("expert", "dp")),
-            P(None, None, ("expert", "dp")),
-            P(None, ("expert", "dp"), None),
-            P(None, "expert", None, None, "dp"),
-            P(None, ("expert", "dp")),
-            P(None, None, ("expert", "dp")),
-            P(None, ("expert", "dp"), None),
-            P(None, "expert", None, None, "dp"),
-            P("group", None, ("expert", "dp")),
-            P("group", None, None, ("expert", "dp")),
-            P("group", None, ("expert", "dp"), None),
-            P("group", None, "expert", None, None, "dp"),
-            P("group", None, ("expert", "dp")),
-            P("group", None, None, ("expert", "dp")),
-            P("group", None, ("expert", "dp"), None),
-            P("group", None, "expert", None, None, "dp"),
-            P(None, ("expert", "dp")),
-            P(None, None, ("expert", "dp")),
-            P(None, ("expert", "dp"), None),
-            P(None, "expert", None, None, "dp"),
+            P(None, (LINE, CORE)),
+            P(None, None, (LINE, CORE)),
+            P(None, (LINE, CORE), None),
+            P(None, LINE, None, None, CORE),
+            P(None, (LINE, CORE)),
+            P(None, None, (LINE, CORE)),
+            P(None, (LINE, CORE), None),
+            P(None, LINE, None, None, CORE),
+            P(GROUP, None, (LINE, CORE)),
+            P(GROUP, None, None, (LINE, CORE)),
+            P(GROUP, None, (LINE, CORE), None),
+            P(GROUP, None, LINE, None, None, CORE),
+            P(GROUP, None, (LINE, CORE)),
+            P(GROUP, None, None, (LINE, CORE)),
+            P(GROUP, None, (LINE, CORE), None),
+            P(GROUP, None, LINE, None, None, CORE),
+            P(None, (LINE, CORE)),
+            P(None, None, (LINE, CORE)),
+            P(None, (LINE, CORE), None),
+            P(None, LINE, None, None, CORE),
         ),
         check_vma=False,
     )

time: 1100 us -> 796 us (0.72)
  waiting for transfers between devices: 281 us -> 0 us
  Pallas kernels: 587 us -> 751 us
  blocking collectives: 94.6 us -> 0 us
  local copies, waits for them, and re-layouts: 52.2 us -> 16.8 us
  other arithmetic: 45.9 us -> 12.1 us
  between operations: 15.9 us -> 1.36 us
    all_gather x7 -> x0, waiting for transfers between devices: 274 us -> none  [the longest x2 147 us: few_experts(): lax.all_gather(to_half(experts[layer]), SHARD, axis=0, tiled=True)]
    pallas_call x6 -> x11, Pallas kernels: 404 us -> 577 us  [the longest x2 297 us: reduce_layer(): pl.pallas_call(functools.partial(reduce_kernel, layer, bool(stems)), out_...]
    all_gather x3 -> x0, blocking collectives: 44.6 us -> none  [the longest x2 28.7 us: few_experts(): factors = lax.all_gather(factors, SHARD, axis=0, tiled=True)]
    psum x1 -> x0, blocking collectives: 38.7 us -> none  [few_experts(): loss_total = lax.psum(jnp.sum(loss_rows), ('group', 'expert', 'dp'))]
    unnamed x170 -> x52, local copies, waits for them, and re-layouts: 34.8 us -> 6.87 us
    another operation x11 -> x5, other arithmetic: 18.7 us -> 1.72 us  [update_layers(): jnp.stack([parts[0][out], parts[1][out]], axis=1 if out in (2, 3) else 0)]
    pallas_call x2, Pallas kernels: 114 us -> 99.4 us  [ffn_backward(): pl.pallas_call(functools.partial(ffn_bwd_kernel, shared_steps, halves), g...]
    unnamed x11 -> x3, other arithmetic: 12.4 us -> 0.89 us
  transfers between devices with their start and end apart: 11 -> 0, of which waited for: 8 -> 0; matrix products, arithmetic and copies ran while one was open for 6% -> 0% of each run, Pallas kernels for 34% -> 0%
where the time goes in v3:
time: 796 us; the launch traced here: 790 us
  Pallas kernels  751 us (94%)
  local copies, waits for them, and re-layouts  16.8 us (2%)
  other arithmetic  12.1 us (2%)
  matrix products  8.2 us (1%)
    pallas_call x2, Pallas kernels, reduce_layer(): pl.pallas_call(functools.partial(reduce_kernel, layer, bool(stems)), out_...  297 us
    pallas_call x1, Pallas kernels, gather_weights(): pl.pallas_call(functools.partial(gather_kernel, kinds, split), out_shape=...  111 us
    pallas_call x2, Pallas kernels, ffn_forward(): pl.pallas_call(functools.partial(ffn_fwd_kernel, shared_steps, halves, le...  109 us
    pallas_call x2, Pallas kernels, ffn_backward(): pl.pallas_call(functools.partial(ffn_bwd_kernel, shared_steps, halves), g...  99.4 us
    pallas_call x2, Pallas kernels, attn_backward(): pl.pallas_call(attn_bwd_kernel, grid=(count // PATCHES,), in_specs=[rows_...  47.8 us
    pallas_call x3, Pallas kernels, update_arrays(): pl.pallas_call(functools.partial(update_kernel, lax.axis_size(GROUP)), gr...  34.2 us
    pallas_call x2, Pallas kernels, attn_forward(): pl.pallas_call(attn_fwd_kernel, grid=(count // PATCHES,), in_specs=[rows_...  21.9 us

profile of v3, /device:TPU:0, one launch (start us, length us, event | category | flops | bytes accessed | tf_op | source)
XLA Modules:
  0.0 790.0 jit_solution(14182621290690387659)
XLA Ops:
  0.7 1.0 multiply_sine_fusion.1
  1.9 1.1 bitcast_convert_fusion
  3.0 0.7 constant_dynamic-update-slice_fusion.2
  4.1 1.2 bitcast_convert_fusion.1.refs_1_
  5.4 0.9 slice_bitcast_fusion.2
  6.3 1.1 copy-done.1
  7.6 1.6 slice_bitcast_fusion
  9.1 111.3 %gather_weights.1 = (bf16[8,48,3072]{2,1,0:T(8,128)(2,1)}, bf16[2,8,864,384]{3,2,1,0:T(8,128)(2,1)}, bf16[8,384,384]{2,1,0:T(8,128)(2,1)}, bf16[8,384,384]{2,1,0:T(8,128)(2,1)}, bf16[8,2,384,768]{3,2,1,0:T(8,128)(2,1)}) custom-call(bf16[48,3072]{1,0:T(8,128)(2,1)} %copy-done.8, bf16[2,864,384]{2,1,0:T(8,128)(2,1)} %bitcast_convert_fusion.1.refs_1_, ...), custom_call_target="tpu_custom_call" | custom-call | tf_op jit(solution)/shard_map/gather_weights/pallas_call | solution.py:1704
  120.4 2.4 bitcast_add_fusion.x_ref
  123.0 0.6 select_maximum_fusion.feat_ref
  123.7 0.6 convert_convert_fusion.1.hot_ref
  124.4 6.1 cond_forward.1
  130.5 1.6 slice_bitcast_fusion.5
  132.1 10.7 %attention_forward.2 = (bf16[1024,384]{1,0:T(8,128)(2,1)}, bf16[1024,1152]{1,0:T(8,128)(2,1)}, bf16[1024,384]{1,0:T(8,128)(2,1)}, f32[1024,384]{1,0:T(8,128)}, f...) custom-call(f32[1024,384]{1,0:T(8,128)} %bitcast_add_fusion.x_ref, f32[8,2304]{1,0:T(8,128)} %get-tuple-element.289.mods_ref, ...), custom_call_target="tpu_custom_call" | custom-call | flops 10871635968 | bytes 6291456 | tf_op jit(solution)/shard_map/attention_forward/pallas_call | solution.py:972
  142.9 1.0 copy.87.g4_ref
  143.9 68.2 %ffn_forward.2 = (bf16[12,1024,768]{2,1,0:T(8,128)(2,1)}, bf16[12,1024,768]{2,1,0:T(8,128)(2,1)}, f32[1024,384]{1,0:T(8,128)}, f32[1024,384]{1,0:T(8,128)}, bf16[8,2,384,768]{3,2,1,0:T(8,128)(2,1)}) custom-call(bf16[1024,384]{1,0:T(8,128)(2,1)} %get-tuple-element.109.n2_ref, f32[1024,384]{1,0:T(8,128)} %get-tuple-element.110.mid_ref, ...), custom_call_target="tpu_custom_call" | custom-call | flops 57982058496 | bytes 75497472 | tf_op jit(solution)/shard_map/ffn_forward/pallas_call | solution.py:1027
  212.1 11.2 %attention_forward.3 = (bf16[1024,384]{1,0:T(8,128)(2,1)}, bf16[1024,1152]{1,0:T(8,128)(2,1)}, bf16[1024,384]{1,0:T(8,128)(2,1)}, f32[1024,384]{1,0:T(8,128)}, f...) custom-call(f32[1024,384]{1,0:T(8,128)} %get-tuple-element.113.x_ref, f32[8,2304]{1,0:T(8,128)} %get-tuple-element.288.mods_ref, ...), custom_call_target="tpu_custom_call" | custom-call | flops 10871635968 | bytes 6291456 | tf_op jit(solution)/shard_map/attention_forward/pallas_call | solution.py:972
  223.3 1.0 copy.88.g4_ref
  224.4 40.4 %ffn_forward.3 = (bf16[12,1024,768]{2,1,0:T(8,128)(2,1)}, bf16[12,1024,768]{2,1,0:T(8,128)(2,1)}, f32[1024,384]{1,0:T(8,128)}, f32[1024,384]{1,0:T(8,128)}) custom-call(bf16[1024,384]{1,0:T(8,128)(2,1)} %get-tuple-element.114.n2_ref, f32[1024,384]{1,0:T(8,128)} %get-tuple-element.115.mid_ref, f32[8,2304]{1,0:T(8,128)} %get-tuple-element.288.mods_ref, ...), custom_call_target="tpu_custom_call" | custom-call | flops 57982058496 | bytes 75497472 | tf_op jit(solution)/shard_map/ffn_forward/pallas_call | solution.py:1027
  264.8 0.9 slice_bitcast_fusion.4
  265.7 0.7 copy.89.fo_ref
  266.3 5.3 final_step.1
  271.7 1.3 convert.69
  273.0 49.7 %ffn_backward.2 = (bf16[3456,384]{1,0:T(8,128)(2,1)}, bf16[3072,384]{1,0:T(8,128)(2,1)}, bf16[8,2,384,768]{3,2,1,0:T(8,128)(2,1)}, f32[1024,384]{1,0:T(8,128)}, f32[8,384]{1,0:T(8,128)}) custom-call(f32[1024,384]{1,0:T(8,128)} %get-tuple-element.120.g_ref, bf16[1024,384]{1,0:T(8,128)(2,1)} %get-tuple-element.114.n2_ref, ...), custom_call_target="tpu_custom_call" | custom-call | flops 57982058496 | bytes 75497472 | tf_op jit(solution)/shard_map/ffn_backward/pallas_call | solution.py:1054
  322.7 23.7 %attention_backward.2 = (f32[1024,384]{1,0:T(8,128)}, f32[8,2304]{1,0:T(8,128)}, bf16[1728,384]{1,0:T(8,128)(2,1)}) custom-call(f32[1024,384]{1,0:T(8,128)} %get-tuple-element.124.gn2_ref, f32[1024,384]{1,0:T(8,128)} %get-tuple-element.120.g_ref, f32[1024,384]{1,0:T(8,128)} %get-tuple-element.115.mid_ref, f32[1024,384]{1,0:T(8,128)} %get-tuple-element.113.x_ref, ...), custom_call_target="tpu_custom_call" | custom-call | flops 26575110144 | bytes 6291456 | tf_op jit(solution)/shard_map/attention_backward/pallas_call | solution.py:997
  346.4 49.7 %ffn_backward.3 = (bf16[3456,384]{1,0:T(8,128)(2,1)}, bf16[3072,384]{1,0:T(8,128)(2,1)}, bf16[8,2,384,768]{3,2,1,0:T(8,128)(2,1)}, f32[1024,384]{1,0:T(8,128)}, f32[8,384]{1,0:T(8,128)}) custom-call(f32[1024,384]{1,0:T(8,128)} %get-tuple-element.130.g_ref, bf16[1024,384]{1,0:T(8,128)(2,1)} %get-tuple-element.109.n2_ref, ...), custom_call_target="tpu_custom_call" | custom-call | flops 57982058496 | bytes 75497472 | tf_op jit(solution)/shard_map/ffn_backward/pallas_call | solution.py:1054
  396.1 24.1 %attention_backward.3 = (f32[1024,384]{1,0:T(8,128)}, f32[8,2304]{1,0:T(8,128)}, bf16[1728,384]{1,0:T(8,128)(2,1)}) custom-call(f32[1024,384]{1,0:T(8,128)} %get-tuple-element.134.gn2_ref, f32[1024,384]{1,0:T(8,128)} %get-tuple-element.130.g_ref, f32[1024,384]{1,0:T(8,128)} %get-tuple-element.110.mid_ref, f32[1024,384]{1,0:T(8,128)} %bitcast_add_fusion.x_ref, ...), custom_call_target="tpu_custom_call" | custom-call | flops 26575110144 | bytes 6291456 | tf_op jit(solution)/shard_map/attention_backward/pallas_call | solution.py:997
  420.2 1.6 fusion
  421.9 0.7 constant_dynamic-update-slice_fusion.12
  422.6 0.9 constant_dynamic-update-slice_fusion.11
  423.5 0.9 constant_dynamic-update-slice_fusion.10
  424.4 0.7 constant_dynamic-update-slice_fusion.9
  425.2 5.1 cond_backward.1
  430.3 0.7 constant_dynamic-update-slice_fusion.8
  431.0 0.7 constant_dynamic-update-slice_fusion.7
  431.7 0.7 constant_dynamic-update-slice_fusion.6
  433.4 14.7 %exchange_small.1 = (bf16[8,16,2688]{2,1,0:T(8,128)(2,1)S(1)}, f32[8,128]{1,0:T(8,128)S(1)}) custom-call(bf16[16,2688]{1,0:T(8,128)(2,1)S(1)} %reshape.234.packed, f32[8,128]{1,0:T(8,128)S(1)} %pad.54.loss), custom_call_target="tpu_custom_call" | custom-call | tf_op jit(solution)/shard_map/exchange_small/pallas_call | solution.py:1785
  448.0 0.6 reduce_sum.38
  449.2 1.5 fusion.15.extra
  452.8 1.3 fusion.10
  454.1 0.7 pad.56.rest_0_
  454.9 149.8 %reduce_layer.2 = (f32[2,384,768]{2,1,0:T(8,128)}, f32[864,384]{1,0:T(8,128)}, f32[384,384]{1,0:T(8,128)}, f32[2,384,768]{2,1,0:T(8,128)}, f32[864,384]{1,0:T(8,...) custom-call(bf16[4,2,2,384,768]{4,3,2,1,0:T(8,128)(2,1)} %bitcast.191, bf16[2,864,384]{2,1,0:T(8,128)(2,1)} %bitcast.205, ...), custom_call_target="tpu_custom_call" | custom-call | tf_op jit(solution)/shard_map/reduce_layer/pallas_call | solution.py:1481
  604.7 2.2 convert_bitcast_fusion
  606.9 1.5 fusion.16.extra
  608.4 147.2 %reduce_layer.3 = (f32[2,384,768]{2,1,0:T(8,128)}, f32[864,384]{1,0:T(8,128)}, f32[384,384]{1,0:T(8,128)}, f32[2,384,768]{2,1,0:T(8,128)}, f32[864,384]{1,0:T(8,128)}, /*index=5*/f32[384,384]{1,0:T(8,128)}) custom-call(bf16[4,2,2,384,768]{4,3,2,1,0:T(8,128)(2,1)} %bitcast.192, bf16[2,864,384]{2,1,0:T(8,128)(2,1)} %bitcast.206, ...), custom_call_target="tpu_custom_call" | custom-call | tf_op jit(solution)/shard_map/reduce_layer/pallas_call | solution.py:1481
  755.6 10.2 %update_arrays.3 = (f32[2,864,384]{2,1,0:T(8,128)}, bf16[2,864,384]{2,1,0:T(8,128)(2,1)}, f32[2,864,384]{2,1,0:T(8,128)}, f32[2,864,384]{2,1,0:T(8,128)}, f32[2,864,384]{2,1,0:T(8,128)}) custom-call(f32[864,384]{1,0:T(8,128)} %get-tuple-element.162.grad_a, f32[864,384]{1,0:T(8,128)} %get-tuple-element.163.grad_b, f32[864,384]{1,0:T(8,128)} %get-tuple-element.164.total_a, ...), custom_call_target="tpu_custom_call" | custom-call | tf_op jit(solution)/shard_map/update_arrays/pallas_call | solution.py:1127
  765.8 5.9 update_arrays.4
  771.7 18.1 %update_arrays.5 = (f32[2,768,768]{2,1,0:T(8,128)}, bf16[2,768,768]{2,1,0:T(8,128)(2,1)}, f32[2,768,768]{2,1,0:T(8,128)}, f32[2,768,768]{2,1,0:T(8,128)}, f32[2,768,768]{2,1,0:T(8,128)}) custom-call(f32[768,768]{1,0:T(8,128)} %bitcast.203, f32[768,768]{1,0:T(8,128)} %bitcast.201, f32[768,768]{1,0:T(8,128)} %bitcast.204, f32[768,768]{1,0:T(8,128)} %bitcast.202, ...), custom_call_target="tpu_custom_call" | custom-call | tf_op jit(solution)/shard_map/update_arrays/pallas_call | solution.py:1127
  (91 shorter events, 4.6 us)
Async XLA Ops:
  0.7 119.8 %copy-start = (bf16[1024,16]{0,1:T(8,128)(2,1)S(1)}, bf16[1024,16]{0,1:T(8,128)(2,1)}, u32[]{:S(2)}) copy-start(bf16[1024,16]{0,1:T(8,128)(2,1)} %param.22) | copy-start | bytes 98308
  0.7 3.4 copy-start.2
  3.7 1.7 copy-start.3
  4.1 1.3 copy-start.8
  4.1 3.2 copy-start.1
  9.1 113.8 %copy-start.19 = (s32[4]{0:T(128)S(1)}, s32[4]{0:T(128)}, u32[]{:S(2)}) copy-start(s32[4]{0:T(128)} %param.24) | copy-start | bytes 52
  9.1 114.5 %copy-start.17 = (s32[4]{0:T(128)S(1)}, s32[4]{0:T(128)}, u32[]{:S(2)}) copy-start(s32[4]{0:T(128)} %param.25) | copy-start | bytes 52
  122.9 1.5 copy-start.13
  122.9 1.5 copy-start.15
  132.1 10.7 %copy-start.10 = (f32[2,1024,2]{1,2,0:T(2,128)S(1)}, f32[2,1024,2]{1,2,0:T(2,128)}, u32[]{:S(2)}) copy-start(f32[2,1024,2]{1,2,0:T(2,128)} %param.27) | copy-start | bytes 49156
  132.1 10.7 %copy-start.11 = (s32[2,1024,2]{1,2,0:T(2,128)S(1)}, s32[2,1024,2]{1,2,0:T(2,128)}, u32[]{:S(2)}) copy-start(s32[2,1024,2]{1,2,0:T(2,128)} %param.26) | copy-start | bytes 49156
  396.1 25.8 %copy-start.9 = (bf16[16,384]{1,0:T(8,128)(2,1)S(1)}, bf16[16,384]{1,0:T(8,128)(2,1)}, u32[]{:S(2)}) copy-start(bf16[16,384]{1,0:T(8,128)(2,1)} %convert.69) | copy-start | bytes 36868
  425.1 7.3 copy-start.14
  425.1 7.3 copy-start.16
  425.1 7.6 copy-start.18
  425.2 8.1 %copy-start.12 = (f32[16,1]{1,0:T(8,128)S(1)}, f32[16,1]{1,0:T(8,128)}, u32[]{:S(2)}) copy-start(f32[16,1]{1,0:T(8,128)} %get-tuple-element.150) | copy-start | bytes 196
  449.2 3.6 copy-start.4
  449.2 3.6 copy-start.5
  449.2 3.6 copy-start.6
  454.9 149.8 %copy-start.7 = (f32[2441,48]{0,1:T(8,128)S(1)}, f32[2441,48]{0,1:T(8,128)}, u32[]{:S(2)}) copy-start(f32[2441,48]{0,1:T(8,128)} %param.40) | copy-start | bytes 1406020

commit v4 on v3

--- a/solution.py
+++ b/solution.py
@@ -823,11 +823,102 @@
             x_ref[rows, :] = mid_ref[rows, :] + mod_row(mods_ref, item, 5) * acc[rows, :]
 
 
+EARLY = 2
+END_ROUTES = {0: [(3, 1), (2, 1), (1, 1)], 3: [(0, -1), (1, -1), (2, -1)]}
+
+
+def early_slot(owner, step, place):
+    return 4 if step == -1 and owner == place - 1 else owner
+
+
+def early_beside(step, last, dex, chip_out, came_out, chip, local, core_send, core_recv, load_sem, line_send, line_recv, out_sem):
+    at, core = lax.axis_index(LINE), lax.axis_index(CORE)
+    units = reduce_units()[:EARLY]
+    sibling = {CORE: 1 - core}
+
+    def source(unit, which):
+        _, matrix, row, rows, _, _ = units[unit]
+        return dex.at[:, which, matrix, pl.ds(row, rows)]
+
+    def given(unit):
+        return pltpu.make_async_remote_copy(
+            source(unit, 1 - core), chip.at[unit], core_send.at[unit], core_recv.at[unit],
+            device_id=sibling, device_id_type=MESH_ID,
+        )
+
+    def loaded(unit):
+        return pltpu.make_async_copy(source(unit, core), local.at[unit], load_sem.at[unit])
+
+    def stored(unit):
+        return pltpu.make_async_copy(chip.at[unit], chip_out.at[unit], out_sem.at[unit])
+
+    def sent(unit, place, owner, direction):
+        slot = early_slot(owner, direction, place)
+        return pltpu.make_async_remote_copy(
+            chip.at[unit, owner], came_out.at[unit, slot], line_send.at[unit, owner], line_recv.at[unit, slot],
+            device_id={LINE: at + direction}, device_id_type=MESH_ID,
+        )
+
+    @pl.when(step == 0)
+    def _():
+        greet([sibling], at, 4)
+        for unit in range(EARLY):
+            given(unit).start()
+            loaded(unit).start()
+
+    for unit in range(EARLY):
+
+        @pl.when(step == 1 + unit)
+        def _(unit=unit):
+            given(unit).wait_recv()
+            loaded(unit).wait()
+            for owner in range(4):
+
+                def add(tile, owner=owner):
+                    total = chip[unit, owner, tile, :].astype(f32) + local[unit, owner, tile, :].astype(f32)
+                    chip[unit, owner, tile, :] = total.astype(bf16)
+
+                row_tiles(units[unit][3], add)
+            stored(unit).start()
+            for place, routes in END_ROUTES.items():
+
+                @pl.when(at == place)
+                def _(place=place, routes=routes):
+                    for owner, direction in routes:
+                        sent(unit, place, owner, direction).start()
+
+    @pl.when(step == last)
+    def _():
+        for unit in range(EARLY):
+            given(unit).wait_send()
+            stored(unit).wait()
+            for place, routes in END_ROUTES.items():
+
+                @pl.when(at == place)
+                def _(unit=unit, place=place, routes=routes):
+                    for owner, direction in routes:
+                        sent(unit, place, owner, direction).wait_send()
+
+                @pl.when(at == place + routes[0][1])
+                def _(unit=unit, place=place, routes=routes):
+                    for owner, direction in routes:
+                        slot = early_slot(owner, direction, place)
+                        pltpu.make_async_remote_copy(
+                            came_out.at[unit, slot], came_out.at[unit, slot], line_send.at[unit, owner],
+                            line_recv.at[unit, slot], device_id=sibling, device_id_type=MESH_ID,
+                        ).wait_recv()
+
+
 def ffn_bwd_kernel(
-    shared_steps, halves, g_ref, n2_ref, mods_ref, g4_ref, mixed_ref, act_ref, dg_ref, up_ref, dn_ref, ex_ref,
-    dup_ref, ddn_ref, dex_ref, gn2_ref, gg_ref, gmix, gs, gst, n2t, din, acc, racc,
+    shared_steps, halves, early, g_ref, n2_ref, mods_ref, g4_ref, mixed_ref, act_ref, dg_ref, up_ref, dn_ref, ex_ref, *rest
 ):
     step = pl.program_id(0)
+    if early:
+        other_dex, *rest = rest
+        early_refs = [other_dex] + rest[5:7] + rest[14:]
+        rest = rest[:5] + rest[7:14]
+        early_beside(step, pl.num_programs(0) - 1, *early_refs)
+    dup_ref, ddn_ref, dex_ref, gn2_ref, gg_ref, gmix, gs, gst, n2t, din, acc, racc = rest
     items = n2_ref.shape[0] // PATCHES
 
     @pl.when(step == 0)
@@ -1045,25 +1136,32 @@
     )(n2, middle, mods, g4, lin, lout, experts_w, *beside)
 
 
-def ffn_backward(layer, grad, n2, mods, g4, mixed, active, slope, lin, lout, experts_w, halves):
+def ffn_backward(layer, grad, n2, mods, g4, mixed, active, slope, lin, lout, experts_w, halves, early=()):
     count = n2.shape[0]
     shared_steps = lout.shape[0] // CHUNK
     steps = shared_steps + experts_w.shape[0]
     wide = pl.BlockSpec((1, count, CHUNK), lambda step: (step, 0, 0))
     specs = weight_specs(layer, shared_steps, lin.shape[1])
+    anywhere = [pl.BlockSpec(memory_space=pl.ANY)] * len(early)
+    remote = pltpu.CompilerParams(vmem_limit_bytes=62 * MIB, collective_id=8, has_side_effects=True)
+    dma = pltpu.SemaphoreType.DMA
+    early_scratch = [pltpu.VMEM((EARLY, 4, D // 2, CHUNK), bf16)] * 2
+    early_scratch += [dma((EARLY,)), dma((EARLY,)), dma((EARLY,)), dma((EARLY, 4)), dma((EARLY, 5)), dma((EARLY,))]
     return pl.pallas_call(
-        functools.partial(ffn_bwd_kernel, shared_steps, halves),
+        functools.partial(ffn_bwd_kernel, shared_steps, halves, len(early)),
         grid=(steps,),
         in_specs=[whole(grad.shape), whole(n2.shape), whole(mods.shape), whole(g4.shape), whole(mixed.shape), wide, wide]
-        + specs,
-        out_specs=[whole((lout.shape[0] + D, D)), specs[1], specs[2], whole((count, D)), whole((8, D))],
+        + specs
+        + anywhere,
+        out_specs=[whole((lout.shape[0] + D, D)), specs[1], specs[2], whole((count, D)), whole((8, D))] + anywhere * 2,
         out_shape=[
             shape_of((lout.shape[0] + D, D), bf16),
             shape_of(lout.shape, bf16),
             shape_of(experts_w.shape, bf16),
             shape_of((count, D), f32),
             shape_of((8, D), f32),
-        ],
+        ]
+        + [shape_of((EARLY, lead, D // 2, CHUNK), bf16) for lead in (4, 5) if early],
         scratch_shapes=[
             pltpu.VMEM((count, D), f32),
             pltpu.VMEM((count, D), bf16),
@@ -1072,11 +1170,12 @@
             pltpu.VMEM((count, CHUNK), bf16),
             pltpu.VMEM((count, D), f32),
             pltpu.VMEM((count, D), f32),
-        ],
-        compiler_params=params(60),
+        ]
+        + (early_scratch if early else []),
+        compiler_params=remote if early else params(60),
         cost_estimate=cost(4 * steps * count * D * CHUNK * 4 // 2, 8 * steps * count * CHUNK),
         name="ffn_backward",
-    )(grad, n2, mods, g4, mixed, active, slope, lin, lout, experts_w)
+    )(grad, n2, mods, g4, mixed, active, slope, lin, lout, experts_w, *early)
 
 
 def final_step(tokens, mods, fo_rows, target_t):
@@ -1200,6 +1299,9 @@
 def reduce_kernel(
     layer, with_stem, dex, dqkvo, dup, ddn, extra, ex_w, ex_f, ex_s, li_w, li_f, li_s, lo_w, lo_f, lo_s, *rest
 ):
+    early = EARLY if with_stem else 0
+    if early:
+        chip_in, came_in, *rest = rest
     if with_stem:
         stem_in, *rest, stem_sem, stem_send, stem_recv, stem_a, stem_b, stem_c, stem_d = rest
         stem_out = rest.pop(6)
@@ -1264,9 +1366,28 @@
             stem_d[...] = stem_a[...].astype(f32) + stem_c[...].astype(f32)
             pltpu.make_async_copy(stem_d, stem_out, stem_sem.at[1]).start()
 
+    early_slots = {1: [3, 2, 1], 2: [0, 1, 4]}
+
+    def early_load(unit, slot, index):
+        sem = (load_sem.at[unit, 1], load_sem.at[unit, 2], load_sem.at[number, 1 + unit])[index]
+        return pltpu.make_async_copy(came_in.at[unit, slot], came[unit].at[slot], sem)
+
     given, loads = [], []
     for unit in range(number):
         given.append([])
+        loads.append([])
+        if unit < early:
+            copy = pltpu.make_async_copy(chip_in.at[unit], chip[unit], load_sem.at[unit, 0])
+            copy.start()
+            loads[unit].append(copy)
+            for place, slots in early_slots.items():
+
+                @pl.when(at == place)
+                def _(unit=unit, slots=slots):
+                    for index, slot in enumerate(slots):
+                        early_load(unit, slot, index).start()
+
+            continue
         for place, (source, where) in enumerate(pieces(unit, 1 - core)):
             copy = pltpu.make_async_remote_copy(
                 source, dest(chip, unit, where), core_send.at[unit, place], core_recv.at[unit, place],
@@ -1274,7 +1395,6 @@
             )
             copy.start()
             given[unit].append(copy)
-        loads.append([])
         for place, (source, where) in enumerate(pieces(unit, core)):
             copy = pltpu.make_async_copy(source, dest(local, unit, where), load_sem.at[unit, place])
             copy.start()
@@ -1302,7 +1422,10 @@
             device_id={LINE: at + step}, device_id_type=MESH_ID,
         )
 
-    def arrived(unit, slot):
+    def arrived(unit, slot, place):
+        if unit < early and slot in early_slots.get(place, ()):
+            early_load(unit, slot, early_slots[place].index(slot)).wait()
+            return
         pltpu.make_async_remote_copy(
             came[unit].at[slot], came[unit].at[slot], line_send.at[unit, 0], line_recv.at[unit, slot],
             device_id=sibling, device_id_type=MESH_ID,
@@ -1310,13 +1433,31 @@
 
     routes_of = {0: [(3, 1), (2, 1), (1, 1)], 1: [(3, 1), (2, 1), (0, -1)], 2: [(0, -1), (1, -1), (3, 1)], 3: [(0, -1), (1, -1), (2, -1)]}
     finals = {0: [4], 1: [1, 4], 2: [2, 4], 3: [3]}
+
+    def forward(unit):
+        rows, absent = units[unit][3], units[unit][5]
+        for middle in (1, 2):
+
+            @pl.when(at == middle)
+            def _(middle=middle):
+                for owner, step in routes_of[middle]:
+                    if owner in absent:
+                        continue
+                    arrived(unit, owner, middle)
+
+                    def add(tile, owner=owner):
+                        total = chip[unit][owner, tile, :].astype(f32) + came[unit][owner, tile, :].astype(f32)
+                        chip[unit][owner, tile, :] = total.astype(bf16)
+
+                    row_tiles(rows, add)
+                    line_copy(unit, owner, step, middle).start()
 
     for unit, (kind, matrix, row, rows, _, absent) in enumerate(units):
         for copy in given[unit]:
             copy.wait_recv()
         for copy in loads[unit]:
             copy.wait()
-        for owner in range(4):
+        for owner in range(0 if unit < early else 4):
             if owner in absent:
                 chip[unit][owner] = jnp.zeros(chip[unit].shape[1:], bf16)
                 continue
@@ -1331,7 +1472,7 @@
             @pl.when(at == end)
             def _(unit=unit, end=end, absent=absent):
                 for owner, step in routes_of[end]:
-                    if owner not in absent:
+                    if owner not in absent and unit >= early:
                         line_copy(unit, owner, step, end).start()
                 came[unit][0 if end == 0 else 4] = jnp.zeros(chip[unit].shape[1:], bf16)
 
@@ -1341,24 +1482,8 @@
             def _(unit=unit, owner=owner):
                 came[unit][owner] = jnp.zeros(chip[unit].shape[1:], bf16)
                 came[unit][4] = jnp.zeros(chip[unit].shape[1:], bf16)
-
-    def forward(unit):
-        rows, absent = units[unit][3], units[unit][5]
-        for middle in (1, 2):
-
-            @pl.when(at == middle)
-            def _(middle=middle):
-                for owner, step in routes_of[middle]:
-                    if owner in absent:
-                        continue
-                    arrived(unit, owner)
-
-                    def add(tile, owner=owner):
-                        total = chip[unit][owner, tile, :].astype(f32) + came[unit][owner, tile, :].astype(f32)
-                        chip[unit][owner, tile, :] = total.astype(bf16)
-
-                    row_tiles(rows, add)
-                    line_copy(unit, owner, step, middle).start()
+        if unit < early:
+            forward(unit)
 
     def plane_copies(unit, second_step):
         rows = units[unit][3]
@@ -1392,7 +1517,7 @@
             def _(place=place):
                 if place not in absent:
                     for slot in finals[place]:
-                        arrived(unit, slot)
+                        arrived(unit, slot, place)
 
         for copy in state_loads[unit]:
             copy.wait()
@@ -1440,7 +1565,7 @@
     for turn in range(number + 3):
         stem_turn(turn)
         for lag, action in enumerate((forward, finish, exchange, close)):
-            if 0 <= turn - lag < number:
+            if 0 <= turn - lag < number and (lag or turn >= early):
                 action(turn - lag)
 
     if with_stem:
@@ -1457,11 +1582,11 @@
             @pl.when(at == place)
             def _(place=place, unit=unit):
                 for owner, step in routes_of[place]:
-                    if owner not in units[unit][5]:
+                    if owner not in units[unit][5] and (unit >= early or place in (1, 2)):
                         line_copy(unit, owner, step, place).wait_send()
 
 
-def reduce_layer(layer, dex, dqkvo, dup, ddn, extra, states, stem_delta=None):
+def reduce_layer(layer, dex, dqkvo, dup, ddn, extra, states, stem_delta=None, begun=()):
     units = reduce_units()
     scratch = []
     for lead, kind in (((4,), bf16), ((4,), bf16), ((5,), bf16), ((), bf16), ((), bf16), ((), bf16), ((), f32), ((), f32), ((), f32)):
@@ -1481,14 +1606,14 @@
     return pl.pallas_call(
         functools.partial(reduce_kernel, layer, bool(stems)),
         out_shape=[shape_of(shape, f32) for shape in shapes],
-        in_specs=[anywhere] * (5 + len(states) + len(stems)),
+        in_specs=[anywhere] * (5 + len(states) + len(stems) + len(begun)),
         out_specs=[anywhere] * len(shapes),
         scratch_shapes=scratch,
         compiler_params=pltpu.CompilerParams(
             vmem_limit_bytes=62 * MIB, collective_id=1 + layer, has_side_effects=True
         ),
         name="reduce_layer",
-    )(dex, dqkvo, dup, ddn, extra, *states, *stems)
+    )(dex, dqkvo, dup, ddn, extra, *states, *begun, *stems)
 
 
 def shard_part(kind, ref, quarter, half=None):
@@ -1523,7 +1648,11 @@
         self.order = (near, 6 - near - far, far)
 
     def enter(self):
-        greet([self.sibling, self.side_x, self.side_y], self.at, 4)
+        barrier = pltpu.get_barrier_semaphore()
+        others = [{LINE: lax.rem(self.at + step, 4)} for step in (1, 2, 3)]
+        for partner in others + [self.sibling, self.side_x, self.side_y]:
+            pl.semaphore_signal(barrier, inc=1, device_id=partner, device_id_type=MESH_ID)
+        pl.semaphore_wait(barrier, 6)
 
     def whole_part(self, unit, owner, core):
         target = self.targets[unit]
@@ -1537,12 +1666,12 @@
             device_id=device, device_id_type=MESH_ID,
         )
 
-    def line_copy(self, unit, owner, to_slot, send_slot, step, own):
-        target = shard_part(self.kinds[unit], self.whole_part(unit, owner, self.core), self.group)
-        source = shard_part(self.kinds[unit], self.sources[unit], self.group) if own else target
+    def line_copy(self, unit, step):
+        target = shard_part(self.kinds[unit], self.whole_part(unit, self.at, self.core), self.group)
+        source = shard_part(self.kinds[unit], self.sources[unit], self.group)
         return pltpu.make_async_remote_copy(
-            source, target, self.sends.at[unit, send_slot, 0], self.recvs.at[unit, to_slot - 1, 0],
-            device_id={LINE: self.at + step}, device_id_type=MESH_ID,
+            source, target, self.sends.at[unit, step - 1, 0], self.recvs.at[unit, 3 - step, 0],
+            device_id={LINE: lax.rem(self.at + step, 4)}, device_id_type=MESH_ID,
         )
 
     def owner_of(self, slot):
@@ -1564,25 +1693,11 @@
             self.sources[unit], self.whole_part(unit, self.at, self.core), self.own_sem.at[unit]
         )
 
-    def own_line(self, unit, act):
-        for step, slot, send_slot, there in ((1, 3, 3, self.at < 3), (-1, 1, 4, self.at > 0)):
-
-            @pl.when(there)
-            def _(step=step, slot=slot, send_slot=send_slot):
-                act(self.line_copy(unit, self.at, slot, send_slot, step, True))
-
     def begin(self, unit):
-        self.own_line(unit, lambda copy: copy.start())
+        for step in (2, 1, 3):
+            self.line_copy(unit, step).start()
         self.core_copy(unit, 0, True).start()
         self.own_copy(unit).start()
-
-    def forwards(self, unit, slot, act):
-        left = self.at + slot >= 4
-        for step, to_slot, there in ((1, slot - 1, left & (self.at < 3)), (-1, slot + 1, (self.at + slot < 4) & (self.at > 0))):
-
-            @pl.when(there)
-            def _(step=step, to_slot=to_slot):
-                act(self.line_copy(unit, self.owner_of(slot), to_slot, slot - 1, step, False))
 
     def plane_copies(self, unit, slot):
         mine = self.part(unit, slot, self.group)
@@ -1605,7 +1720,6 @@
         for slot in self.order:
             mine = self.part(unit, slot, self.group)
             self.copy(unit, mine, mine, slot - 1, 0, self.sibling).wait_recv()
-            self.forwards(unit, slot, lambda copy: copy.start())
             for copy in self.plane_copies(unit, slot):
                 copy.start()
 
@@ -1624,7 +1738,6 @@
 
     def end(self, unit):
         self.own_copy(unit).wait()
-        self.own_line(unit, lambda copy: copy.wait_send())
         for slot in range(4):
             self.core_copy(unit, slot, slot == 0).wait_send()
             other = self.whole_part(unit, self.owner_of(slot), 1 - self.core)
@@ -1633,14 +1746,14 @@
                 device_id=self.sibling, device_id_type=MESH_ID,
             ).wait_recv()
         for slot in (1, 2, 3):
-            self.forwards(unit, slot, lambda copy: copy.wait_send())
+            self.line_copy(unit, slot).wait_send()
             for copy in self.plane_copies(unit, slot) + self.corner_copies(unit, slot):
                 copy.wait_send()
 
 
 def gather_semaphores(number):
     dma = pltpu.SemaphoreType.DMA
-    return [dma((number, 5, 5)), dma((number, 3, 5)), dma((number, 4)), dma((number, 4)), dma((number,))]
+    return [dma((number, 3, 5)), dma((number, 3, 5)), dma((number, 4)), dma((number, 4)), dma((number,))]
 
 
 def gather_kernel(kinds, split, *refs):
@@ -1675,10 +1788,12 @@
     schedule = {
         0: [(work.begin, 0), (work.begin, 1)],
         2: [(line, 0), (work.begin, 2)],
-        4: [(line, 1), (plane, 0), (work.begin, 3)],
-        6: [(line, 2), (plane, 1), (pair, 0)],
-        8: [(line, 3), (plane, 2), (pair, 1)],
-        10: [(plane, 3), (pair, 2)],
+        3: [(line, 1), (work.begin, 3)],
+        5: [(plane, 0), (line, 2)],
+        6: [(plane, 1), (line, 3)],
+        8: [(pair, 0), (plane, 2)],
+        9: [(pair, 1), (plane, 3)],
+        10: [(pair, 2)],
         11: [(pair, 3)] + [(work.end, unit) for unit in range(4)],
     }
     for when, actions in schedule.items():
@@ -1874,8 +1989,9 @@
     grad_mods, reduced, outgoing = [None] * LAYERS, [None] * LAYERS, [None] * LAYERS
     for layer in reversed(range(LAYERS)):
         tokens, g4, normed, qkv, attended, branch, middle, n2, active, slope, mixed = saved[layer]
-        dup, ddn, dex, gn2, grad_gate = ffn_backward(
-            layer, grad, n2, mods[layer], g4, mixed, active, slope, lin_all, lout_all[layer], expert_all[layer], halves
+        early = () if outgoing[1] is None else (outgoing[1][0].reshape((-1, halves) + pairs[0].shape),)
+        dup, ddn, dex, gn2, grad_gate, *begun = ffn_backward(
+            layer, grad, n2, mods[layer], g4, mixed, active, slope, lin_all, lout_all[layer], expert_all[layer], halves, early
         )
         grad, grad_mods[layer], dqkvo = attn_backward(
             layer, gn2, grad, middle, tokens, normed, qkv, attended, branch, mods[layer], grad_gate, lin_all,
@@ -1936,6 +2052,7 @@
             outer(window, cond_f),
             states,
             stem_delta if layer == 1 else None,
+            begun if layer == 1 else (),
         )
     stem_total = reduced[1][6]
     group_count = lax.axis_size(GROUP)

time: 796 us -> 767 us (0.964)
  Pallas kernels: 751 us -> 723 us
    pallas_call x2, Pallas kernels: 297 us -> 265 us  [reduce_layer(): pl.pallas_call(functools.partial(reduce_kernel, layer, bool(stems)), out_...]
    pallas_call x2, Pallas kernels: 99.4 us -> 109 us  [ffn_backward(): pl.pallas_call(functools.partial(ffn_bwd_kernel, shared_steps, halves, le...]
where the time goes in v4:
time: 767 us; the launch traced here: 761 us
  Pallas kernels  723 us (94%)
  local copies, waits for them, and re-layouts  16.9 us (2%)
  other arithmetic  12.2 us (2%)
  matrix products  8.21 us (1%)
    pallas_call x2, Pallas kernels, reduce_layer(): pl.pallas_call(functools.partial(reduce_kernel, layer, bool(stems)), out_...  265 us
    pallas_call x1, Pallas kernels, gather_weights(): pl.pallas_call(functools.partial(gather_kernel, kinds, split), out_shape=...  112 us
    pallas_call x2, Pallas kernels, ffn_backward(): pl.pallas_call(functools.partial(ffn_bwd_kernel, shared_steps, halves, le...  109 us
    pallas_call x2, Pallas kernels, ffn_forward(): pl.pallas_call(functools.partial(ffn_fwd_kernel, shared_steps, halves, le...  102 us
    pallas_call x2, Pallas kernels, attn_backward(): pl.pallas_call(attn_bwd_kernel, grid=(count // PATCHES,), in_specs=[rows_...  47.6 us
    pallas_call x3, Pallas kernels, update_arrays(): pl.pallas_call(functools.partial(update_kernel, lax.axis_size(GROUP)), gr...  34.2 us
    pallas_call x2, Pallas kernels, attn_forward(): pl.pallas_call(attn_fwd_kernel, grid=(count // PATCHES,), in_specs=[rows_...  21.4 us

profile of v4, /device:TPU:0, one launch (start us, length us, event | category | flops | bytes accessed | tf_op | source)
XLA Modules:
  0.0 761.4 jit_solution(13507911291151469197)
XLA Ops:
  0.7 1.0 multiply_sine_fusion.1
  1.9 1.1 bitcast_convert_fusion
  3.0 0.7 constant_dynamic-update-slice_fusion.2
  4.1 1.2 bitcast_convert_fusion.1.refs_1_
  5.4 0.9 slice_bitcast_fusion.2
  6.3 1.1 copy-done.1
  7.6 1.6 slice_bitcast_fusion
  9.1 112.4 %gather_weights.1 = (bf16[8,48,3072]{2,1,0:T(8,128)(2,1)}, bf16[2,8,864,384]{3,2,1,0:T(8,128)(2,1)}, bf16[8,384,384]{2,1,0:T(8,128)(2,1)}, bf16[8,384,384]{2,1,0:T(8,128)(2,1)}, bf16[8,2,384,768]{3,2,1,0:T(8,128)(2,1)}) custom-call(bf16[48,3072]{1,0:T(8,128)(2,1)} %copy-done.8, bf16[2,864,384]{2,1,0:T(8,128)(2,1)} %bitcast_convert_fusion.1.refs_1_, ...), custom_call_target="tpu_custom_call" | custom-call | tf_op jit(solution)/shard_map/gather_weights/pallas_call | solution.py:1819
  121.6 2.4 bitcast_add_fusion.x_ref
  124.2 0.6 select_maximum_fusion.feat_ref
  124.9 0.6 convert_convert_fusion.1.hot_ref
  125.5 6.0 cond_forward.1
  131.5 1.6 slice_bitcast_fusion.5
  133.1 10.7 %attention_forward.2 = (bf16[1024,384]{1,0:T(8,128)(2,1)}, bf16[1024,1152]{1,0:T(8,128)(2,1)}, bf16[1024,384]{1,0:T(8,128)(2,1)}, f32[1024,384]{1,0:T(8,128)}, f...) custom-call(f32[1024,384]{1,0:T(8,128)} %bitcast_add_fusion.x_ref, f32[8,2304]{1,0:T(8,128)} %get-tuple-element.293.mods_ref, ...), custom_call_target="tpu_custom_call" | custom-call | flops 10871635968 | bytes 6291456 | tf_op jit(solution)/shard_map/attention_forward/pallas_call | solution.py:1063
  143.9 1.0 copy.87.g4_ref
  144.9 61.5 %ffn_forward.2 = (bf16[12,1024,768]{2,1,0:T(8,128)(2,1)}, bf16[12,1024,768]{2,1,0:T(8,128)(2,1)}, f32[1024,384]{1,0:T(8,128)}, f32[1024,384]{1,0:T(8,128)}, bf16[8,2,384,768]{3,2,1,0:T(8,128)(2,1)}) custom-call(bf16[1024,384]{1,0:T(8,128)(2,1)} %get-tuple-element.111.n2_ref, f32[1024,384]{1,0:T(8,128)} %get-tuple-element.112.mid_ref, ...), custom_call_target="tpu_custom_call" | custom-call | flops 57982058496 | bytes 75497472 | tf_op jit(solution)/shard_map/ffn_forward/pallas_call | solution.py:1118
  206.4 10.7 %attention_forward.3 = (bf16[1024,384]{1,0:T(8,128)(2,1)}, bf16[1024,1152]{1,0:T(8,128)(2,1)}, bf16[1024,384]{1,0:T(8,128)(2,1)}, f32[1024,384]{1,0:T(8,128)}, f...) custom-call(f32[1024,384]{1,0:T(8,128)} %get-tuple-element.115.x_ref, f32[8,2304]{1,0:T(8,128)} %get-tuple-element.292.mods_ref, ...), custom_call_target="tpu_custom_call" | custom-call | flops 10871635968 | bytes 6291456 | tf_op jit(solution)/shard_map/attention_forward/pallas_call | solution.py:1063
  217.1 1.0 copy.88.g4_ref
  218.2 40.8 %ffn_forward.3 = (bf16[12,1024,768]{2,1,0:T(8,128)(2,1)}, bf16[12,1024,768]{2,1,0:T(8,128)(2,1)}, f32[1024,384]{1,0:T(8,128)}, f32[1024,384]{1,0:T(8,128)}) custom-call(bf16[1024,384]{1,0:T(8,128)(2,1)} %get-tuple-element.116.n2_ref, f32[1024,384]{1,0:T(8,128)} %get-tuple-element.117.mid_ref, f32[8,2304]{1,0:T(8,128)} %get-tuple-element.292.mods_ref, ...), custom_call_target="tpu_custom_call" | custom-call | flops 57982058496 | bytes 75497472 | tf_op jit(solution)/shard_map/ffn_forward/pallas_call | solution.py:1118
  258.9 0.9 slice_bitcast_fusion.4
  259.8 0.7 copy.89.fo_ref
  260.5 5.3 final_step.1
  265.9 1.3 convert.69
  267.2 49.5 %ffn_backward.2 = (bf16[3456,384]{1,0:T(8,128)(2,1)}, bf16[3072,384]{1,0:T(8,128)(2,1)}, bf16[8,2,384,768]{3,2,1,0:T(8,128)(2,1)}, f32[1024,384]{1,0:T(8,128)}, f32[8,384]{1,0:T(8,128)}) custom-call(f32[1024,384]{1,0:T(8,128)} %get-tuple-element.122.g_ref, bf16[1024,384]{1,0:T(8,128)(2,1)} %get-tuple-element.116.n2_ref, ...), custom_call_target="tpu_custom_call" | custom-call | flops 57982058496 | bytes 75497472 | tf_op jit(solution)/shard_map/ffn_backward/pallas_call | solution.py:1150
  316.7 23.7 %attention_backward.2 = (f32[1024,384]{1,0:T(8,128)}, f32[8,2304]{1,0:T(8,128)}, bf16[1728,384]{1,0:T(8,128)(2,1)}) custom-call(f32[1024,384]{1,0:T(8,128)} %get-tuple-element.126.gn2_ref, f32[1024,384]{1,0:T(8,128)} %get-tuple-element.122.g_ref, f32[1024,384]{1,0:T(8,128)} %get-tuple-element.117.mid_ref, f32[1024,384]{1,0:T(8,128)} %get-tuple-element.115.x_ref, ...), custom_call_target="tpu_custom_call" | custom-call | flops 26575110144 | bytes 6291456 | tf_op jit(solution)/shard_map/attention_backward/pallas_call | solution.py:1088
  340.4 59.4 %ffn_backward.3 = (bf16[3456,384]{1,0:T(8,128)(2,1)}, bf16[3072,384]{1,0:T(8,128)(2,1)}, bf16[8,2,384,768]{3,2,1,0:T(8,128)(2,1)}, f32[1024,384]{1,0:T(8,128)}, ...) custom-call(f32[1024,384]{1,0:T(8,128)} %get-tuple-element.132.g_ref, ...), custom_call_target="tpu_custom_call" | custom-call | flops 57982058496 | bytes 75497472 | tf_op jit(solution)/shard_map/ffn_backward/pallas_call | solution.py:1150
  399.8 23.9 %attention_backward.3 = (f32[1024,384]{1,0:T(8,128)}, f32[8,2304]{1,0:T(8,128)}, bf16[1728,384]{1,0:T(8,128)(2,1)}) custom-call(f32[1024,384]{1,0:T(8,128)} %get-tuple-element.137.gn2_ref, f32[1024,384]{1,0:T(8,128)} %get-tuple-element.132.g_ref, f32[1024,384]{1,0:T(8,128)} %get-tuple-element.112.mid_ref, f32[1024,384]{1,0:T(8,128)} %bitcast_add_fusion.x_ref, ...), custom_call_target="tpu_custom_call" | custom-call | flops 26575110144 | bytes 6291456 | tf_op jit(solution)/shard_map/attention_backward/pallas_call | solution.py:1088
  423.7 1.6 fusion
  425.3 0.7 constant_dynamic-update-slice_fusion.12
  426.0 0.9 constant_dynamic-update-slice_fusion.11
  426.9 0.9 constant_dynamic-update-slice_fusion.10
  427.8 0.7 constant_dynamic-update-slice_fusion.9
  428.6 5.1 cond_backward.1
  433.7 0.7 constant_dynamic-update-slice_fusion.8
  434.4 0.7 constant_dynamic-update-slice_fusion.7
  435.1 0.7 constant_dynamic-update-slice_fusion.6
  436.8 14.1 %exchange_small.1 = (bf16[8,16,2688]{2,1,0:T(8,128)(2,1)S(1)}, f32[8,128]{1,0:T(8,128)S(1)}) custom-call(bf16[16,2688]{1,0:T(8,128)(2,1)S(1)} %reshape.236.packed, f32[8,128]{1,0:T(8,128)S(1)} %pad.54.loss), custom_call_target="tpu_custom_call" | custom-call | tf_op jit(solution)/shard_map/exchange_small/pallas_call | solution.py:1900
  450.8 0.6 reduce_sum.38
  452.0 1.6 fusion.15.extra
  455.6 1.3 fusion.10
  457.0 0.7 pad.56.rest_2_
  457.7 114.1 %reduce_layer.2 = (f32[2,384,768]{2,1,0:T(8,128)}, f32[864,384]{1,0:T(8,128)}, f32[384,384]{1,0:T(8,128)}, f32[2,384,768]{2,1,0:T(8,128)}, f32[864,384]{1,0:T(8,...) custom-call(bf16[4,2,2,384,768]{4,3,2,1,0:T(8,128)(2,1)} %bitcast.192, bf16[2,864,384]{2,1,0:T(8,128)(2,1)} %bitcast.206, ...), custom_call_target="tpu_custom_call" | custom-call | tf_op jit(solution)/shard_map/reduce_layer/pallas_call | solution.py:1606
  571.8 2.2 convert_bitcast_fusion
  574.0 1.5 fusion.16.extra
  575.6 151.3 %reduce_layer.3 = (f32[2,384,768]{2,1,0:T(8,128)}, f32[864,384]{1,0:T(8,128)}, f32[384,384]{1,0:T(8,128)}, f32[2,384,768]{2,1,0:T(8,128)}, f32[864,384]{1,0:T(8,128)}, /*index=5*/f32[384,384]{1,0:T(8,128)}) custom-call(bf16[4,2,2,384,768]{4,3,2,1,0:T(8,128)(2,1)} %bitcast.193, bf16[2,864,384]{2,1,0:T(8,128)(2,1)} %bitcast.207, ...), custom_call_target="tpu_custom_call" | custom-call | tf_op jit(solution)/shard_map/reduce_layer/pallas_call | solution.py:1606
  726.9 10.2 %update_arrays.3 = (f32[2,864,384]{2,1,0:T(8,128)}, bf16[2,864,384]{2,1,0:T(8,128)(2,1)}, f32[2,864,384]{2,1,0:T(8,128)}, f32[2,864,384]{2,1,0:T(8,128)}, f32[2,864,384]{2,1,0:T(8,128)}) custom-call(f32[864,384]{1,0:T(8,128)} %get-tuple-element.166.grad_a, f32[864,384]{1,0:T(8,128)} %get-tuple-element.167.grad_b, f32[864,384]{1,0:T(8,128)} %get-tuple-element.168.total_a, ...), custom_call_target="tpu_custom_call" | custom-call | tf_op jit(solution)/shard_map/update_arrays/pallas_call | solution.py:1226
  737.1 5.9 update_arrays.4
  743.0 18.1 %update_arrays.5 = (f32[2,768,768]{2,1,0:T(8,128)}, bf16[2,768,768]{2,1,0:T(8,128)(2,1)}, f32[2,768,768]{2,1,0:T(8,128)}, f32[2,768,768]{2,1,0:T(8,128)}, f32[2,768,768]{2,1,0:T(8,128)}) custom-call(f32[768,768]{1,0:T(8,128)} %bitcast.204, f32[768,768]{1,0:T(8,128)} %bitcast.202, f32[768,768]{1,0:T(8,128)} %bitcast.205, f32[768,768]{1,0:T(8,128)} %bitcast.203, ...), custom_call_target="tpu_custom_call" | custom-call | tf_op jit(solution)/shard_map/update_arrays/pallas_call | solution.py:1226
  (91 shorter events, 4.7 us)
Async XLA Ops:
  0.7 120.9 %copy-start = (bf16[1024,16]{0,1:T(8,128)(2,1)S(1)}, bf16[1024,16]{0,1:T(8,128)(2,1)}, u32[]{:S(2)}) copy-start(bf16[1024,16]{0,1:T(8,128)(2,1)} %param.22) | copy-start | bytes 98308
  0.7 3.4 copy-start.2
  3.7 1.7 copy-start.3
  4.1 1.3 copy-start.8
  4.1 3.2 copy-start.1
  9.1 114.9 %copy-start.19 = (s32[4]{0:T(128)S(1)}, s32[4]{0:T(128)}, u32[]{:S(2)}) copy-start(s32[4]{0:T(128)} %param.24) | copy-start | bytes 52
  9.1 115.6 %copy-start.17 = (s32[4]{0:T(128)S(1)}, s32[4]{0:T(128)}, u32[]{:S(2)}) copy-start(s32[4]{0:T(128)} %param.25) | copy-start | bytes 52
  124.0 7.5 copy-start.13
  124.0 7.5 copy-start.15
  133.1 10.7 %copy-start.10 = (f32[2,1024,2]{1,2,0:T(2,128)S(1)}, f32[2,1024,2]{1,2,0:T(2,128)}, u32[]{:S(2)}) copy-start(f32[2,1024,2]{1,2,0:T(2,128)} %param.27) | copy-start | bytes 49156
  133.1 10.7 %copy-start.11 = (s32[2,1024,2]{1,2,0:T(2,128)S(1)}, s32[2,1024,2]{1,2,0:T(2,128)}, u32[]{:S(2)}) copy-start(s32[2,1024,2]{1,2,0:T(2,128)} %param.26) | copy-start | bytes 49156
  399.7 25.5 %copy-start.9 = (bf16[16,384]{1,0:T(8,128)(2,1)S(1)}, bf16[16,384]{1,0:T(8,128)(2,1)}, u32[]{:S(2)}) copy-start(bf16[16,384]{1,0:T(8,128)(2,1)} %convert.69) | copy-start | bytes 36868
  428.6 7.3 copy-start.14
  428.6 7.3 copy-start.16
  428.6 7.6 copy-start.18
  428.6 8.1 %copy-start.12 = (f32[16,1]{1,0:T(8,128)S(1)}, f32[16,1]{1,0:T(8,128)}, u32[]{:S(2)}) copy-start(f32[16,1]{1,0:T(8,128)} %get-tuple-element.153) | copy-start | bytes 196
  452.0 3.6 copy-start.4
  452.0 3.6 copy-start.5
  452.0 3.6 copy-start.6
  457.7 114.1 %copy-start.7 = (f32[2441,48]{0,1:T(8,128)S(1)}, f32[2441,48]{0,1:T(8,128)}, u32[]{:S(2)}) copy-start(f32[2441,48]{0,1:T(8,128)} %param.40) | copy-start | bytes 1406020

commit v5 on v4

--- a/solution.py
+++ b/solution.py
@@ -683,18 +683,17 @@
     normed_ref[...] = normed
     qkv_ref[...] = dot_nt(normed, w_ref[0 : 3 * D, :]).astype(bf16)
     lane, masks = head_masks()
+    heads = [(pair, half) for pair in range(HEADS // 2) for half in range(2)]
+
+    def part(place, pair):
+        return qkv_ref[:, place * D + pair * 128 : place * D + pair * 128 + 128]
+
+    all_scores = [dot_nt(part(0, pair) * (masks[half] * jnp.asarray(0.125, bf16)), part(1, pair)) for pair, half in heads]
+    powers = [jnp.exp(scores - jnp.max(scores, axis=-1, keepdims=True)) for scores in all_scores]
+    probs = [(power * (1.0 / jnp.sum(power, axis=-1, keepdims=True))).astype(bf16) for power in powers]
+    outs = [dot_nn(prob, part(2, pair)) for prob, (pair, _) in zip(probs, heads)]
     for pair in range(HEADS // 2):
-        at = pair * 128
-        queries = qkv_ref[:, at : at + 128]
-        keys = qkv_ref[:, D + at : D + at + 128]
-        vals = qkv_ref[:, 2 * D + at : 2 * D + at + 128]
-        outs = []
-        for half in range(2):
-            scores = dot_nt(queries * masks[half], keys) * 0.125
-            powers = jnp.exp(scores - jnp.max(scores, axis=-1, keepdims=True))
-            probs = (powers * (1.0 / jnp.sum(powers, axis=-1, keepdims=True))).astype(bf16)
-            outs.append(dot_nn(probs, vals))
-        att_ref[:, at : at + 128] = jnp.where(lane < 64, outs[0], outs[1]).astype(bf16)
+        att_ref[:, pair * 128 : pair * 128 + 128] = jnp.where(lane < 64, outs[2 * pair], outs[2 * pair + 1]).astype(bf16)
     branch = dot_nt(att_ref[...], w_ref[3 * D : 4 * D, :])
     branch_ref[...] = branch
     middle = tokens + mod_row(mods_ref, item, 2) * branch
@@ -725,26 +724,31 @@
     acc[3 * D : 4 * D, :] += dot_tn(grad_branch, att_ref[...])
     grad_att = dot_nn(grad_branch, w_ref[3 * D : 4 * D, :]).astype(bf16)
     lane, masks = head_masks()
+    heads = [(pair, half) for pair in range(HEADS // 2) for half in range(2)]
+
+    def part(place, pair):
+        return qkv_ref[:, place * D + pair * 128 : place * D + pair * 128 + 128]
+
+    outs = [grad_att[:, pair * 128 : pair * 128 + 128] for pair in range(HEADS // 2)]
+    all_scores = [dot_nt(part(0, pair) * (masks[half] * jnp.asarray(0.125, bf16)), part(1, pair)) for pair, half in heads]
+    all_grads = [dot_nt(outs[pair] * masks[half], part(2, pair)) for pair, half in heads]
+    powers = [jnp.exp(scores - jnp.max(scores, axis=-1, keepdims=True)) for scores in all_scores]
+    probs = [power * (1.0 / jnp.sum(power, axis=-1, keepdims=True)) for power in powers]
+    halved = [prob.astype(bf16) for prob in probs]
+    grad_scores = [
+        (prob * (grads - jnp.sum(prob * grads, axis=-1, keepdims=True))).astype(bf16)
+        for prob, grads in zip(probs, all_grads)
+    ]
     for pair in range(HEADS // 2):
         at = pair * 128
-        queries = qkv_ref[:, at : at + 128]
-        keys = qkv_ref[:, D + at : D + at + 128]
-        vals = qkv_ref[:, 2 * D + at : 2 * D + at + 128]
-        grad_out = grad_att[:, at : at + 128]
-        parts = []
-        for half in range(2):
-            scores = dot_nt(queries * masks[half], keys) * 0.125
-            powers = jnp.exp(scores - jnp.max(scores, axis=-1, keepdims=True))
-            probs = powers * (1.0 / jnp.sum(powers, axis=-1, keepdims=True))
-            grad_vals = dot_tn(probs.astype(bf16), grad_out)
-            grad_probs = dot_nt(grad_out * masks[half], vals)
-            inner = jnp.sum(probs * grad_probs, axis=-1, keepdims=True)
-            grad_scores = (probs * (grad_probs - inner)).astype(bf16)
-            parts.append((dot_nn(grad_scores, keys) * 0.125, dot_tn(grad_scores, queries) * 0.125, grad_vals))
-        for place in range(3):
-            dqkv[:, place * D + at : place * D + at + 128] = jnp.where(
-                lane < 64, parts[0][place], parts[1][place]
-            ).astype(bf16)
+        two = (2 * pair, 2 * pair + 1)
+        results = (
+            [dot_nn(grad_scores[head], part(1, pair)) * 0.125 for head in two],
+            [dot_tn(grad_scores[head], part(0, pair)) * 0.125 for head in two],
+            [dot_tn(halved[head], outs[pair]) for head in two],
+        )
+        for place, (low, high) in enumerate(results):
+            dqkv[:, place * D + at : place * D + at + 128] = jnp.where(lane < 64, low, high).astype(bf16)
     acc[0 : 3 * D, :] += dot_tn(dqkv[...], normed_ref[...])
     grad_normed = dot_nn(dqkv[...], w_ref[0 : 3 * D, :])
     grad_in, dshift, dscale = norm_back(x_ref[...], mod_row(mods_ref, item, 1), grad_normed)
@@ -1787,12 +1791,15 @@
     line, plane, pair = work.along_line, work.in_plane, work.to_sibling
     schedule = {
         0: [(work.begin, 0), (work.begin, 1)],
-        2: [(line, 0), (work.begin, 2)],
-        3: [(line, 1), (work.begin, 3)],
-        5: [(plane, 0), (line, 2)],
-        6: [(plane, 1), (line, 3)],
-        8: [(pair, 0), (plane, 2)],
-        9: [(pair, 1), (plane, 3)],
+        1: [(work.begin, 2)],
+        2: [(work.begin, 3)],
+        3: [(line, 0)],
+        4: [(line, 1)],
+        5: [(plane, 0)],
+        6: [(line, 2), (plane, 1)],
+        7: [(line, 3), (pair, 0)],
+        8: [(plane, 2)],
+        9: [(plane, 3), (pair, 1)],
         10: [(pair, 2)],
         11: [(pair, 3)] + [(work.end, unit) for unit in range(4)],
     }

time: 767 us -> 750 us (0.978)
  Pallas kernels: 723 us -> 706 us
    pallas_call x2, Pallas kernels: 47.6 us -> 34.2 us  [attn_backward(): pl.pallas_call(attn_bwd_kernel, grid=(count // PATCHES,), in_specs=[rows_...]
where the time goes in v5:
time: 750 us; the launch traced here: 745 us
  Pallas kernels  706 us (94%)
  local copies, waits for them, and re-layouts  16.9 us (2%)
  other arithmetic  12.2 us (2%)
  matrix products  8.2 us (1%)
    pallas_call x2, Pallas kernels, reduce_layer(): pl.pallas_call(functools.partial(reduce_kernel, layer, bool(stems)), out_...  265 us
    pallas_call x1, Pallas kernels, gather_weights(): pl.pallas_call(functools.partial(gather_kernel, kinds, split), out_shape=...  112 us
    pallas_call x2, Pallas kernels, ffn_backward(): pl.pallas_call(functools.partial(ffn_bwd_kernel, shared_steps, halves, le...  109 us
    pallas_call x2, Pallas kernels, ffn_forward(): pl.pallas_call(functools.partial(ffn_fwd_kernel, shared_steps, halves, le...  101 us
    pallas_call x3, Pallas kernels, update_arrays(): pl.pallas_call(functools.partial(update_kernel, lax.axis_size(GROUP)), gr...  34.2 us
    pallas_call x2, Pallas kernels, attn_backward(): pl.pallas_call(attn_bwd_kernel, grid=(count // PATCHES,), in_specs=[rows_...  34.2 us
    pallas_call x2, Pallas kernels, attn_forward(): pl.pallas_call(attn_fwd_kernel, grid=(count // PATCHES,), in_specs=[rows_...  18.9 us

profile of v5, /device:TPU:0, one launch (start us, length us, event | category | flops | bytes accessed | tf_op | source)
XLA Modules:
  0.0 744.8 jit_solution(8089748171003767216)
XLA Ops:
  0.7 1.0 multiply_sine_fusion.1
  1.9 1.1 bitcast_convert_fusion
  3.0 0.7 constant_dynamic-update-slice_fusion.2
  4.1 1.2 bitcast_convert_fusion.1.refs_1_
  5.4 0.9 slice_bitcast_fusion.2
  6.3 1.1 copy-done.1
  7.6 1.6 slice_bitcast_fusion
  9.1 112.4 %gather_weights.1 = (bf16[8,48,3072]{2,1,0:T(8,128)(2,1)}, bf16[2,8,864,384]{3,2,1,0:T(8,128)(2,1)}, bf16[8,384,384]{2,1,0:T(8,128)(2,1)}, bf16[8,384,384]{2,1,0:T(8,128)(2,1)}, bf16[8,2,384,768]{3,2,1,0:T(8,128)(2,1)}) custom-call(bf16[48,3072]{1,0:T(8,128)(2,1)} %copy-done.8, bf16[2,864,384]{2,1,0:T(8,128)(2,1)} %bitcast_convert_fusion.1.refs_1_, ...), custom_call_target="tpu_custom_call" | custom-call | tf_op jit(solution)/shard_map/gather_weights/pallas_call | solution.py:1826
  121.6 2.4 bitcast_add_fusion.x_ref
  124.2 0.6 select_maximum_fusion.feat_ref
  124.9 0.6 convert_convert_fusion.1.hot_ref
  125.5 6.0 cond_forward.1
  131.5 1.6 slice_bitcast_fusion.5
  133.1 9.5 %attention_forward.2 = (bf16[1024,384]{1,0:T(8,128)(2,1)}, bf16[1024,1152]{1,0:T(8,128)(2,1)}, bf16[1024,384]{1,0:T(8,128)(2,1)}, f32[1024,384]{1,0:T(8,128)}, f...) custom-call(f32[1024,384]{1,0:T(8,128)} %bitcast_add_fusion.x_ref, f32[8,2304]{1,0:T(8,128)} %get-tuple-element.293.mods_ref, ...), custom_call_target="tpu_custom_call" | custom-call | flops 10871635968 | bytes 6291456 | tf_op jit(solution)/shard_map/attention_forward/pallas_call | solution.py:1067
  142.6 1.0 copy.87.g4_ref
  143.7 60.8 %ffn_forward.2 = (bf16[12,1024,768]{2,1,0:T(8,128)(2,1)}, bf16[12,1024,768]{2,1,0:T(8,128)(2,1)}, f32[1024,384]{1,0:T(8,128)}, f32[1024,384]{1,0:T(8,128)}, bf16[8,2,384,768]{3,2,1,0:T(8,128)(2,1)}) custom-call(bf16[1024,384]{1,0:T(8,128)(2,1)} %get-tuple-element.111.n2_ref, f32[1024,384]{1,0:T(8,128)} %get-tuple-element.112.mid_ref, ...), custom_call_target="tpu_custom_call" | custom-call | flops 57982058496 | bytes 75497472 | tf_op jit(solution)/shard_map/ffn_forward/pallas_call | solution.py:1122
  204.5 9.5 %attention_forward.3 = (bf16[1024,384]{1,0:T(8,128)(2,1)}, bf16[1024,1152]{1,0:T(8,128)(2,1)}, bf16[1024,384]{1,0:T(8,128)(2,1)}, f32[1024,384]{1,0:T(8,128)}, f...) custom-call(f32[1024,384]{1,0:T(8,128)} %get-tuple-element.115.x_ref, f32[8,2304]{1,0:T(8,128)} %get-tuple-element.292.mods_ref, ...), custom_call_target="tpu_custom_call" | custom-call | flops 10871635968 | bytes 6291456 | tf_op jit(solution)/shard_map/attention_forward/pallas_call | solution.py:1067
  213.9 1.0 copy.88.g4_ref
  215.0 40.6 %ffn_forward.3 = (bf16[12,1024,768]{2,1,0:T(8,128)(2,1)}, bf16[12,1024,768]{2,1,0:T(8,128)(2,1)}, f32[1024,384]{1,0:T(8,128)}, f32[1024,384]{1,0:T(8,128)}) custom-call(bf16[1024,384]{1,0:T(8,128)(2,1)} %get-tuple-element.116.n2_ref, f32[1024,384]{1,0:T(8,128)} %get-tuple-element.117.mid_ref, f32[8,2304]{1,0:T(8,128)} %get-tuple-element.292.mods_ref, ...), custom_call_target="tpu_custom_call" | custom-call | flops 57982058496 | bytes 75497472 | tf_op jit(solution)/shard_map/ffn_forward/pallas_call | solution.py:1122
  255.6 0.9 slice_bitcast_fusion.4
  256.5 0.7 copy.89.fo_ref
  257.1 5.3 final_step.1
  262.5 1.3 convert.69
  263.8 49.9 %ffn_backward.2 = (bf16[3456,384]{1,0:T(8,128)(2,1)}, bf16[3072,384]{1,0:T(8,128)(2,1)}, bf16[8,2,384,768]{3,2,1,0:T(8,128)(2,1)}, f32[1024,384]{1,0:T(8,128)}, f32[8,384]{1,0:T(8,128)}) custom-call(f32[1024,384]{1,0:T(8,128)} %get-tuple-element.122.g_ref, bf16[1024,384]{1,0:T(8,128)(2,1)} %get-tuple-element.116.n2_ref, ...), custom_call_target="tpu_custom_call" | custom-call | flops 57982058496 | bytes 75497472 | tf_op jit(solution)/shard_map/ffn_backward/pallas_call | solution.py:1154
  313.7 17.1 %attention_backward.2 = (f32[1024,384]{1,0:T(8,128)}, f32[8,2304]{1,0:T(8,128)}, bf16[1728,384]{1,0:T(8,128)(2,1)}) custom-call(f32[1024,384]{1,0:T(8,128)} %get-tuple-element.126.gn2_ref, f32[1024,384]{1,0:T(8,128)} %get-tuple-element.122.g_ref, f32[1024,384]{1,0:T(8,128)} %get-tuple-element.117.mid_ref, f32[1024,384]{1,0:T(8,128)} %get-tuple-element.115.x_ref, ...), custom_call_target="tpu_custom_call" | custom-call | flops 26575110144 | bytes 6291456 | tf_op jit(solution)/shard_map/attention_backward/pallas_call | solution.py:1092
  330.8 58.9 %ffn_backward.3 = (bf16[3456,384]{1,0:T(8,128)(2,1)}, bf16[3072,384]{1,0:T(8,128)(2,1)}, bf16[8,2,384,768]{3,2,1,0:T(8,128)(2,1)}, f32[1024,384]{1,0:T(8,128)}, ...) custom-call(f32[1024,384]{1,0:T(8,128)} %get-tuple-element.132.g_ref, ...), custom_call_target="tpu_custom_call" | custom-call | flops 57982058496 | bytes 75497472 | tf_op jit(solution)/shard_map/ffn_backward/pallas_call | solution.py:1154
  389.7 17.1 %attention_backward.3 = (f32[1024,384]{1,0:T(8,128)}, f32[8,2304]{1,0:T(8,128)}, bf16[1728,384]{1,0:T(8,128)(2,1)}) custom-call(f32[1024,384]{1,0:T(8,128)} %get-tuple-element.137.gn2_ref, f32[1024,384]{1,0:T(8,128)} %get-tuple-element.132.g_ref, f32[1024,384]{1,0:T(8,128)} %get-tuple-element.112.mid_ref, f32[1024,384]{1,0:T(8,128)} %bitcast_add_fusion.x_ref, ...), custom_call_target="tpu_custom_call" | custom-call | flops 26575110144 | bytes 6291456 | tf_op jit(solution)/shard_map/attention_backward/pallas_call | solution.py:1092
  406.8 1.6 fusion
  408.5 0.7 constant_dynamic-update-slice_fusion.12
  409.2 0.9 constant_dynamic-update-slice_fusion.11
  410.1 0.9 constant_dynamic-update-slice_fusion.10
  411.0 0.7 constant_dynamic-update-slice_fusion.9
  411.8 5.3 cond_backward.1
  417.1 0.7 constant_dynamic-update-slice_fusion.8
  417.8 0.7 constant_dynamic-update-slice_fusion.7
  418.5 0.7 constant_dynamic-update-slice_fusion.6
  420.1 14.1 %exchange_small.1 = (bf16[8,16,2688]{2,1,0:T(8,128)(2,1)S(1)}, f32[8,128]{1,0:T(8,128)S(1)}) custom-call(bf16[16,2688]{1,0:T(8,128)(2,1)S(1)} %reshape.236.packed, f32[8,128]{1,0:T(8,128)S(1)} %pad.54.loss), custom_call_target="tpu_custom_call" | custom-call | tf_op jit(solution)/shard_map/exchange_small/pallas_call | solution.py:1907
  434.3 0.6 reduce_sum.38
  435.5 1.5 fusion.15.extra
  439.1 1.3 fusion.10
  440.4 0.7 pad.56.rest_2_
  441.1 114.1 %reduce_layer.2 = (f32[2,384,768]{2,1,0:T(8,128)}, f32[864,384]{1,0:T(8,128)}, f32[384,384]{1,0:T(8,128)}, f32[2,384,768]{2,1,0:T(8,128)}, f32[864,384]{1,0:T(8,...) custom-call(bf16[4,2,2,384,768]{4,3,2,1,0:T(8,128)(2,1)} %bitcast.192, bf16[2,864,384]{2,1,0:T(8,128)(2,1)} %bitcast.206, ...), custom_call_target="tpu_custom_call" | custom-call | tf_op jit(solution)/shard_map/reduce_layer/pallas_call | solution.py:1610
  555.2 2.2 convert_bitcast_fusion
  557.4 1.5 fusion.16.extra
  559.0 151.3 %reduce_layer.3 = (f32[2,384,768]{2,1,0:T(8,128)}, f32[864,384]{1,0:T(8,128)}, f32[384,384]{1,0:T(8,128)}, f32[2,384,768]{2,1,0:T(8,128)}, f32[864,384]{1,0:T(8,128)}, /*index=5*/f32[384,384]{1,0:T(8,128)}) custom-call(bf16[4,2,2,384,768]{4,3,2,1,0:T(8,128)(2,1)} %bitcast.193, bf16[2,864,384]{2,1,0:T(8,128)(2,1)} %bitcast.207, ...), custom_call_target="tpu_custom_call" | custom-call | tf_op jit(solution)/shard_map/reduce_layer/pallas_call | solution.py:1610
  710.3 10.2 %update_arrays.3 = (f32[2,864,384]{2,1,0:T(8,128)}, bf16[2,864,384]{2,1,0:T(8,128)(2,1)}, f32[2,864,384]{2,1,0:T(8,128)}, f32[2,864,384]{2,1,0:T(8,128)}, f32[2,864,384]{2,1,0:T(8,128)}) custom-call(f32[864,384]{1,0:T(8,128)} %get-tuple-element.166.grad_a, f32[864,384]{1,0:T(8,128)} %get-tuple-element.167.grad_b, f32[864,384]{1,0:T(8,128)} %get-tuple-element.168.total_a, ...), custom_call_target="tpu_custom_call" | custom-call | tf_op jit(solution)/shard_map/update_arrays/pallas_call | solution.py:1230
  720.5 5.9 update_arrays.4
  726.4 18.1 %update_arrays.5 = (f32[2,768,768]{2,1,0:T(8,128)}, bf16[2,768,768]{2,1,0:T(8,128)(2,1)}, f32[2,768,768]{2,1,0:T(8,128)}, f32[2,768,768]{2,1,0:T(8,128)}, f32[2,768,768]{2,1,0:T(8,128)}) custom-call(f32[768,768]{1,0:T(8,128)} %bitcast.204, f32[768,768]{1,0:T(8,128)} %bitcast.202, f32[768,768]{1,0:T(8,128)} %bitcast.205, f32[768,768]{1,0:T(8,128)} %bitcast.203, ...), custom_call_target="tpu_custom_call" | custom-call | tf_op jit(solution)/shard_map/update_arrays/pallas_call | solution.py:1230
  (91 shorter events, 4.7 us)
Async XLA Ops:
  0.7 120.9 %copy-start = (bf16[1024,16]{0,1:T(8,128)(2,1)S(1)}, bf16[1024,16]{0,1:T(8,128)(2,1)}, u32[]{:S(2)}) copy-start(bf16[1024,16]{0,1:T(8,128)(2,1)} %param.22) | copy-start | bytes 98308
  0.7 3.4 copy-start.2
  3.7 1.7 copy-start.3
  4.1 1.3 copy-start.8
  4.1 3.2 copy-start.1
  9.1 114.9 %copy-start.19 = (s32[4]{0:T(128)S(1)}, s32[4]{0:T(128)}, u32[]{:S(2)}) copy-start(s32[4]{0:T(128)} %param.24) | copy-start | bytes 52
  9.1 115.6 %copy-start.17 = (s32[4]{0:T(128)S(1)}, s32[4]{0:T(128)}, u32[]{:S(2)}) copy-start(s32[4]{0:T(128)} %param.25) | copy-start | bytes 52
  124.0 7.5 %copy-start.13 = (f32[128]{0:T(128)}, f32[128]{0:T(128)S(1)}, u32[]{:S(2)}) copy-start(f32[128]{0:T(128)S(1)} %multiply_exponential_fusion) | copy-start | bytes 1540
  124.0 7.5 %copy-start.15 = (f32[4]{0:T(128)}, f32[4]{0:T(128)S(1)}, u32[]{:S(2)}) copy-start(f32[4]{0:T(128)S(1)} %convert_element_type.107) | copy-start | bytes 52
  133.1 9.5 %copy-start.10 = (f32[2,1024,2]{1,2,0:T(2,128)S(1)}, f32[2,1024,2]{1,2,0:T(2,128)}, u32[]{:S(2)}) copy-start(f32[2,1024,2]{1,2,0:T(2,128)} %param.27) | copy-start | bytes 49156
  133.1 9.5 %copy-start.11 = (s32[2,1024,2]{1,2,0:T(2,128)S(1)}, s32[2,1024,2]{1,2,0:T(2,128)}, u32[]{:S(2)}) copy-start(s32[2,1024,2]{1,2,0:T(2,128)} %param.26) | copy-start | bytes 49156
  389.7 18.7 %copy-start.9 = (bf16[16,384]{1,0:T(8,128)(2,1)S(1)}, bf16[16,384]{1,0:T(8,128)(2,1)}, u32[]{:S(2)}) copy-start(bf16[16,384]{1,0:T(8,128)(2,1)} %convert.69) | copy-start | bytes 36868
  411.7 7.5 %copy-start.14 = (f32[128]{0:T(128)S(1)}, f32[128]{0:T(128)}, u32[]{:S(2)}) copy-start(f32[128]{0:T(128)} %copy-done.13) | copy-start | bytes 1540
  411.7 7.5 %copy-start.16 = (f32[4]{0:T(128)S(1)}, f32[4]{0:T(128)}, u32[]{:S(2)}) copy-start(f32[4]{0:T(128)} %copy-done.15) | copy-start | bytes 52
  411.7 7.8 %copy-start.18 = (s32[4]{0:T(128)S(1)}, s32[4]{0:T(128)}, u32[]{:S(2)}) copy-start(s32[4]{0:T(128)} %param.25) | copy-start | bytes 52
  411.7 8.3 %copy-start.12 = (f32[16,1]{1,0:T(8,128)S(1)}, f32[16,1]{1,0:T(8,128)}, u32[]{:S(2)}) copy-start(f32[16,1]{1,0:T(8,128)} %get-tuple-element.153) | copy-start | bytes 196
  435.4 3.6 copy-start.4
  435.4 3.6 copy-start.5
  435.4 3.6 copy-start.6
  441.1 114.1 %copy-start.7 = (f32[2441,48]{0,1:T(8,128)S(1)}, f32[2441,48]{0,1:T(8,128)}, u32[]{:S(2)}) copy-start(f32[2441,48]{0,1:T(8,128)} %param.40) | copy-start | bytes 1406020

commit v6 on v5

--- a/solution.py
+++ b/solution.py
@@ -794,18 +794,20 @@
 
     @pl.when(step < shared_steps)
     def _():
-        for block in range(n2_ref.shape[0] // FWD_ROWS):
-            rows = pl.ds(block * FWD_ROWS, FWD_ROWS)
-            active, slope = gelu_both(dot_nt(n2_ref[rows, :], up_ref[...]))
+        blocks = [pl.ds(block * FWD_ROWS, FWD_ROWS) for block in range(n2_ref.shape[0] // FWD_ROWS)]
+        inners = [dot_nt(n2_ref[rows, :], up_ref[...]) for rows in blocks]
+        for inner, rows in zip(inners, blocks):
+            active, slope = gelu_both(inner)
             act_ref[0, rows, :] = active
             dg_ref[0, rows, :] = slope
             acc[rows, :] += dot_nn(active, dn_ref[...])
 
     @pl.when(step >= shared_steps)
     def _():
-        for block in range(n2_ref.shape[0] // FWD_ROWS):
-            rows = pl.ds(block * FWD_ROWS, FWD_ROWS)
-            active, slope = gelu_both(dot_nn(n2_ref[rows, :], ex_ref[0, 0]))
+        blocks = [pl.ds(block * FWD_ROWS, FWD_ROWS) for block in range(n2_ref.shape[0] // FWD_ROWS)]
+        inners = [dot_nn(n2_ref[rows, :], ex_ref[0, 0]) for rows in blocks]
+        for inner, rows in zip(inners, blocks):
+            active, slope = gelu_both(inner)
             act_ref[0, rows, :] = active
             dg_ref[0, rows, :] = slope
             racc[rows, :] += dot_nt(active, ex_ref[0, 1])
@@ -943,14 +945,16 @@
 
     @pl.when(step < shared_steps)
     def _():
-        for block in range(n2_ref.shape[0] // BWD_ROWS):
-            rows = pl.ds(block * BWD_ROWS, BWD_ROWS)
-            inner = (dot_nt(gs[rows, :], dn_ref[...]) * dg_ref[0, rows, :].astype(f32)).astype(bf16)
+        ddn_ref[...] = dot_nn(gst[...], act_ref[0]).astype(bf16).T
+        blocks = [pl.ds(block * BWD_ROWS, BWD_ROWS) for block in range(n2_ref.shape[0] // BWD_ROWS)]
+        grads = [dot_nt(gs[rows, :], dn_ref[...]) for rows in blocks]
+        inners = [(grad * dg_ref[0, rows, :].astype(f32)).astype(bf16) for grad, rows in zip(grads, blocks)]
+        for inner, rows in zip(inners, blocks):
             din[rows, :] = inner
+        for inner, rows in zip(inners, blocks):
             acc[rows, :] += dot_nn(inner, up_ref[...])
         at = dup_ref.shape[0] - shared_steps * CHUNK + step * CHUNK
         dup_ref[pl.ds(pl.multiple_of(at, D), CHUNK), :] = dot_nn(n2t[...], din[...]).astype(bf16).T
-        ddn_ref[...] = dot_nn(gst[...], act_ref[0]).astype(bf16).T
 
     @pl.when(step >= shared_steps)
     def _():
@@ -964,14 +968,16 @@
                 gs[rows, :] = grad
                 gst[:, rows] = grad.T
 
-        for block in range(n2_ref.shape[0] // BWD_ROWS):
-            rows = pl.ds(block * BWD_ROWS, BWD_ROWS)
-            inner = (dot_nn(gs[rows, :], ex_ref[0, 1]) * dg_ref[0, rows, :].astype(f32)).astype(bf16)
+        dex_ref[0, 1] = dot_nn(gst[...], act_ref[0]).astype(bf16)
+        blocks = [pl.ds(block * BWD_ROWS, BWD_ROWS) for block in range(n2_ref.shape[0] // BWD_ROWS)]
+        grads = [dot_nn(gs[rows, :], ex_ref[0, 1]) for rows in blocks]
+        inners = [(grad * dg_ref[0, rows, :].astype(f32)).astype(bf16) for grad, rows in zip(grads, blocks)]
+        for inner, rows in zip(inners, blocks):
             din[rows, :] = inner
+        for inner, rows in zip(inners, blocks):
             racc[rows, :] += dot_nt(inner, ex_ref[0, 0])
 
         dex_ref[0, 0] = dot_nn(n2t[...], din[...]).astype(bf16)
-        dex_ref[0, 1] = dot_nn(gst[...], act_ref[0]).astype(bf16)
 
         @pl.when(half == halves - 1)
         def _():

time: 750 us -> 746 us (level)
  no operation moved by 1% of the time
where the time goes in v6:
time: 746 us; the launch traced here: 740 us
  Pallas kernels  702 us (94%)
  local copies, waits for them, and re-layouts  16.9 us (2%)
  other arithmetic  12.2 us (2%)
  matrix products  8.21 us (1%)
    pallas_call x2, Pallas kernels, reduce_layer(): pl.pallas_call(functools.partial(reduce_kernel, layer, bool(stems)), out_...  265 us
    pallas_call x1, Pallas kernels, gather_weights(): pl.pallas_call(functools.partial(gather_kernel, kinds, split), out_shape=...  112 us
    pallas_call x2, Pallas kernels, ffn_backward(): pl.pallas_call(functools.partial(ffn_bwd_kernel, shared_steps, halves, le...  108 us
    pallas_call x2, Pallas kernels, ffn_forward(): pl.pallas_call(functools.partial(ffn_fwd_kernel, shared_steps, halves, le...  97.3 us
    pallas_call x2, Pallas kernels, attn_backward(): pl.pallas_call(attn_bwd_kernel, grid=(count // PATCHES,), in_specs=[rows_...  34.3 us
    pallas_call x3, Pallas kernels, update_arrays(): pl.pallas_call(functools.partial(update_kernel, lax.axis_size(GROUP)), gr...  34.2 us
    pallas_call x2, Pallas kernels, attn_forward(): pl.pallas_call(attn_fwd_kernel, grid=(count // PATCHES,), in_specs=[rows_...  18.9 us

profile of v6, /device:TPU:0, one launch (start us, length us, event | category | flops | bytes accessed | tf_op | source)
XLA Modules:
  0.0 740.3 jit_solution(11311682172697271918)
XLA Ops:
  0.7 1.0 multiply_sine_fusion.1
  1.9 1.1 bitcast_convert_fusion
  3.0 0.7 constant_dynamic-update-slice_fusion.2
  4.1 1.2 bitcast_convert_fusion.1.refs_1_
  5.4 0.9 slice_bitcast_fusion.2
  6.3 1.1 copy-done.1
  7.6 1.6 slice_bitcast_fusion
  9.1 112.4 %gather_weights.1 = (bf16[8,48,3072]{2,1,0:T(8,128)(2,1)}, bf16[2,8,864,384]{3,2,1,0:T(8,128)(2,1)}, bf16[8,384,384]{2,1,0:T(8,128)(2,1)}, bf16[8,384,384]{2,1,0:T(8,128)(2,1)}, bf16[8,2,384,768]{3,2,1,0:T(8,128)(2,1)}) custom-call(bf16[48,3072]{1,0:T(8,128)(2,1)} %copy-done.8, bf16[2,864,384]{2,1,0:T(8,128)(2,1)} %bitcast_convert_fusion.1.refs_1_, ...), custom_call_target="tpu_custom_call" | custom-call | tf_op jit(solution)/shard_map/gather_weights/pallas_call | solution.py:1832
  121.6 2.4 bitcast_add_fusion.x_ref
  124.2 0.6 select_maximum_fusion.feat_ref
  124.9 0.6 convert_convert_fusion.1.hot_ref
  125.5 6.0 cond_forward.1
  131.5 1.6 slice_bitcast_fusion.5
  133.1 9.5 %attention_forward.2 = (bf16[1024,384]{1,0:T(8,128)(2,1)}, bf16[1024,1152]{1,0:T(8,128)(2,1)}, bf16[1024,384]{1,0:T(8,128)(2,1)}, f32[1024,384]{1,0:T(8,128)}, f...) custom-call(f32[1024,384]{1,0:T(8,128)} %bitcast_add_fusion.x_ref, f32[8,2304]{1,0:T(8,128)} %get-tuple-element.293.mods_ref, ...), custom_call_target="tpu_custom_call" | custom-call | flops 10871635968 | bytes 6291456 | tf_op jit(solution)/shard_map/attention_forward/pallas_call | solution.py:1073
  142.6 1.0 copy.87.g4_ref
  143.7 59.6 %ffn_forward.2 = (bf16[12,1024,768]{2,1,0:T(8,128)(2,1)}, bf16[12,1024,768]{2,1,0:T(8,128)(2,1)}, f32[1024,384]{1,0:T(8,128)}, f32[1024,384]{1,0:T(8,128)}, bf16[8,2,384,768]{3,2,1,0:T(8,128)(2,1)}) custom-call(bf16[1024,384]{1,0:T(8,128)(2,1)} %get-tuple-element.111.n2_ref, f32[1024,384]{1,0:T(8,128)} %get-tuple-element.112.mid_ref, ...), custom_call_target="tpu_custom_call" | custom-call | flops 57982058496 | bytes 75497472 | tf_op jit(solution)/shard_map/ffn_forward/pallas_call | solution.py:1128
  203.3 9.5 %attention_forward.3 = (bf16[1024,384]{1,0:T(8,128)(2,1)}, bf16[1024,1152]{1,0:T(8,128)(2,1)}, bf16[1024,384]{1,0:T(8,128)(2,1)}, f32[1024,384]{1,0:T(8,128)}, f...) custom-call(f32[1024,384]{1,0:T(8,128)} %get-tuple-element.115.x_ref, f32[8,2304]{1,0:T(8,128)} %get-tuple-element.292.mods_ref, ...), custom_call_target="tpu_custom_call" | custom-call | flops 10871635968 | bytes 6291456 | tf_op jit(solution)/shard_map/attention_forward/pallas_call | solution.py:1073
  212.7 1.0 copy.88.g4_ref
  213.8 37.7 %ffn_forward.3 = (bf16[12,1024,768]{2,1,0:T(8,128)(2,1)}, bf16[12,1024,768]{2,1,0:T(8,128)(2,1)}, f32[1024,384]{1,0:T(8,128)}, f32[1024,384]{1,0:T(8,128)}) custom-call(bf16[1024,384]{1,0:T(8,128)(2,1)} %get-tuple-element.116.n2_ref, f32[1024,384]{1,0:T(8,128)} %get-tuple-element.117.mid_ref, f32[8,2304]{1,0:T(8,128)} %get-tuple-element.292.mods_ref, ...), custom_call_target="tpu_custom_call" | custom-call | flops 57982058496 | bytes 75497472 | tf_op jit(solution)/shard_map/ffn_forward/pallas_call | solution.py:1128
  251.5 0.9 slice_bitcast_fusion.4
  252.4 0.7 copy.89.fo_ref
  253.1 5.3 final_step.1
  258.4 1.3 convert.69
  259.8 49.3 %ffn_backward.2 = (bf16[3456,384]{1,0:T(8,128)(2,1)}, bf16[3072,384]{1,0:T(8,128)(2,1)}, bf16[8,2,384,768]{3,2,1,0:T(8,128)(2,1)}, f32[1024,384]{1,0:T(8,128)}, f32[8,384]{1,0:T(8,128)}) custom-call(f32[1024,384]{1,0:T(8,128)} %get-tuple-element.122.g_ref, bf16[1024,384]{1,0:T(8,128)(2,1)} %get-tuple-element.116.n2_ref, ...), custom_call_target="tpu_custom_call" | custom-call | flops 57982058496 | bytes 75497472 | tf_op jit(solution)/shard_map/ffn_backward/pallas_call | solution.py:1160
  309.0 17.1 %attention_backward.2 = (f32[1024,384]{1,0:T(8,128)}, f32[8,2304]{1,0:T(8,128)}, bf16[1728,384]{1,0:T(8,128)(2,1)}) custom-call(f32[1024,384]{1,0:T(8,128)} %get-tuple-element.126.gn2_ref, f32[1024,384]{1,0:T(8,128)} %get-tuple-element.122.g_ref, f32[1024,384]{1,0:T(8,128)} %get-tuple-element.117.mid_ref, f32[1024,384]{1,0:T(8,128)} %get-tuple-element.115.x_ref, ...), custom_call_target="tpu_custom_call" | custom-call | flops 26575110144 | bytes 6291456 | tf_op jit(solution)/shard_map/attention_backward/pallas_call | solution.py:1098
  326.2 59.1 %ffn_backward.3 = (bf16[3456,384]{1,0:T(8,128)(2,1)}, bf16[3072,384]{1,0:T(8,128)(2,1)}, bf16[8,2,384,768]{3,2,1,0:T(8,128)(2,1)}, f32[1024,384]{1,0:T(8,128)}, ...) custom-call(f32[1024,384]{1,0:T(8,128)} %get-tuple-element.132.g_ref, ...), custom_call_target="tpu_custom_call" | custom-call | flops 57982058496 | bytes 75497472 | tf_op jit(solution)/shard_map/ffn_backward/pallas_call | solution.py:1160
  385.3 17.1 %attention_backward.3 = (f32[1024,384]{1,0:T(8,128)}, f32[8,2304]{1,0:T(8,128)}, bf16[1728,384]{1,0:T(8,128)(2,1)}) custom-call(f32[1024,384]{1,0:T(8,128)} %get-tuple-element.137.gn2_ref, f32[1024,384]{1,0:T(8,128)} %get-tuple-element.132.g_ref, f32[1024,384]{1,0:T(8,128)} %get-tuple-element.112.mid_ref, f32[1024,384]{1,0:T(8,128)} %bitcast_add_fusion.x_ref, ...), custom_call_target="tpu_custom_call" | custom-call | flops 26575110144 | bytes 6291456 | tf_op jit(solution)/shard_map/attention_backward/pallas_call | solution.py:1098
  402.4 1.6 fusion
  404.1 0.7 constant_dynamic-update-slice_fusion.12
  404.8 0.9 constant_dynamic-update-slice_fusion.11
  405.7 0.9 constant_dynamic-update-slice_fusion.10
  406.6 0.7 constant_dynamic-update-slice_fusion.9
  407.3 5.1 cond_backward.1
  412.4 0.7 constant_dynamic-update-slice_fusion.8
  413.2 0.7 constant_dynamic-update-slice_fusion.7
  413.9 0.7 constant_dynamic-update-slice_fusion.6
  415.5 14.3 %exchange_small.1 = (bf16[8,16,2688]{2,1,0:T(8,128)(2,1)S(1)}, f32[8,128]{1,0:T(8,128)S(1)}) custom-call(bf16[16,2688]{1,0:T(8,128)(2,1)S(1)} %reshape.236.packed, f32[8,128]{1,0:T(8,128)S(1)} %pad.54.loss), custom_call_target="tpu_custom_call" | custom-call | tf_op jit(solution)/shard_map/exchange_small/pallas_call | solution.py:1913
  429.8 0.6 reduce_sum.38
  431.0 1.6 fusion.15.extra
  434.6 1.3 fusion.10
  435.9 0.7 pad.56.rest_2_
  436.6 114.1 %reduce_layer.2 = (f32[2,384,768]{2,1,0:T(8,128)}, f32[864,384]{1,0:T(8,128)}, f32[384,384]{1,0:T(8,128)}, f32[2,384,768]{2,1,0:T(8,128)}, f32[864,384]{1,0:T(8,...) custom-call(bf16[4,2,2,384,768]{4,3,2,1,0:T(8,128)(2,1)} %bitcast.192, bf16[2,864,384]{2,1,0:T(8,128)(2,1)} %bitcast.206, ...), custom_call_target="tpu_custom_call" | custom-call | tf_op jit(solution)/shard_map/reduce_layer/pallas_call | solution.py:1616
  550.7 2.2 convert_bitcast_fusion
  553.0 1.5 fusion.16.extra
  554.5 151.3 %reduce_layer.3 = (f32[2,384,768]{2,1,0:T(8,128)}, f32[864,384]{1,0:T(8,128)}, f32[384,384]{1,0:T(8,128)}, f32[2,384,768]{2,1,0:T(8,128)}, f32[864,384]{1,0:T(8,128)}, /*index=5*/f32[384,384]{1,0:T(8,128)}) custom-call(bf16[4,2,2,384,768]{4,3,2,1,0:T(8,128)(2,1)} %bitcast.193, bf16[2,864,384]{2,1,0:T(8,128)(2,1)} %bitcast.207, ...), custom_call_target="tpu_custom_call" | custom-call | tf_op jit(solution)/shard_map/reduce_layer/pallas_call | solution.py:1616
  705.8 10.2 %update_arrays.3 = (f32[2,864,384]{2,1,0:T(8,128)}, bf16[2,864,384]{2,1,0:T(8,128)(2,1)}, f32[2,864,384]{2,1,0:T(8,128)}, f32[2,864,384]{2,1,0:T(8,128)}, f32[2,864,384]{2,1,0:T(8,128)}) custom-call(f32[864,384]{1,0:T(8,128)} %get-tuple-element.166.grad_a, f32[864,384]{1,0:T(8,128)} %get-tuple-element.167.grad_b, f32[864,384]{1,0:T(8,128)} %get-tuple-element.168.total_a, ...), custom_call_target="tpu_custom_call" | custom-call | tf_op jit(solution)/shard_map/update_arrays/pallas_call | solution.py:1236
  716.0 5.9 update_arrays.4
  721.9 18.1 %update_arrays.5 = (f32[2,768,768]{2,1,0:T(8,128)}, bf16[2,768,768]{2,1,0:T(8,128)(2,1)}, f32[2,768,768]{2,1,0:T(8,128)}, f32[2,768,768]{2,1,0:T(8,128)}, f32[2,768,768]{2,1,0:T(8,128)}) custom-call(f32[768,768]{1,0:T(8,128)} %bitcast.204, f32[768,768]{1,0:T(8,128)} %bitcast.202, f32[768,768]{1,0:T(8,128)} %bitcast.205, f32[768,768]{1,0:T(8,128)} %bitcast.203, ...), custom_call_target="tpu_custom_call" | custom-call | tf_op jit(solution)/shard_map/update_arrays/pallas_call | solution.py:1236
  (91 shorter events, 4.7 us)
Async XLA Ops:
  0.7 120.9 %copy-start = (bf16[1024,16]{0,1:T(8,128)(2,1)S(1)}, bf16[1024,16]{0,1:T(8,128)(2,1)}, u32[]{:S(2)}) copy-start(bf16[1024,16]{0,1:T(8,128)(2,1)} %param.22) | copy-start | bytes 98308
  0.7 3.4 copy-start.2
  3.7 1.7 copy-start.3
  4.1 1.3 copy-start.8
  4.1 3.2 copy-start.1
  9.1 114.9 %copy-start.19 = (s32[4]{0:T(128)S(1)}, s32[4]{0:T(128)}, u32[]{:S(2)}) copy-start(s32[4]{0:T(128)} %param.24) | copy-start | bytes 52
  9.1 115.6 %copy-start.17 = (s32[4]{0:T(128)S(1)}, s32[4]{0:T(128)}, u32[]{:S(2)}) copy-start(s32[4]{0:T(128)} %param.25) | copy-start | bytes 52
  124.0 7.5 %copy-start.13 = (f32[128]{0:T(128)}, f32[128]{0:T(128)S(1)}, u32[]{:S(2)}) copy-start(f32[128]{0:T(128)S(1)} %multiply_exponential_fusion) | copy-start | bytes 1540
  124.0 7.5 %copy-start.15 = (f32[4]{0:T(128)}, f32[4]{0:T(128)S(1)}, u32[]{:S(2)}) copy-start(f32[4]{0:T(128)S(1)} %convert_element_type.107) | copy-start | bytes 52
  133.1 9.5 %copy-start.10 = (f32[2,1024,2]{1,2,0:T(2,128)S(1)}, f32[2,1024,2]{1,2,0:T(2,128)}, u32[]{:S(2)}) copy-start(f32[2,1024,2]{1,2,0:T(2,128)} %param.27) | copy-start | bytes 49156
  133.1 9.5 %copy-start.11 = (s32[2,1024,2]{1,2,0:T(2,128)S(1)}, s32[2,1024,2]{1,2,0:T(2,128)}, u32[]{:S(2)}) copy-start(s32[2,1024,2]{1,2,0:T(2,128)} %param.26) | copy-start | bytes 49156
  385.3 18.8 %copy-start.9 = (bf16[16,384]{1,0:T(8,128)(2,1)S(1)}, bf16[16,384]{1,0:T(8,128)(2,1)}, u32[]{:S(2)}) copy-start(bf16[16,384]{1,0:T(8,128)(2,1)} %convert.69) | copy-start | bytes 36868
  407.3 7.3 copy-start.14
  407.3 7.3 copy-start.16
  407.3 7.6 %copy-start.18 = (s32[4]{0:T(128)S(1)}, s32[4]{0:T(128)}, u32[]{:S(2)}) copy-start(s32[4]{0:T(128)} %param.25) | copy-start | bytes 52
  407.3 8.1 %copy-start.12 = (f32[16,1]{1,0:T(8,128)S(1)}, f32[16,1]{1,0:T(8,128)}, u32[]{:S(2)}) copy-start(f32[16,1]{1,0:T(8,128)} %get-tuple-element.153) | copy-start | bytes 196
  430.9 3.6 copy-start.4
  430.9 3.6 copy-start.5
  431.0 3.6 copy-start.6
  436.6 114.1 %copy-start.7 = (f32[2441,48]{0,1:T(8,128)S(1)}, f32[2441,48]{0,1:T(8,128)}, u32[]{:S(2)}) copy-start(f32[2441,48]{0,1:T(8,128)} %param.40) | copy-start | bytes 1406020
